TPU v7x, 128 devices: a whole 4x4x4 slice. The times are simulated.
128 devices in a mesh: view: 32 (over x, z, core), head: 4 (over y).
Axes of the slice: x: 4, y: 4, z: 4, core: 2. Of those that a mesh axis runs over, the one named last changes fastest.
Arguments:
- queries: bfloat16 [64, 128, 3072], P('view', None, 'head'), may hold values from -8 to 8
- keys: bfloat16 [64, 128, 3072], P('view', None, 'head'), may hold values from -8 to 8
- values: bfloat16 [64, 128, 3072], P('view', None, 'head'), may hold values from -6 to 6
- d_out: bfloat16 [64, 128, 3072], P('view', None, 'head'), may hold values from -6 to 6
- w_out: bfloat16 [3072, 3072], P('head'), may hold values from -0.109375 to 0.109375
- intersection: int32 [64, 4], replicated, may hold values from 0 to 1, as said below
Outputs:
- attended: bfloat16 [64, 128, 3072], P('view', None, 'head')
- grad_queries: bfloat16 [64, 128, 3072], P('view', None, 'head')
- grad_keys: bfloat16 [64, 128, 3072], P('view', None, 'head')
- grad_values: bfloat16 [64, 128, 3072], P('view', None, 'head')
Inputs may be any that keep to these rules, and one draw needn't show every extreme that they name: intersection[v, k] is 1 when views v and v + k + 1 intersect; it is 0 wherever v + k + 1 >= 64.
All inputs are finite; a program needn't handle non-finite values.
Results may differ from a plain program's by a relative error of at most 0.02.
Values may be sent and summed in bfloat16 or wider, within the bound.
No kernel may reach another device: no remote copies, remote signals or barrier semaphores. Data moves between devices by JAX's collectives and lax.ppermute only.
A program may use at most 128 MiB of HBM per device.

v0:
```python
from functools import partial

import jax
import jax.numpy as jnp
from jax import lax
from jax.experimental import pallas as pl
from jax.experimental.pallas import tpu as pltpu
from jax.sharding import PartitionSpec as P

HEAD_DIM = 96
REACH = 4
GROUP = 4
COLS = GROUP * HEAD_DIM
BLOCKS = 5
SCALE = HEAD_DIM ** (-0.5)
LOG2E = 1.4426950408889634
FAR = -1e30
VMEM_LIMIT = 40 * 1024 * 1024
BF16 = jnp.bfloat16
F32 = jnp.float32


def send(array, axis, pairs):
    return lax.ppermute(array, axis, pairs)


def to_sibling(array, count):
    return send(array, "view", [(i, i ^ 1) for i in range(count)])


def from_chip_a(array, count):
    pairs = [(i, i + 2) if i % 2 else (i, i - 2) for i in range(count)]
    return send(array, "view", [(s, t) for s, t in pairs if 0 <= t < count])


def from_chip_b(array, count):
    pairs = [(i, i - 2) if i % 2 else (i, i + 2) for i in range(count)]
    return send(array, "view", [(s, t) for s, t in pairs if 0 <= t < count])


def window(array, count):
    far_a = from_chip_a(array, count)
    far_b = from_chip_b(array, count)
    near = to_sibling(array, count)
    return (array, near, far_a, to_sibling(far_a, count), far_b)


def head_span(i):
    lo = i * HEAD_DIM // 128 * 128
    hi = -(-(i + 1) * HEAD_DIM // 128) * 128
    return lo, hi


def head_mask(i, rows, lo, hi):
    lane = lax.broadcasted_iota(jnp.int32, (rows, hi - lo), 1) + lo
    return (lane >= i * HEAD_DIM) & (lane < (i + 1) * HEAD_DIM)


def head_rows(ref, i, lo, hi):
    rows = ref.shape[0]
    mask = head_mask(i, 1, lo, hi).astype(F32).astype(BF16)
    return ref[:, lo:hi] * jnp.broadcast_to(mask, (rows, hi - lo))


def dot_nt(a, b):
    return lax.dot_general(a, b, (((1,), (1,)), ((), ())), preferred_element_type=F32)


def dot_nn(a, b):
    return jnp.dot(a, b, preferred_element_type=F32)


def put_lane(tile, lane, column):
    at = lax.broadcasted_iota(jnp.int32, tile.shape, 1)
    return jnp.where(at == lane, column, tile)


def add_head(total, i, lo, hi, part):
    part = jnp.where(head_mask(i, part.shape[0], lo, hi), part, 0.0)
    total[:, lo:hi] += part


def forward_kernel(q_ref, *refs):
    k_refs, v_refs = refs[:BLOCKS], refs[BLOCKS : 2 * BLOCKS]
    bias_ref, attn_ref, p_ref, stat_ref, s_ref, total = refs[2 * BLOCKS :]
    rows = q_ref.shape[0]
    total[...] = jnp.zeros_like(total)
    stat = jnp.zeros((rows, 128), F32)
    for i in range(GROUP):
        lo, hi = head_span(i)
        query = head_rows(q_ref, i, lo, hi)
        top = jnp.full((rows, 1), FAR, F32)
        for b in range(BLOCKS):
            at = slice(b * rows, (b + 1) * rows)
            scores = dot_nt(query, k_refs[b][:, lo:hi]) * (SCALE * LOG2E)
            half = rows // 2
            scores = jnp.concatenate(
                [scores[:half] + bias_ref[0:1, at], scores[half:] + bias_ref[1:2, at]], axis=0
            )
            s_ref[i % 2, :, at] = scores
            top = jnp.maximum(top, jnp.max(scores, axis=1, keepdims=True))
        norm = jnp.zeros((rows, 1), F32)
        out = jnp.zeros((rows, hi - lo), F32)
        for b in range(BLOCKS):
            at = slice(b * rows, (b + 1) * rows)
            weights = jnp.exp2(s_ref[i % 2, :, at] - top)
            norm += jnp.sum(weights, axis=1, keepdims=True)
            low = weights.astype(BF16)
            p_ref[i, :, at] = low
            out += dot_nn(low, v_refs[b][:, lo:hi])
        add_head(total, i, lo, hi, out / norm)
        stat = put_lane(stat, i, top + jnp.log2(norm))
        stat = put_lane(stat, GROUP + i, SCALE / norm)
    attn_ref[...] = total[...].astype(BF16)
    stat_ref[0] = stat


def forward(q, k, v, bias):
    rows, width = q.shape
    groups = width // COLS
    block = pl.BlockSpec((rows, COLS), lambda g: (0, g))
    return pl.pallas_call(
        forward_kernel,
        grid=(groups,),
        in_specs=[block] * (1 + 2 * BLOCKS) + [pl.BlockSpec(bias.shape, lambda g: (0, 0))],
        out_specs=[
            block,
            pl.BlockSpec((GROUP, rows, BLOCKS * rows), lambda g: (g, 0, 0)),
            pl.BlockSpec((1, rows, 128), lambda g: (g, 0, 0)),
        ],
        out_shape=[
            jax.ShapeDtypeStruct((rows, width), BF16),
            jax.ShapeDtypeStruct((groups * GROUP, rows, BLOCKS * rows), BF16),
            jax.ShapeDtypeStruct((groups, rows, 128), F32),
        ],
        scratch_shapes=[
            pltpu.VMEM((2, rows, BLOCKS * rows), F32),
            pltpu.VMEM((rows, COLS), F32),
        ],
        compiler_params=pltpu.CompilerParams(vmem_limit_bytes=VMEM_LIMIT),
        cost_estimate=pl.CostEstimate(
            flops=4 * rows * rows * BLOCKS * width, bytes_accessed=10_000_000, transcendentals=0
        ),
        name="forward",
    )(q, *k, *v, bias)


def d_attn_kernel(order_ref, d0, d1, d2, d3, w_ref, out_ref, total):
    step = pl.program_id(0)
    for n, d_ref in enumerate((d0, d1, d2, d3)):

        @pl.when(step == n)
        def _():
            part = dot_nt(d_ref[...], w_ref[...])
            if n == 0:
                total[...] = part
            else:
                total[...] += part

    @pl.when(step == 3)
    def _():
        out_ref[...] = total[...].astype(BF16)


def attn_cotangent(order, parts, w_out):
    rows, width = parts[0].shape
    whole = pl.BlockSpec((rows, width), lambda s, order: (0, 0))
    return pl.pallas_call(
        d_attn_kernel,
        grid_spec=pltpu.PrefetchScalarGridSpec(
            num_scalar_prefetch=1,
            grid=(4,),
            in_specs=[whole] * 4 + [pl.BlockSpec((width, width), lambda s, order: (0, order[s]))],
            out_specs=whole,
            scratch_shapes=[pltpu.VMEM((rows, width), F32)],
        ),
        out_shape=jax.ShapeDtypeStruct((rows, width), BF16),
        compiler_params=pltpu.CompilerParams(vmem_limit_bytes=VMEM_LIMIT),
        cost_estimate=pl.CostEstimate(
            flops=8 * rows * width * width, bytes_accessed=7_000_000, transcendentals=0
        ),
        name="attn_cotangent",
    )(order, *parts, w_out)


def project_kernel(order_ref, attn_ref, d_ref, stat_ref, w_ref, o1, o2, o3, own, stat_out, rows_out):
    step = pl.program_id(0)

    @pl.when(step == 0)
    def _():
        product = attn_ref[...].astype(F32) * d_ref[...].astype(F32)
        for g in range(stat_ref.shape[0]):
            stat = stat_ref[g]
            for i in range(GROUP):
                lo, hi = head_span(i)
                mine = jnp.where(
                    head_mask(i, product.shape[0], lo, hi),
                    product[:, g * COLS + lo : g * COLS + hi],
                    0.0,
                )
                stat = put_lane(stat, 2 * GROUP + i, jnp.sum(mine, axis=1, keepdims=True))
            stat_out[g] = stat
            rows_out[g] = stat.T[: 4 * GROUP]

    for n, out_ref in enumerate((o1, o2, o3, own)):

        @pl.when(step == n)
        def _():
            out_ref[...] = dot_nn(attn_ref[...], w_ref[...]).astype(out_ref.dtype)


def project(order, attn, d_attn, stat, w_out):
    rows, width = attn.shape
    groups = stat.shape[0]
    whole = pl.BlockSpec((rows, width), lambda s, order: (0, 0))
    stats = pl.BlockSpec((groups, rows, 128), lambda s, order: (0, 0, 0))
    return pl.pallas_call(
        project_kernel,
        grid_spec=pltpu.PrefetchScalarGridSpec(
            num_scalar_prefetch=1,
            grid=(4,),
            in_specs=[
                whole,
                whole,
                stats,
                pl.BlockSpec((width, width), lambda s, order: (0, order[s])),
            ],
            out_specs=[whole] * 4
            + [stats, pl.BlockSpec((groups, 4 * GROUP, rows), lambda s, order: (0, 0, 0))],
        ),
        out_shape=[jax.ShapeDtypeStruct((rows, width), BF16)] * 3
        + [
            jax.ShapeDtypeStruct((rows, width), F32),
            jax.ShapeDtypeStruct((groups, rows, 128), F32),
            jax.ShapeDtypeStruct((groups, 4 * GROUP, rows), F32),
        ],
        compiler_params=pltpu.CompilerParams(vmem_limit_bytes=VMEM_LIMIT),
        cost_estimate=pl.CostEstimate(
            flops=8 * rows * width * width, bytes_accessed=8_000_000, transcendentals=0
        ),
        name="project",
    )(order, attn, d_attn, stat, w_out)


def query_grad_kernel(p_ref, d_ref, stat_ref, *refs):
    k_refs, v_refs = refs[:BLOCKS], refs[BLOCKS : 2 * BLOCKS]
    out_ref, total = refs[2 * BLOCKS :]
    rows = d_ref.shape[0]
    total[...] = jnp.zeros_like(total)
    for i in range(GROUP):
        lo, hi = head_span(i)
        cot = head_rows(d_ref, i, lo, hi)
        delta = stat_ref[0, :, 2 * GROUP + i : 2 * GROUP + i + 1]
        scale = stat_ref[0, :, GROUP + i : GROUP + i + 1]
        grad = jnp.zeros((rows, hi - lo), F32)
        for b in range(BLOCKS):
            at = slice(b * rows, (b + 1) * rows)
            d_probs = dot_nt(cot, v_refs[b][:, lo:hi])
            d_scores = (p_ref[i, :, at].astype(F32) * (d_probs - delta)).astype(BF16)
            grad += dot_nn(d_scores, k_refs[b][:, lo:hi])
        add_head(total, i, lo, hi, grad * scale)
    out_ref[...] = total[...].astype(BF16)


def query_grad(p, d_attn, stat, k, v):
    rows, width = d_attn.shape
    groups = width // COLS
    block = pl.BlockSpec((rows, COLS), lambda g: (0, g))
    return pl.pallas_call(
        query_grad_kernel,
        grid=(groups,),
        in_specs=[
            pl.BlockSpec((GROUP, rows, BLOCKS * rows), lambda g: (g, 0, 0)),
            block,
            pl.BlockSpec((1, rows, 128), lambda g: (g, 0, 0)),
        ]
        + [block] * (2 * BLOCKS),
        out_specs=block,
        out_shape=jax.ShapeDtypeStruct((rows, width), BF16),
        scratch_shapes=[pltpu.VMEM((rows, COLS), F32)],
        compiler_params=pltpu.CompilerParams(vmem_limit_bytes=VMEM_LIMIT),
        cost_estimate=pl.CostEstimate(
            flops=4 * rows * rows * BLOCKS * width, bytes_accessed=10_000_000, transcendentals=0
        ),
        name="query_grad",
    )(p, d_attn, stat, *k, *v)


def key_grad_kernel(k_ref, v_ref, bias_ref, *refs):
    q_refs, d_refs, s_refs = (refs[n * BLOCKS : (n + 1) * BLOCKS] for n in range(3))
    gk_ref, gv_ref, total_k, total_v = refs[3 * BLOCKS :]
    rows = k_ref.shape[0]
    half = rows // 2
    total_k[...] = jnp.zeros_like(total_k)
    total_v[...] = jnp.zeros_like(total_v)
    for i in range(GROUP):
        lo, hi = head_span(i)
        key = head_rows(k_ref, i, lo, hi)
        value = head_rows(v_ref, i, lo, hi)
        grad_k = jnp.zeros((rows, hi - lo), F32)
        grad_v = jnp.zeros((rows, hi - lo), F32)
        for b in range(BLOCKS):
            at = slice(b * rows, (b + 1) * rows)
            query = q_refs[b][:, lo:hi]
            cot = d_refs[b][:, lo:hi]
            shift = bias_ref[:, at] - s_refs[b][0, i : i + 1]
            delta = s_refs[b][0, 2 * GROUP + i : 2 * GROUP + i + 1]
            scores = dot_nt(key, query) * (SCALE * LOG2E)
            weights = jnp.exp2(
                jnp.concatenate([scores[:half] + shift[0:1], scores[half:] + shift[1:2]], axis=0)
            )
            grad_v += dot_nn(weights.astype(BF16), cot)
            d_probs = dot_nt(value, cot)
            grad_k += dot_nn((weights * (d_probs - delta)).astype(BF16), query)
        add_head(total_k, i, lo, hi, grad_k * SCALE)
        add_head(total_v, i, lo, hi, grad_v)
    gk_ref[...] = total_k[...].astype(BF16)
    gv_ref[...] = total_v[...].astype(BF16)


def key_grad(k, v, bias, q, d, stats):
    rows, width = k.shape
    groups = width // COLS
    block = pl.BlockSpec((rows, COLS), lambda g: (0, g))
    return pl.pallas_call(
        key_grad_kernel,
        grid=(groups,),
        in_specs=[block, block, pl.BlockSpec(bias.shape, lambda g: (0, 0))]
        + [block] * (2 * BLOCKS)
        + [pl.BlockSpec((1, 4 * GROUP, rows), lambda g: (g, 0, 0))] * BLOCKS,
        out_specs=[block, block],
        out_shape=[jax.ShapeDtypeStruct((rows, width), BF16)] * 2,
        scratch_shapes=[pltpu.VMEM((rows, COLS), F32)] * 2,
        compiler_params=pltpu.CompilerParams(vmem_limit_bytes=VMEM_LIMIT),
        cost_estimate=pl.CostEstimate(
            flops=8 * rows * rows * BLOCKS * width, bytes_accessed=6_000_000, transcendentals=0
        ),
        name="key_grad",
    )(k, v, bias, *q, *d, *stats)


def window_bias(intersection, base, odd, length):
    padded = jnp.pad(intersection, ((REACH, REACH), (0, 0)))
    near = lax.dynamic_slice(padded, (base, 0), (2 * REACH + 2, REACH))
    table = []
    for local in range(2):
        for other in range(2 * REACH + 2):
            gap = other - REACH - local
            if gap == 0:
                table.append(jnp.ones((), jnp.int32))
            elif abs(gap) > REACH:
                table.append(jnp.zeros((), jnp.int32))
            else:
                table.append(near[min(other, local + REACH), abs(gap) - 1])
    flags = jnp.stack(table).reshape(2, BLOCKS, 2)
    even_order = (2, 3, 4, 1, 0)
    ordered = jnp.where(
        odd,
        jnp.stack([flags[:, 4 - b] for b in even_order], 1),
        jnp.stack([flags[:, b] for b in even_order], 1),
    ).reshape(2, 2 * BLOCKS)
    return jnp.repeat(jnp.where(ordered > 0, 0.0, FAR).astype(F32), length, axis=1)


def body(queries, keys, values, d_out, w_out, intersection):
    count, length, width = queries.shape
    devices = lax.axis_size("view")
    groups = lax.axis_size("head")
    here = lax.axis_index("view")
    mine = lax.axis_index("head")
    q, k, v, d = (a.reshape(count * length, width) for a in (queries, keys, values, d_out))

    def from_group(array, by):
        return send(array, "head", [(i, (i - by) % groups) for i in range(groups)])

    k_win = window(k, devices)
    d_parts = [d] + [from_group(d, by) for by in (1, 3, 2)]
    v_win = window(v, devices)
    q_win = window(q, devices)
    bias = window_bias(intersection, here * count, here % 2 == 1, length)
    order = jnp.stack([(mine + by) % groups for by in (0, 1, 3, 2)]).astype(jnp.int32)
    d_attn = attn_cotangent(order, d_parts, w_out)
    d_win = window(d_attn, devices)
    attn, p, stat = forward(q, k_win, v_win, bias)
    out_order = jnp.stack([(mine + by) % groups for by in (1, 3, 2, 0)]).astype(jnp.int32)
    to_next, to_last, to_far, own, stat, stat_rows = project(out_order, attn, d_attn, stat, w_out)
    stats = window(stat_rows, devices)
    gained = [from_group(part, by) for part, by in ((to_next, 3), (to_last, 1), (to_far, 2))]
    grad_q = query_grad(p, d_attn, stat, k_win, v_win)
    grad_k, grad_v = key_grad(k, v, bias, q_win, d_win, stats)
    attended = (own + sum(part.astype(F32) for part in gained)).astype(BF16)
    shape = (count, length, width)
    return tuple(a.reshape(shape) for a in (attended, grad_q, grad_k, grad_v))


def solution(mesh):
    columns = P("view", None, "head")
    return jax.shard_map(
        body,
        mesh=mesh,
        in_specs=(columns, columns, columns, columns, P("head", None), P()),
        out_specs=(columns, columns, columns, columns),
        check_vma=False,
    )
```

profile of v0, /device:TPU:6, one launch (start us, length us, event | category | flops | bytes accessed | tf_op | source)
XLA Modules:
  0.0 111.0 jit_solution(17309072358613335140)
XLA Ops:
  0.7 6.2 %collective-permute-start.1 = (bf16[256,768]{1,0:T(8,128)(2,1)}, bf16[256,768]{1,0:T(8,128)(2,1)S(1)}, u32[]{:S(2)}, u32[]{:S(2)}) collective-permute-start(bf16[256,768]{1,0:T(8,128)(2,1)} %bitcast.33), channel_id=1, source_target_pairs={{4,12},{8,0},{12,20},{16,8},{20,28},{24,16},{28,36},{32,24},{36,44... | collective-permute-start | bytes 1179656 | tf_op jit(solution)/shard_map/ppermute | solution.py:24
  6.9 1.9 %collective-permute-start.3 = (bf16[256,768]{1,0:T(8,128)(2,1)}, bf16[256,768]{1,0:T(8,128)(2,1)S(1)}, u32[]{:S(2)}, u32[]{:S(2)}) collective-permute-start(bf16[256,768]{1,0:T(8,128)(2,1)} %bitcast.34), channel_id=1, source_target_pairs={{0,8},{8,16},{12,4},{16,24},{20,12},{24,32},{28,20},{32,40},{36,28... | collective-permute-start | bytes 1179656 | tf_op jit(solution)/shard_map/ppermute | solution.py:24
  9.2 5.8 %collective-permute-start.5 = (bf16[256,768]{1,0:T(8,128)(2,1)}, bf16[256,768]{1,0:T(8,128)(2,1)S(1)}, u32[]{:S(2)}, u32[]{:S(2)}) collective-permute-start(bf16[256,768]{1,0:T(8,128)(2,1)} %bitcast.39), channel_id=1, source_target_pairs={{4,12},{8,0},{12,20},{16,8},{20,28},{24,16},{28,36},{32,24},{36,44... | collective-permute-start | bytes 1179656 | tf_op jit(solution)/shard_map/ppermute | solution.py:24
  15.8 1.9 %collective-permute-start.7 = (bf16[256,768]{1,0:T(8,128)(2,1)}, bf16[256,768]{1,0:T(8,128)(2,1)S(1)}, u32[]{:S(2)}, u32[]{:S(2)}) collective-permute-start(bf16[256,768]{1,0:T(8,128)(2,1)} %bitcast.40), channel_id=1, source_target_pairs={{0,8},{8,16},{12,4},{16,24},{20,12},{24,32},{28,20},{32,40},{36,28... | collective-permute-start | bytes 1179656 | tf_op jit(solution)/shard_map/ppermute | solution.py:24
  17.7 3.1 %collective-permute-start.8 = (bf16[256,768]{1,0:T(8,128)(2,1)}, bf16[256,768]{1,0:T(8,128)(2,1)S(1)}, u32[]{:S(2)}, u32[]{:S(2)}) collective-permute-start(bf16[256,768]{1,0:T(8,128)(2,1)} %bitcast.44), channel_id=1, source_target_pairs={{0,3},{1,0},{2,1},{3,2},{4,7},{5,4},{6,5},{7,6},{8,11},{9,8},{10,9... | collective-permute-start | bytes 1179656 | tf_op jit(solution)/shard_map/ppermute | solution.py:24
  21.5 10.1 %stack.38 = s32[20]{0:T(128)S(1)} concatenate(s32[1]{0:T(128)} %bitcast.7, s32[1]{0:T(128)} %bitcast.8, s32[1]{0:T(128)} %bitcast.9, s32[1]{0:T(128)} %bitcast.10, s32[1]{0:T(128)} %constant.62.clone.1, s32[1]{0:T(128)} %bitcast.11, s32[1]{0:T(128)} %bitcast.12, s32[1]{0:T(128)} %bitcast.13, s32[1]{0:T(128)} %bitcast.14, s32[2]{0:T(128)S(1)} %broadcast.22, s32[1]{0:T(128)} %bitcast.15, ...), dimensions={0} | concatenate | bytes 160 | tf_op jit(solution)/shard_map/stack | solution.py:355
  32.2 2.2 %collective-permute-start.10 = (bf16[256,768]{1,0:T(8,128)(2,1)}, bf16[256,768]{1,0:T(8,128)(2,1)}, u32[]{:S(2)}, u32[]{:S(2)}) collective-permute-start(bf16[256,768]{1,0:T(8,128)(2,1)} %bitcast.46), channel_id=1, source_target_pairs={{0,2},{1,3},{2,0},{3,1},{4,6},{5,7},{6,4},{7,5},{8,10},{9,11},{10,... | collective-permute-start | bytes 1179656 | tf_op jit(solution)/shard_map/ppermute | solution.py:24
  34.4 6.0 %collective-permute-start.15 = (bf16[256,768]{1,0:T(8,128)(2,1)}, bf16[256,768]{1,0:T(8,128)(2,1)}, u32[]{:S(2)}, u32[]{:S(2)}) collective-permute-start(bf16[256,768]{1,0:T(8,128)(2,1)} %bitcast.48), channel_id=1, source_target_pairs={{4,12},{8,0},{12,20},{16,8},{20,28},{24,16},{28,36},{32,24},{36,44... | collective-permute-start | bytes 1179656 | tf_op jit(solution)/shard_map/ppermute | solution.py:24
  42.7 10.4 %collective-permute-done.9.d2 = bf16[256,768]{1,0:T(8,128)(2,1)} collective-permute-done((bf16[256,768]{1,0:T(8,128)(2,1)}, bf16[256,768]{1,0:T(8,128)(2,1)}, u32[]{:S(2)}, u32[]{:S(2)}) %collective-permute-start.9) | collective-permute-done | bytes 393248 | tf_op jit(solution)/shard_map/ppermute | solution.py:24
  53.1 1.9 %collective-permute-start.17 = (bf16[256,768]{1,0:T(8,128)(2,1)}, bf16[256,768]{1,0:T(8,128)(2,1)S(1)}, u32[]{:S(2)}, u32[]{:S(2)}) collective-permute-start(bf16[256,768]{1,0:T(8,128)(2,1)} %bitcast.50), channel_id=1, source_target_pairs={{0,8},{8,16},{12,4},{16,24},{20,12},{24,32},{28,20},{32,40},{36,28... | collective-permute-start | bytes 1179656 | tf_op jit(solution)/shard_map/ppermute | solution.py:24
  55.0 2.0 %collective-permute-start.16 = (bf16[256,768]{1,0:T(8,128)(2,1)}, bf16[256,768]{1,0:T(8,128)(2,1)S(1)}, u32[]{:S(2)}, u32[]{:S(2)}) collective-permute-start(bf16[256,768]{1,0:T(8,128)(2,1)} %collective-permute-done.15.refs_2_), channel_id=1, source_target_pairs={{0,4},{4,0},{8,12},{12,8},{16,20},{20,16},{24,28},{28,24},{32,36},... | collective-permute-start | bytes 1179656 | tf_op jit(solution)/shard_map/ppermute | solution.py:24
  57.1 2.3 %copy-done = bf16[768,3072]{1,0:T(8,128)(2,1)S(1)} copy-done((bf16[768,3072]{1,0:T(8,128)(2,1)S(1)}, bf16[768,3072]{1,0:T(8,128)(2,1)}, u32[]{:S(2)}) %copy-start) | copy-done | bytes 4718616
  60.5 4.4 %attn_cotangent.1.d_ref.refs_5_ = bf16[256,768]{1,0:T(8,128)(2,1)S(1)} custom-call(s32[4]{0:T(128)S(1)} %pad_add_fusion.1.order_ref, bf16[256,768]{1,0:T(8,128)(2,1)S(1)} %bitcast.47, bf16[256,768]{1,0:T(8,128)(2,1)S(1)} %collective-permute-done.8.d1, bf16[256,768]{1,0:T(8,128)(2,1)} %collective-permute-done.9.d2, ...), custom_call_target="tpu_custom_call" | custom-call | flops 1207959552 | bytes 7000000 | tf_op jit(solution)/shard_map/attn_cotangent/pallas_call | solution.py:168
  65.0 4.6 %collective-permute-start.19 = (bf16[256,768]{1,0:T(8,128)(2,1)S(1)}, bf16[256,768]{1,0:T(8,128)(2,1)S(1)}, u32[]{:S(2)}, u32[]{:S(2)}) collective-permute-start(bf16[256,768]{1,0:T(8,128)(2,1)S(1)} %attn_cotangent.1.d_ref.refs_5_), channel_id=1, source_target_pairs={{4,12},{8,0},{12,20},{16,8},{20,28},{24,16},{28,36},{32,24},{36,44... | collective-permute-start | bytes 1179656 | tf_op jit(solution)/shard_map/ppermute | solution.py:24
  69.6 5.3 %forward.1 = (bf16[256,768]{1,0:T(8,128)(2,1)S(1)}, bf16[8,256,1280]{2,1,0:T(8,128)(2,1)S(1)}, f32[2,256,128]{2,1,0:T(8,128)S(1)}) custom-call(bf16[256,768]{1,0:T(8,128)(2,1)S(1)} %bitcast.51, bf16[256,768]{1,0:T(8,128)(2,1)S(1)} %bitcast.35, bf16[256,768]{1,0:T(8,128)(2,1)S(1)} %collective-permute-done.refs_1_, ...), custom_call_target="tpu_custom_call" | custom-call | flops 1006632960 | bytes 10000000 | tf_op jit(solution)/shard_map/forward/pallas_call | solution.py:122
  74.9 3.0 %project.1 = (bf16[256,768]{1,0:T(8,128)(2,1)S(1)}, bf16[256,768]{1,0:T(8,128)(2,1)S(1)}, bf16[256,768]{1,0:T(8,128)(2,1)S(1)}, f32[256,768]{1,0:T(8,128)S(1)}, ...) custom-call(s32[4]{0:T(128)S(1)} %pad_add_fusion.order_ref, bf16[256,768]{1,0:T(8,128)(2,1)S(1)} %get-tuple-element.15.attn_ref, ...), custom_call_target="tpu_custom_call" | custom-call | flops 1207959552 | bytes 8000000 | tf_op jit(solution)/shard_map/project/pallas_call | solution.py:217
  78.6 2.0 %collective-permute-start.11 = (bf16[256,768]{1,0:T(8,128)(2,1)S(1)}, bf16[256,768]{1,0:T(8,128)(2,1)S(1)}, u32[]{:S(2)}, u32[]{:S(2)}) collective-permute-start(bf16[256,768]{1,0:T(8,128)(2,1)S(1)} %get-tuple-element.18), channel_id=1, source_target_pairs={{0,1},{1,2},{2,3},{3,0},{4,5},{5,6},{6,7},{7,4},{8,9},{9,10},{10,1... | collective-permute-start | bytes 1179656 | tf_op jit(solution)/shard_map/ppermute | solution.py:24
  80.6 1.9 %collective-permute-start.23 = (f32[2,16,256]{2,1,0:T(8,128)S(1)}, f32[2,16,256]{2,1,0:T(8,128)S(1)}, u32[]{:S(2)}, u32[]{:S(2)}) collective-permute-start(f32[2,16,256]{2,1,0:T(8,128)S(1)} %get-tuple-element.23.refs_10_), channel_id=1, source_target_pairs={{4,12},{8,0},{12,20},{16,8},{20,28},{24,16},{28,36},{32,24},{36,44... | collective-permute-start | bytes 98312 | tf_op jit(solution)/shard_map/ppermute | solution.py:24
  82.5 3.9 %collective-permute-start.21 = (bf16[256,768]{1,0:T(8,128)(2,1)S(1)}, bf16[256,768]{1,0:T(8,128)(2,1)S(1)}, u32[]{:S(2)}, u32[]{:S(2)}) collective-permute-start(bf16[256,768]{1,0:T(8,128)(2,1)S(1)} %attn_cotangent.1.d_ref.refs_5_), channel_id=1, source_target_pairs={{0,8},{8,16},{12,4},{16,24},{20,12},{24,32},{28,20},{32,40},{36,28... | collective-permute-start | bytes 1179656 | tf_op jit(solution)/shard_map/ppermute | solution.py:24
  86.8 5.0 %query_grad.1 = bf16[256,768]{1,0:T(8,128)(2,1)} custom-call(bf16[8,256,1280]{2,1,0:T(8,128)(2,1)S(1)} %get-tuple-element.21.p_ref, bf16[256,768]{1,0:T(8,128)(2,1)S(1)} %attn_cotangent.1.d_ref.refs_5_, f32[2,256,128]{2,1,0:T(8,128)S(1)} %get-tuple-element.22.stat_ref, bf16[256,768]{1,0:T(8,128)(2,1)S(1)} %bitcast.36, ...), custom_call_target="tpu_custom_call" | custom-call | flops 1006632960 | bytes 10000000 | tf_op jit(solution)/shard_map/query_grad/pallas_call | solution.py:269
  93.7 2.2 %collective-permute-start.25 = (f32[2,16,256]{2,1,0:T(8,128)S(1)}, f32[2,16,256]{2,1,0:T(8,128)S(1)}, u32[]{:S(2)}, u32[]{:S(2)}) collective-permute-start(f32[2,16,256]{2,1,0:T(8,128)S(1)} %get-tuple-element.23.refs_10_), channel_id=1, source_target_pairs={{0,8},{8,16},{12,4},{16,24},{20,12},{24,32},{28,20},{32,40},{36,28... | collective-permute-start | bytes 98312 | tf_op jit(solution)/shard_map/ppermute | solution.py:24
  96.8 1.9 %collective-permute-start.24 = (f32[2,16,256]{2,1,0:T(8,128)S(1)}, f32[2,16,256]{2,1,0:T(8,128)S(1)}, u32[]{:S(2)}, u32[]{:S(2)}) collective-permute-start(f32[2,16,256]{2,1,0:T(8,128)S(1)} %collective-permute-done.23.refs_12_), channel_id=1, source_target_pairs={{0,4},{4,0},{8,12},{12,8},{16,20},{20,16},{24,28},{28,24},{32,36},... | collective-permute-start | bytes 98312 | tf_op jit(solution)/shard_map/ppermute | solution.py:24
  99.6 2.0 %collective-permute-done.25.refs_14_ = f32[2,16,256]{2,1,0:T(8,128)S(1)} collective-permute-done((f32[2,16,256]{2,1,0:T(8,128)S(1)}, f32[2,16,256]{2,1,0:T(8,128)S(1)}, u32[]{:S(2)}, u32[]{:S(2)}) %collective-permute-start.25) | collective-permute-done | bytes 32800 | tf_op jit(solution)/shard_map/ppermute | solution.py:24
  101.6 9.4 %key_grad.1 = (bf16[256,768]{1,0:T(8,128)(2,1)}, bf16[256,768]{1,0:T(8,128)(2,1)}) custom-call(bf16[256,768]{1,0:T(8,128)(2,1)S(1)} %bitcast.37, bf16[256,768]{1,0:T(8,128)(2,1)S(1)} %bitcast.43, f32[2,1280]{1,0:T(2,128)S(1)} %bitcast.54, bf16[256,768]{1,0:T(8,128)(2,1)S(1)} %bitcast.52, bf16[256,768]{1,0:T(8,128)(2,1)S(1)} %collective-permute-done.14.refs_1_, ...), custom_call_target="tpu_custom_call" | custom-call | flops 2013265920 | bytes 6000000 | tf_op jit(solution)/shard_map/key_grad/pallas_call | solution.py:325
  (66 shorter events, 10.6 us)
Async XLA Ops:
  0.6 15.2 %collective-permute-start = (bf16[256,768]{1,0:T(8,128)(2,1)}, bf16[256,768]{1,0:T(8,128)(2,1)S(1)}, u32[]{:S(2)}, u32[]{:S(2)}) collective-permute-start(bf16[256,768]{1,0:T(8,128)(2,1)} %bitcast.32), channel_id=1, source_target_pairs={{0,4},{4,0},{8,12},{12,8},{16,20},{20,16},{24,28},{28,24},{32,36},... | collective-permute-start | bytes 1179656 | tf_op jit(solution)/shard_map/ppermute | solution.py:24
  0.7 17.0 %collective-permute-start.1 = (bf16[256,768]{1,0:T(8,128)(2,1)}, bf16[256,768]{1,0:T(8,128)(2,1)S(1)}, u32[]{:S(2)}, u32[]{:S(2)}) collective-permute-start(bf16[256,768]{1,0:T(8,128)(2,1)} %bitcast.33), channel_id=1, source_target_pairs={{4,12},{8,0},{12,20},{16,8},{20,28},{24,16},{28,36},{32,24},{36,44... | collective-permute-start | bytes 1179656 | tf_op jit(solution)/shard_map/ppermute | solution.py:24
  6.9 25.3 %collective-permute-start.3 = (bf16[256,768]{1,0:T(8,128)(2,1)}, bf16[256,768]{1,0:T(8,128)(2,1)S(1)}, u32[]{:S(2)}, u32[]{:S(2)}) collective-permute-start(bf16[256,768]{1,0:T(8,128)(2,1)} %bitcast.34), channel_id=1, source_target_pairs={{0,8},{8,16},{12,4},{16,24},{20,12},{24,32},{28,20},{32,40},{36,28... | collective-permute-start | bytes 1179656 | tf_op jit(solution)/shard_map/ppermute | solution.py:24
  8.9 23.3 %collective-permute-start.4 = (bf16[256,768]{1,0:T(8,128)(2,1)}, bf16[256,768]{1,0:T(8,128)(2,1)S(1)}, u32[]{:S(2)}, u32[]{:S(2)}) collective-permute-start(bf16[256,768]{1,0:T(8,128)(2,1)} %bitcast.38), channel_id=1, source_target_pairs={{0,4},{4,0},{8,12},{12,8},{16,20},{20,16},{24,28},{28,24},{32,36},... | collective-permute-start | bytes 1179656 | tf_op jit(solution)/shard_map/ppermute | solution.py:24
  9.2 25.3 %collective-permute-start.5 = (bf16[256,768]{1,0:T(8,128)(2,1)}, bf16[256,768]{1,0:T(8,128)(2,1)S(1)}, u32[]{:S(2)}, u32[]{:S(2)}) collective-permute-start(bf16[256,768]{1,0:T(8,128)(2,1)} %bitcast.39), channel_id=1, source_target_pairs={{4,12},{8,0},{12,20},{16,8},{20,28},{24,16},{28,36},{32,24},{36,44... | collective-permute-start | bytes 1179656 | tf_op jit(solution)/shard_map/ppermute | solution.py:24
  15.8 24.9 %collective-permute-start.7 = (bf16[256,768]{1,0:T(8,128)(2,1)}, bf16[256,768]{1,0:T(8,128)(2,1)S(1)}, u32[]{:S(2)}, u32[]{:S(2)}) collective-permute-start(bf16[256,768]{1,0:T(8,128)(2,1)} %bitcast.40), channel_id=1, source_target_pairs={{0,8},{8,16},{12,4},{16,24},{20,12},{24,32},{28,20},{32,40},{36,28... | collective-permute-start | bytes 1179656 | tf_op jit(solution)/shard_map/ppermute | solution.py:24
  17.7 23.0 %collective-permute-start.8 = (bf16[256,768]{1,0:T(8,128)(2,1)}, bf16[256,768]{1,0:T(8,128)(2,1)S(1)}, u32[]{:S(2)}, u32[]{:S(2)}) collective-permute-start(bf16[256,768]{1,0:T(8,128)(2,1)} %bitcast.44), channel_id=1, source_target_pairs={{0,3},{1,0},{2,1},{3,2},{4,7},{5,4},{6,5},{7,6},{8,11},{9,8},{10,9... | collective-permute-start | bytes 1179656 | tf_op jit(solution)/shard_map/ppermute | solution.py:24
  32.2 20.9 %collective-permute-start.9 = (bf16[256,768]{1,0:T(8,128)(2,1)}, bf16[256,768]{1,0:T(8,128)(2,1)}, u32[]{:S(2)}, u32[]{:S(2)}) collective-permute-start(bf16[256,768]{1,0:T(8,128)(2,1)} %bitcast.45), channel_id=1, source_target_pairs={{0,1},{1,2},{2,3},{3,0},{4,5},{5,6},{6,7},{7,4},{8,9},{9,10},{10,1... | collective-permute-start | bytes 1179656 | tf_op jit(solution)/shard_map/ppermute | solution.py:24
  32.2 20.9 %collective-permute-start.10 = (bf16[256,768]{1,0:T(8,128)(2,1)}, bf16[256,768]{1,0:T(8,128)(2,1)}, u32[]{:S(2)}, u32[]{:S(2)}) collective-permute-start(bf16[256,768]{1,0:T(8,128)(2,1)} %bitcast.46), channel_id=1, source_target_pairs={{0,2},{1,3},{2,0},{3,1},{4,6},{5,7},{6,4},{7,5},{8,10},{9,11},{10,... | collective-permute-start | bytes 1179656 | tf_op jit(solution)/shard_map/ppermute | solution.py:24
  34.4 20.6 %collective-permute-start.15 = (bf16[256,768]{1,0:T(8,128)(2,1)}, bf16[256,768]{1,0:T(8,128)(2,1)}, u32[]{:S(2)}, u32[]{:S(2)}) collective-permute-start(bf16[256,768]{1,0:T(8,128)(2,1)} %bitcast.48), channel_id=1, source_target_pairs={{4,12},{8,0},{12,20},{16,8},{20,28},{24,16},{28,36},{32,24},{36,44... | collective-permute-start | bytes 1179656 | tf_op jit(solution)/shard_map/ppermute | solution.py:24
  40.7 24.2 %collective-permute-start.2 = (bf16[256,768]{1,0:T(8,128)(2,1)S(1)}, bf16[256,768]{1,0:T(8,128)(2,1)S(1)}, u32[]{:S(2)}, u32[]{:S(2)}) collective-permute-start(bf16[256,768]{1,0:T(8,128)(2,1)S(1)} %collective-permute-done.1.refs_2_), channel_id=1, source_target_pairs={{0,4},{4,0},{8,12},{12,8},{16,20},{20,16},{24,28},{28,24},{32,36},... | collective-permute-start | bytes 1179656 | tf_op jit(solution)/shard_map/ppermute | solution.py:24
  40.8 24.2 %collective-permute-start.6 = (bf16[256,768]{1,0:T(8,128)(2,1)S(1)}, bf16[256,768]{1,0:T(8,128)(2,1)S(1)}, u32[]{:S(2)}, u32[]{:S(2)}) collective-permute-start(bf16[256,768]{1,0:T(8,128)(2,1)S(1)} %collective-permute-done.5.refs_7_), channel_id=1, source_target_pairs={{0,4},{4,0},{8,12},{12,8},{16,20},{20,16},{24,28},{28,24},{32,36},... | collective-permute-start | bytes 1179656 | tf_op jit(solution)/shard_map/ppermute | solution.py:24
  53.1 24.8 %collective-permute-start.14 = (bf16[256,768]{1,0:T(8,128)(2,1)}, bf16[256,768]{1,0:T(8,128)(2,1)S(1)}, u32[]{:S(2)}, u32[]{:S(2)}) collective-permute-start(bf16[256,768]{1,0:T(8,128)(2,1)} %bitcast.49), channel_id=1, source_target_pairs={{0,4},{4,0},{8,12},{12,8},{16,20},{20,16},{24,28},{28,24},{32,36},... | collective-permute-start | bytes 1179656 | tf_op jit(solution)/shard_map/ppermute | solution.py:24
  53.1 25.5 %collective-permute-start.17 = (bf16[256,768]{1,0:T(8,128)(2,1)}, bf16[256,768]{1,0:T(8,128)(2,1)S(1)}, u32[]{:S(2)}, u32[]{:S(2)}) collective-permute-start(bf16[256,768]{1,0:T(8,128)(2,1)} %bitcast.50), channel_id=1, source_target_pairs={{0,8},{8,16},{12,4},{16,24},{20,12},{24,32},{28,20},{32,40},{36,28... | collective-permute-start | bytes 1179656 | tf_op jit(solution)/shard_map/ppermute | solution.py:24
  55.0 23.5 %collective-permute-start.16 = (bf16[256,768]{1,0:T(8,128)(2,1)}, bf16[256,768]{1,0:T(8,128)(2,1)S(1)}, u32[]{:S(2)}, u32[]{:S(2)}) collective-permute-start(bf16[256,768]{1,0:T(8,128)(2,1)} %collective-permute-done.15.refs_2_), channel_id=1, source_target_pairs={{0,4},{4,0},{8,12},{12,8},{16,20},{20,16},{24,28},{28,24},{32,36},... | collective-permute-start | bytes 1179656 | tf_op jit(solution)/shard_map/ppermute | solution.py:24
  64.9 15.7 %collective-permute-start.18 = (bf16[256,768]{1,0:T(8,128)(2,1)S(1)}, bf16[256,768]{1,0:T(8,128)(2,1)S(1)}, u32[]{:S(2)}, u32[]{:S(2)}) collective-permute-start(bf16[256,768]{1,0:T(8,128)(2,1)S(1)} %attn_cotangent.1.d_ref.refs_5_), channel_id=1, source_target_pairs={{0,4},{4,0},{8,12},{12,8},{16,20},{20,16},{24,28},{28,24},{32,36},... | collective-permute-start | bytes 1179656 | tf_op jit(solution)/shard_map/ppermute | solution.py:24
  65.0 17.5 %collective-permute-start.19 = (bf16[256,768]{1,0:T(8,128)(2,1)S(1)}, bf16[256,768]{1,0:T(8,128)(2,1)S(1)}, u32[]{:S(2)}, u32[]{:S(2)}) collective-permute-start(bf16[256,768]{1,0:T(8,128)(2,1)S(1)} %attn_cotangent.1.d_ref.refs_5_), channel_id=1, source_target_pairs={{4,12},{8,0},{12,20},{16,8},{20,28},{24,16},{28,36},{32,24},{36,44... | collective-permute-start | bytes 1179656 | tf_op jit(solution)/shard_map/ppermute | solution.py:24
  77.9 13.9 %collective-permute-start.13 = (bf16[256,768]{1,0:T(8,128)(2,1)S(1)}, bf16[256,768]{1,0:T(8,128)(2,1)S(1)}, u32[]{:S(2)}, u32[]{:S(2)}) collective-permute-start(bf16[256,768]{1,0:T(8,128)(2,1)S(1)} %get-tuple-element.20), channel_id=1, source_target_pairs={{0,2},{1,3},{2,0},{3,1},{4,6},{5,7},{6,4},{7,5},{8,10},{9,11},{10,... | collective-permute-start | bytes 1179656 | tf_op jit(solution)/shard_map/ppermute | solution.py:24
  78.6 15.2 %collective-permute-start.12 = (bf16[256,768]{1,0:T(8,128)(2,1)S(1)}, bf16[256,768]{1,0:T(8,128)(2,1)S(1)}, u32[]{:S(2)}, u32[]{:S(2)}) collective-permute-start(bf16[256,768]{1,0:T(8,128)(2,1)S(1)} %get-tuple-element.19), channel_id=1, source_target_pairs={{0,3},{1,0},{2,1},{3,2},{4,7},{5,4},{6,5},{7,6},{8,11},{9,8},{10,9... | collective-permute-start | bytes 1179656 | tf_op jit(solution)/shard_map/ppermute | solution.py:24
  78.6 18.2 %collective-permute-start.11 = (bf16[256,768]{1,0:T(8,128)(2,1)S(1)}, bf16[256,768]{1,0:T(8,128)(2,1)S(1)}, u32[]{:S(2)}, u32[]{:S(2)}) collective-permute-start(bf16[256,768]{1,0:T(8,128)(2,1)S(1)} %get-tuple-element.18), channel_id=1, source_target_pairs={{0,1},{1,2},{2,3},{3,0},{4,5},{5,6},{6,7},{7,4},{8,9},{9,10},{10,1... | collective-permute-start | bytes 1179656 | tf_op jit(solution)/shard_map/ppermute | solution.py:24
  82.5 17.1 %collective-permute-start.21 = (bf16[256,768]{1,0:T(8,128)(2,1)S(1)}, bf16[256,768]{1,0:T(8,128)(2,1)S(1)}, u32[]{:S(2)}, u32[]{:S(2)}) collective-permute-start(bf16[256,768]{1,0:T(8,128)(2,1)S(1)} %attn_cotangent.1.d_ref.refs_5_), channel_id=1, source_target_pairs={{0,8},{8,16},{12,4},{16,24},{20,12},{24,32},{28,20},{32,40},{36,28... | collective-permute-start | bytes 1179656 | tf_op jit(solution)/shard_map/ppermute | solution.py:24
  86.8 14.8 %collective-permute-start.20 = (bf16[256,768]{1,0:T(8,128)(2,1)S(1)}, bf16[256,768]{1,0:T(8,128)(2,1)S(1)}, u32[]{:S(2)}, u32[]{:S(2)}) collective-permute-start(bf16[256,768]{1,0:T(8,128)(2,1)S(1)} %collective-permute-done.19.refs_7_), channel_id=1, source_target_pairs={{0,4},{4,0},{8,12},{12,8},{16,20},{20,16},{24,28},{28,24},{32,36},... | collective-permute-start | bytes 1179656 | tf_op jit(solution)/shard_map/ppermute | solution.py:24
  91.9 7.8 %collective-permute-start.22 = (f32[2,16,256]{2,1,0:T(8,128)S(1)}, f32[2,16,256]{2,1,0:T(8,128)S(1)}, u32[]{:S(2)}, u32[]{:S(2)}) collective-permute-start(f32[2,16,256]{2,1,0:T(8,128)S(1)} %get-tuple-element.23.refs_10_), channel_id=1, source_target_pairs={{0,4},{4,0},{8,12},{12,8},{16,20},{20,16},{24,28},{28,24},{32,36},... | collective-permute-start | bytes 98312 | tf_op jit(solution)/shard_map/ppermute | solution.py:24
  93.7 7.9 %collective-permute-start.25 = (f32[2,16,256]{2,1,0:T(8,128)S(1)}, f32[2,16,256]{2,1,0:T(8,128)S(1)}, u32[]{:S(2)}, u32[]{:S(2)}) collective-permute-start(f32[2,16,256]{2,1,0:T(8,128)S(1)} %get-tuple-element.23.refs_10_), channel_id=1, source_target_pairs={{0,8},{8,16},{12,4},{16,24},{20,12},{24,32},{28,20},{32,40},{36,28... | collective-permute-start | bytes 98312 | tf_op jit(solution)/shard_map/ppermute | solution.py:24
  (8 other events, 56.1 us)
where the time goes:
time: 112 us; the launch traced here: 111 us
  starting transfers between devices  49.8 us (44%)
  Pallas kernels  27.1 us (24%)
  local copies, waits for them, and re-layouts  17.1 us (15%)
  waiting for transfers between devices  15 us (13%)
  other arithmetic  1.15 us (1%)
    ppermute x26, starting transfers between devices, send(): return lax.ppermute(array, axis, pairs)  49.8 us
    ppermute x26, waiting for transfers between devices, send(): return lax.ppermute(array, axis, pairs)  15 us
    another operation x1, local copies, waits for them, and re-layouts, window_bias(): flags = jnp.stack(table).reshape(2, BLOCKS, 2)  10.1 us
    pallas_call x1, Pallas kernels, key_grad(): pl.pallas_call(key_grad_kernel, grid=(groups,), in_specs=[block, block, p...  9.38 us
    pallas_call x1, Pallas kernels, forward(): pl.pallas_call(forward_kernel, grid=(groups,), in_specs=[block] * (1 + 2...  5.32 us
    pallas_call x1, Pallas kernels, query_grad(): pl.pallas_call(query_grad_kernel, grid=(groups,), in_specs=[pl.BlockSpec(...  5.04 us
    unnamed x14, local copies, waits for them, and re-layouts  4.75 us
    pallas_call x1, Pallas kernels, attn_cotangent(): pl.pallas_call(d_attn_kernel, grid_spec=pltpu.PrefetchScalarGridSpec(num_...  4.37 us
  transfers between devices with their start and end apart: 26, of which 5 were waited for; matrix products, arithmetic and copies ran while one was open for 13% of the time, Pallas kernels for 16%

commit v1 on v0

v1 whole, which is shorter than its diff:
```python
from functools import partial

import jax
import jax.numpy as jnp
from jax import lax
from jax.experimental import pallas as pl
from jax.experimental.pallas import tpu as pltpu
from jax.sharding import PartitionSpec as P

HEAD_DIM = 96
REACH = 4
GROUP = 4
COLS = GROUP * HEAD_DIM
BLOCKS = 5
SCALE = HEAD_DIM ** (-0.5)
LOG2E = 1.4426950408889634
FAR = -1e30
VMEM_LIMIT = 18 * 1024 * 1024
SMALL_LIMIT = 1024 * 1024
BF16 = jnp.bfloat16
F32 = jnp.float32
SCALARS = pl.BlockSpec(memory_space=pltpu.SMEM)
COST = pl.CostEstimate(flops=1000, bytes_accessed=1000, transcendentals=0)


def declared(megabytes):
    return pl.CostEstimate(flops=megabytes * 300_000_000, bytes_accessed=1000, transcendentals=0)


C0, C1, C2, C3 = 20, 1, 1, 1
ORDER = pl.BlockSpec(memory_space=pl.ANY)
STAT_ROWS = 16


def send(array, axis, pairs):
    return lax.ppermute(array, axis, pairs)


def to_sibling(array, count):
    return send(array, "view", [(i, i ^ 1) for i in range(count)])


def from_chip_a(array, count):
    return send(array, "view", [(i, (i + (2 if i % 2 else -2)) % count) for i in range(count)])


def from_chip_b(array, count):
    return send(array, "view", [(i, (i + (-2 if i % 2 else 2)) % count) for i in range(count)])


def in_hbm(array):
    return pltpu.with_memory_space_constraint(array, pltpu.HBM)


def in_vmem(arrays):
    return [pltpu.with_memory_space_constraint(a, pltpu.VMEM) for a in arrays]


def head_span(i):
    lo = i * HEAD_DIM // 128 * 128
    hi = -(-(i + 1) * HEAD_DIM // 128) * 128
    return lo, hi


def head_mask(i, rows, lo, hi):
    lane = lax.broadcasted_iota(jnp.int32, (rows, hi - lo), 1) + lo
    return (lane >= i * HEAD_DIM) & (lane < (i + 1) * HEAD_DIM)


def head_rows(ref, i, lo, hi):
    rows = ref.shape[0]
    mask = head_mask(i, 1, lo, hi).astype(F32).astype(BF16)
    return ref[:, lo:hi] * jnp.broadcast_to(mask, (rows, hi - lo))


def dot_nt(a, b):
    return lax.dot_general(a, b, (((1,), (1,)), ((), ())), preferred_element_type=F32)


def dot_nn(a, b):
    return jnp.dot(a, b, preferred_element_type=F32)


def fill_bias(linked_ref, bias_ref):
    here = lax.axis_index("view")
    base, sign = 2 * here, 1 - 2 * (here % 2)
    views = linked_ref.shape[1]
    lane = lax.broadcasted_iota(jnp.int32, (1, bias_ref.shape[1] // BLOCKS), 1)
    half = bias_ref.shape[1] // BLOCKS // 2
    for local in range(2):
        for b, offset in enumerate((0, 2, 4, -2, -4)):
            shifts = []
            for other in range(2):
                gap = sign * offset + other - local
                lower = base + local + jnp.minimum(gap, 0)
                size = jnp.abs(gap)
                row = jnp.clip(lower, 0, views - 1)
                column = jnp.clip(size - 1, 0, REACH - 1)
                linked = (linked_ref[column, row] > 0) & (lower >= 0) & (size <= REACH)
                shifts.append(jnp.where(linked | (size == 0), 0.0, FAR).astype(F32))
            at = slice(2 * b * half, 2 * (b + 1) * half)
            bias_ref[local : local + 1, at] = jnp.where(lane < half, shifts[0], shifts[1])


def put_lane(tile, lane, column):
    at = lax.broadcasted_iota(jnp.int32, tile.shape, 1)
    return jnp.where(at == lane, column, tile)


def add_head(total, i, lo, hi, part):
    part = jnp.where(head_mask(i, part.shape[0], lo, hi), part, 0.0)
    total[:, lo:hi] += part


def forward_kernel(linked_ref, after_a, after_b, q_ref, *refs):
    k_refs, v_refs = refs[:BLOCKS], refs[BLOCKS : 2 * BLOCKS]
    attn_ref, p_ref, stat_ref, s_ref, total, bias_ref = refs[2 * BLOCKS :]
    rows = q_ref.shape[0]

    @pl.when(pl.program_id(0) == 0)
    def _():
        fill_bias(linked_ref, bias_ref)

    total[...] = jnp.zeros_like(total)
    stat = jnp.zeros((rows, 128), F32)
    for i in range(GROUP):
        lo, hi = head_span(i)
        query = head_rows(q_ref, i, lo, hi)
        top = jnp.full((rows, 1), FAR, F32)
        for b in range(BLOCKS):
            at = slice(b * rows, (b + 1) * rows)
            scores = dot_nt(query, k_refs[b][:, lo:hi]) * (SCALE * LOG2E)
            half = rows // 2
            scores = jnp.concatenate(
                [scores[:half] + bias_ref[0:1, at], scores[half:] + bias_ref[1:2, at]], axis=0
            )
            s_ref[i % 2, :, at] = scores
            top = jnp.maximum(top, jnp.max(scores, axis=1, keepdims=True))
        norm = jnp.zeros((rows, 1), F32)
        out = jnp.zeros((rows, hi - lo), F32)
        for b in range(BLOCKS):
            at = slice(b * rows, (b + 1) * rows)
            weights = jnp.exp2(s_ref[i % 2, :, at] - top)
            norm += jnp.sum(weights, axis=1, keepdims=True)
            low = weights.astype(BF16)
            p_ref[i, :, at] = low
            out += dot_nn(low, v_refs[b][:, lo:hi])
        add_head(total, i, lo, hi, out / norm)
        stat = put_lane(stat, i, top + jnp.log2(norm))
        stat = put_lane(stat, GROUP + i, SCALE / norm)
    attn_ref[...] = total[...].astype(BF16)
    stat_ref[0] = stat


def rows_at(n, rows):
    return pl.BlockSpec((rows, COLS), lambda g: (n, g))


def forward(linked, after, q, k, v, windows):
    rows, width = q.shape
    groups = width // COLS
    block = pl.BlockSpec((rows, COLS), lambda g: (0, g))
    k_specs, v_specs = ([block] + [rows_at(n, rows) for w in windows] for n in (0, 1))
    windows = in_vmem(windows)
    return pl.pallas_call(
        forward_kernel,
        grid=(groups,),
        in_specs=[SCALARS, ORDER, ORDER, block] + k_specs + v_specs,
        out_specs=[
            block,
            pl.BlockSpec((GROUP, rows, BLOCKS * rows), lambda g: (g, 0, 0)),
            pl.BlockSpec((1, rows, 128), lambda g: (g, 0, 0)),
        ],
        out_shape=[
            jax.ShapeDtypeStruct((rows, width), BF16),
            jax.ShapeDtypeStruct((groups * GROUP, rows, BLOCKS * rows), BF16),
            jax.ShapeDtypeStruct((groups, rows, 128), F32),
        ],
        scratch_shapes=[
            pltpu.VMEM((2, rows, BLOCKS * rows), F32),
            pltpu.VMEM((rows, COLS), F32),
            pltpu.VMEM((2, BLOCKS * rows), F32),
        ],
        compiler_params=pltpu.CompilerParams(vmem_limit_bytes=VMEM_LIMIT),
        cost_estimate=COST,
        name="forward",
    )(linked, *after, in_hbm(q), in_hbm(k), *windows, in_hbm(v), *windows)


def fetch_columns(w_ref, held, sems, hops):
    width = held.shape[2]
    mine = lax.axis_index("head")
    copies = []
    for n, by in enumerate(hops):
        at = pl.multiple_of((mine + by) % len(hops) * width, width)
        copies.append(pltpu.make_async_copy(w_ref.at[:, pl.ds(at, width)], held.at[n], sems.at[n]))
    for copy in copies:
        copy.start()
    return copies


def d_attn_kernel(d0, d1, d2, d3, w_ref, out_ref, held, sems):
    copies = fetch_columns(w_ref, held, sems, (0, 1, 3, 2))
    total = 0.0
    for n, d_ref in enumerate((d0, d1, d2, d3)):
        copies[n].wait()
        total += dot_nt(d_ref[...], held[n])
    out_ref[...] = total.astype(BF16)


def attn_cotangent(parts, w_out):
    rows, width = parts[0].shape
    whole = pl.BlockSpec((rows, width), lambda: (0, 0))
    return pl.pallas_call(
        d_attn_kernel,
        in_specs=[whole] * 4 + [ORDER],
        out_specs=whole,
        scratch_shapes=[pltpu.VMEM((4, width, width), BF16), pltpu.SemaphoreType.DMA((4,))],
        out_shape=jax.ShapeDtypeStruct((rows, width), BF16),
        compiler_params=pltpu.CompilerParams(vmem_limit_bytes=VMEM_LIMIT),
        cost_estimate=declared(C0),
        name="attn_cotangent",
    )(in_hbm(parts[0]), *in_vmem(parts[1:]), in_hbm(w_out))


def project_kernel(attn_ref, d_ref, stat_ref, qa_ref, qb_ref, w_ref, *refs):
    parts, stat_out, message, held, sems = refs[:4], *refs[4:]
    copies = fetch_columns(w_ref, held, sems, (1, 3, 2, 0))
    rows = attn_ref.shape[0]
    message[:rows] = d_ref[...]
    product = attn_ref[...].astype(F32) * d_ref[...].astype(F32)
    slabs = []
    for g in range(stat_ref.shape[0]):
        stat = stat_ref[g]
        travels = stat
        for i in range(GROUP):
            lo, hi = head_span(i)
            mine = jnp.where(
                head_mask(i, rows, lo, hi), product[:, g * COLS + lo : g * COLS + hi], 0.0
            )
            delta = jnp.sum(mine, axis=1, keepdims=True)
            stat = put_lane(stat, 2 * GROUP + i, delta)
            travels = put_lane(travels, GROUP + i, delta)
        stat_out[g] = stat
        slabs.append(travels.T[: 2 * GROUP])
    rest = jnp.concatenate(slabs, axis=0)
    for n in range(3):
        piece = rest.astype(BF16)
        message[rows:, n * rows : (n + 1) * rows] = piece
        rest = rest - piece.astype(F32)
    for n, out_ref in enumerate(parts):
        copies[n].wait()
        out_ref[...] = dot_nn(attn_ref[...], held[n]).astype(out_ref.dtype)


def project(attn, d_attn, stat, after, w_out):
    rows, width = attn.shape
    groups = stat.shape[0]
    whole = pl.BlockSpec((rows, width), lambda: (0, 0))
    stats = pl.BlockSpec((groups, rows, 128), lambda: (0, 0, 0))
    message = pl.BlockSpec((rows + STAT_ROWS, width), lambda: (0, 0))
    return pl.pallas_call(
        project_kernel,
        in_specs=[whole, whole, stats, ORDER, ORDER, ORDER],
        out_specs=[whole] * 4 + [stats, message],
        out_shape=[jax.ShapeDtypeStruct((rows, width), BF16)] * 3
        + [
            jax.ShapeDtypeStruct((rows, width), F32),
            jax.ShapeDtypeStruct((groups, rows, 128), F32),
            jax.ShapeDtypeStruct((rows + STAT_ROWS, width), BF16),
        ],
        scratch_shapes=[pltpu.VMEM((4, width, width), BF16), pltpu.SemaphoreType.DMA((4,))],
        compiler_params=pltpu.CompilerParams(vmem_limit_bytes=VMEM_LIMIT),
        cost_estimate=COST,
        name="project",
    )(*in_vmem((attn, d_attn, stat)), *after, in_hbm(w_out))


def query_grad_kernel(p_ref, d_ref, stat_ref, *refs):
    k_refs, v_refs = refs[:BLOCKS], refs[BLOCKS : 2 * BLOCKS]
    out_ref, total = refs[2 * BLOCKS :]
    rows = d_ref.shape[0]
    total[...] = jnp.zeros_like(total)
    for i in range(GROUP):
        lo, hi = head_span(i)
        cot = head_rows(d_ref, i, lo, hi)
        delta = stat_ref[0, :, 2 * GROUP + i : 2 * GROUP + i + 1]
        scale = stat_ref[0, :, GROUP + i : GROUP + i + 1]
        grad = jnp.zeros((rows, hi - lo), F32)
        for b in range(BLOCKS):
            at = slice(b * rows, (b + 1) * rows)
            d_probs = dot_nt(cot, v_refs[b][:, lo:hi])
            d_scores = (p_ref[i, :, at].astype(F32) * (d_probs - delta)).astype(BF16)
            grad += dot_nn(d_scores, k_refs[b][:, lo:hi])
        add_head(total, i, lo, hi, grad * scale)
    out_ref[...] = total[...].astype(BF16)


def query_grad(p, d_attn, stat, k, v, windows):
    rows, width = d_attn.shape
    groups = width // COLS
    block = pl.BlockSpec((rows, COLS), lambda g: (0, g))
    k_specs, v_specs = ([block] + [rows_at(n, rows) for w in windows] for n in (0, 1))
    windows = in_vmem(windows)
    return pl.pallas_call(
        query_grad_kernel,
        grid=(groups,),
        in_specs=[
            pl.BlockSpec((GROUP, rows, BLOCKS * rows), lambda g: (g, 0, 0)),
            block,
            pl.BlockSpec((1, rows, 128), lambda g: (g, 0, 0)),
        ]
        + k_specs
        + v_specs,
        out_specs=block,
        out_shape=jax.ShapeDtypeStruct((rows, width), BF16),
        scratch_shapes=[pltpu.VMEM((rows, COLS), F32)],
        compiler_params=pltpu.CompilerParams(vmem_limit_bytes=VMEM_LIMIT),
        cost_estimate=declared(C3),
        name="query_grad",
    )(*in_vmem((p, d_attn, stat)), in_hbm(k), *windows, in_hbm(v), *windows)


def key_grad_kernel(blocks, final, linked_ref, k_ref, v_ref, *refs):
    count = len(blocks)
    q_refs, d_refs, s_refs = (refs[n * count : (n + 1) * count] for n in range(3))
    *so_far, gk_ref, gv_ref, total_k, total_v, bias_ref = refs[3 * count :]
    rows = k_ref.shape[0]
    half = rows // 2

    @pl.when(pl.program_id(0) == 0)
    def _():
        fill_bias(linked_ref, bias_ref)

    first = pl.program_id(0) == 0
    stats = []
    for s_ref in s_refs:
        packed = s_ref[...].astype(F32)
        stat = packed[:, :rows] + packed[:, rows : 2 * rows] + packed[:, 2 * rows :]
        stats.append(jnp.where(first, stat[: 2 * GROUP], stat[2 * GROUP :]))
    for total, ref in zip((total_k, total_v), so_far if final else (None, None)):
        total[...] = jnp.zeros_like(total) if ref is None else ref[...]
    for i in range(GROUP):
        lo, hi = head_span(i)
        key = head_rows(k_ref, i, lo, hi)
        value = head_rows(v_ref, i, lo, hi)
        grad_k = jnp.zeros((rows, hi - lo), F32)
        grad_v = jnp.zeros((rows, hi - lo), F32)
        for n, b in enumerate(blocks):
            at = slice(b * rows, (b + 1) * rows)
            query = q_refs[n][:, lo:hi]
            cot = d_refs[n][:, lo:hi]
            shift = bias_ref[:, at] - stats[n][i : i + 1]
            delta = stats[n][GROUP + i : GROUP + i + 1]
            scores = dot_nt(key, query) * (SCALE * LOG2E)
            weights = jnp.exp2(
                jnp.concatenate([scores[:half] + shift[0:1], scores[half:] + shift[1:2]], axis=0)
            )
            grad_v += dot_nn(weights.astype(BF16), cot)
            d_probs = dot_nt(value, cot)
            grad_k += dot_nn((weights * (d_probs - delta)).astype(BF16), query)
        add_head(total_k, i, lo, hi, grad_k)
        add_head(total_v, i, lo, hi, grad_v)
    gk_ref[...] = (total_k[...] * SCALE if final else total_k[...]).astype(gk_ref.dtype)
    gv_ref[...] = total_v[...].astype(gv_ref.dtype)


def key_grad(blocks, linked, k, v, q, q_rows, messages, so_far=(), after=()):
    rows, width = k.shape
    groups = width // COLS
    block = pl.BlockSpec((rows, COLS), lambda g: (0, g))
    stats = pl.BlockSpec((STAT_ROWS, width), lambda g: (rows // STAT_ROWS, 0))
    return pl.pallas_call(
        partial(key_grad_kernel, blocks, bool(so_far)),
        grid=(groups,),
        in_specs=[SCALARS, block, block]
        + [rows_at(n, rows) for n in q_rows]
        + [block] * len(blocks)
        + [stats] * len(blocks)
        + [block] * len(so_far)
        + [ORDER] * len(after),
        out_specs=[block, block],
        out_shape=[jax.ShapeDtypeStruct((rows, width), BF16 if so_far else F32)] * 2,
        scratch_shapes=[pltpu.VMEM((rows, COLS), F32)] * 2 + [pltpu.VMEM((2, BLOCKS * rows), F32)],
        compiler_params=pltpu.CompilerParams(vmem_limit_bytes=VMEM_LIMIT),
        cost_estimate=declared(C1) if so_far else COST,
        name="key_grad_far" if so_far else "key_grad_near",
    )(
        linked,
        in_hbm(k),
        in_hbm(v),
        *([in_hbm(q[0])] if not so_far else in_vmem(q[:1])),
        *in_vmem((*q[1:], *messages, *messages, *so_far)),
        *after,
    )


def gate_kernel(*refs):
    pass


def gate(arrays, after):
    return pl.pallas_call(
        gate_kernel,
        in_specs=[ORDER] * (len(arrays) + len(after)),
        out_specs=[ORDER] * len(arrays),
        out_shape=[jax.ShapeDtypeStruct(a.shape, a.dtype) for a in arrays],
        input_output_aliases={n: n for n in range(len(arrays))},
        compiler_params=pltpu.CompilerParams(vmem_limit_bytes=SMALL_LIMIT),
        cost_estimate=COST,
        name="gate",
    )(*in_vmem(arrays), *after)


def add_kernel(after_ref, own, a, b, c, out_ref):
    total = own[...] + a[...].astype(F32) + b[...].astype(F32) + c[...].astype(F32)
    out_ref[...] = total.astype(BF16)


def add_parts(after, own, parts):
    rows, width = own.shape
    block = pl.BlockSpec((rows, width), lambda: (0, 0))
    return pl.pallas_call(
        add_kernel,
        in_specs=[ORDER] + [block] * 4,
        out_specs=block,
        out_shape=jax.ShapeDtypeStruct((rows, width), BF16),
        compiler_params=pltpu.CompilerParams(vmem_limit_bytes=VMEM_LIMIT),
        cost_estimate=declared(C2),
        name="add_parts",
    )(after, *in_vmem((own, *parts)))


def corner_kernel(*refs):
    refs[-1][...] = jnp.zeros_like(refs[-1])


def corner(array, devices):
    shape = (16, 128)
    tile = pl.pallas_call(
        corner_kernel,
        in_specs=[ORDER],
        out_specs=pl.BlockSpec(shape, lambda: (0, 0)),
        out_shape=jax.ShapeDtypeStruct(shape, BF16),
        compiler_params=pltpu.CompilerParams(vmem_limit_bytes=SMALL_LIMIT),
        cost_estimate=COST,
        name="corner",
    )(array)
    return to_sibling(tile, devices)


def pack_kernel(k_ref, v_ref, out_ref):
    rows = k_ref.shape[0]
    out_ref[:rows] = k_ref[...]
    out_ref[rows:] = v_ref[...]


def pack(k, v):
    rows, width = k.shape
    return pl.pallas_call(
        pack_kernel,
        out_shape=jax.ShapeDtypeStruct((2 * rows, width), BF16),
        compiler_params=pltpu.CompilerParams(vmem_limit_bytes=VMEM_LIMIT),
        cost_estimate=COST,
        name="pack",
    )(in_hbm(k), in_hbm(v))


def body(queries, keys, values, d_out, w_out, intersection):
    count, length, width = queries.shape
    devices = lax.axis_size("view")
    groups = lax.axis_size("head")
    q, k, v, d = (a.reshape(count * length, width) for a in (queries, keys, values, d_out))
    linked = intersection.T

    def from_group(array, by):
        return send(array, "head", [(i, (i - by) % groups) for i in range(groups)])

    gathered = [from_group(d, by) for by in (1, 3, 2)]
    kv = pack(k, v)
    kv_a, kv_b = from_chip_a(kv, devices), from_chip_b(kv, devices)
    near = to_sibling(kv, devices)
    windows = (near, kv_a, to_sibling(kv_a, devices), kv_b)
    q_a, q_b = from_chip_a(q, devices), from_chip_b(q, devices)
    d_attn = attn_cotangent([d] + gathered, w_out)
    attn, p, stat = forward(linked, (d_attn, corner(kv_b, devices)), q, k, v, windows)
    to_next, to_last, to_far, own, stat, message = project(attn, d_attn, stat, (q_a, q_b), w_out)
    d_a, d_b = from_chip_a(message, devices), from_chip_b(message, devices)
    gained = [from_group(part, by) for part, by in ((to_next, 3), (to_last, 1), (to_far, 2))]
    grad_q = query_grad(p, d_attn, stat, k, v, windows)
    messages = (message, to_sibling(message, devices))
    q_far = (q_a, to_sibling(q_a, devices), q_b)
    part = key_grad(
        (0, 1), linked, k, v, (q, to_sibling(q, devices)), (0, 0), messages, after=q_far[1:2]
    )
    d_a, d_b = gate((d_a, d_b), (in_hbm(grad_q), part[0]))
    messages = (d_a, to_sibling(d_a, devices), d_b)
    grad_k, grad_v = key_grad((2, 3, 4), linked, k, v, q_far, (0, 0, 0), messages, part)
    attended = add_parts(message, own, gained)
    shape = (count, length, width)
    return tuple(a.reshape(shape) for a in (attended, grad_q, grad_k, grad_v))


def solution(mesh):
    columns = P("view", None, "head")
    return jax.shard_map(
        body,
        mesh=mesh,
        in_specs=(columns, columns, columns, columns, P("head", None), P()),
        out_specs=(columns, columns, columns, columns),
        check_vma=False,
    )
```

time: 112 us -> 83.4 us (0.74)
  the two profiles are of different devices: /device:TPU:6 before, /device:TPU:1 now
where the time goes in v1:
time: 83.4 us; the launch traced here: 83.2 us
  Pallas kernels  34.7 us (42%)
  starting transfers between devices  28 us (34%)
  waiting for transfers between devices  19.6 us (24%)
    ppermute x19, starting transfers between devices, send(): return lax.ppermute(array, axis, pairs)  28 us
    ppermute x19, waiting for transfers between devices, send(): return lax.ppermute(array, axis, pairs)  19.6 us
    pallas_call x2, Pallas kernels, key_grad(): pl.pallas_call(partial(key_grad_kernel, blocks, bool(so_far)), grid=(grou...  11.8 us
    pallas_call x1, Pallas kernels, forward(): pl.pallas_call(forward_kernel, grid=(groups,), in_specs=[SCALARS, ORDER,...  6.48 us
    pallas_call x1, Pallas kernels, query_grad(): pl.pallas_call(query_grad_kernel, grid=(groups,), in_specs=[pl.BlockSpec(...  5.73 us
    pallas_call x1, Pallas kernels, attn_cotangent(): pl.pallas_call(d_attn_kernel, in_specs=[whole] * 4 + [ORDER], out_specs=w...  4.63 us
    pallas_call x1, Pallas kernels, project(): pl.pallas_call(project_kernel, in_specs=[whole, whole, stats, ORDER, ORDE...  3.99 us
  transfers between devices with their start and end apart: 19, of which 3 were waited for; matrix products, arithmetic and copies ran while one was open for 0% of the time, Pallas kernels for 27%

profile of v1, /device:TPU:1, one launch (start us, length us, event | category | flops | bytes accessed | tf_op | source)
XLA Modules:
  0.0 83.2 jit_solution(6727531324553695191)
XLA Ops:
  0.6 1.2 %pack.1 = bf16[512,768]{1,0:T(8,128)(2,1)S(1)} custom-call(bf16[256,768]{1,0:T(8,128)(2,1)} %bitcast.12, bf16[256,768]{1,0:T(8,128)(2,1)} %bitcast.17), custom_call_target="tpu_custom_call" | custom-call | flops 1000 | bytes 1000 | tf_op jit(solution)/shard_map/pack/pallas_call | solution.py:460
  1.8 6.8 %collective-permute-start.3 = (bf16[512,768]{1,0:T(8,128)(2,1)S(1)}, bf16[512,768]{1,0:T(8,128)(2,1)S(1)}, u32[]{:S(2)}, u32[]{:S(2)}) collective-permute-start(bf16[512,768]{1,0:T(8,128)(2,1)S(1)} %pack.1), channel_id=1, source_target_pairs={{0,8},{4,124},{8,16},{12,4},{16,24},{20,12},{24,32},{28,20},{32,40... | collective-permute-start | bytes 2359304 | tf_op jit(solution)/shard_map/ppermute | solution.py:36
  8.7 2.7 %collective-permute-start = (bf16[256,768]{1,0:T(8,128)(2,1)}, bf16[256,768]{1,0:T(8,128)(2,1)S(1)}, u32[]{:S(2)}, u32[]{:S(2)}) collective-permute-start(bf16[256,768]{1,0:T(8,128)(2,1)} %bitcast.29), channel_id=1, source_target_pairs={{0,3},{1,0},{2,1},{3,2},{4,7},{5,4},{6,5},{7,6},{8,11},{9,8},{10,9... | collective-permute-start | bytes 1179656 | tf_op jit(solution)/shard_map/ppermute | solution.py:36
  11.4 1.6 %collective-permute-start.2 = (bf16[256,768]{1,0:T(8,128)(2,1)}, bf16[256,768]{1,0:T(8,128)(2,1)S(1)}, u32[]{:S(2)}, u32[]{:S(2)}) collective-permute-start(bf16[256,768]{1,0:T(8,128)(2,1)} %bitcast.31), channel_id=1, source_target_pairs={{0,2},{1,3},{2,0},{3,1},{4,6},{5,7},{6,4},{7,5},{8,10},{9,11},{10,... | collective-permute-start | bytes 1179656 | tf_op jit(solution)/shard_map/ppermute | solution.py:36
  13.0 11.7 %collective-permute-done.3.refs_0_.refs_4_.refs_9_ = bf16[512,768]{1,0:T(8,128)(2,1)S(1)} collective-permute-done((bf16[512,768]{1,0:T(8,128)(2,1)S(1)}, bf16[512,768]{1,0:T(8,128)(2,1)S(1)}, u32[]{:S(2)}, u32[]{:S(2)}) %collective-permute-start.3) | collective-permute-done | bytes 786464 | tf_op jit(solution)/shard_map/ppermute | solution.py:36
  24.8 2.5 %collective-permute-done.6.refs_2_.refs_7_ = bf16[512,768]{1,0:T(8,128)(2,1)S(1)} collective-permute-done((bf16[512,768]{1,0:T(8,128)(2,1)S(1)}, bf16[512,768]{1,0:T(8,128)(2,1)S(1)}, u32[]{:S(2)}, u32[]{:S(2)}) %collective-permute-start.6) | collective-permute-done | bytes 786464 | tf_op jit(solution)/shard_map/ppermute | solution.py:36
  27.3 0.0 copy-start
  27.3 0.1 collective-permute-start.8
  27.4 8.1 %collective-permute-start.9 = (bf16[256,768]{1,0:T(8,128)(2,1)}, bf16[256,768]{1,0:T(8,128)(2,1)S(1)}, u32[]{:S(2)}, u32[]{:S(2)}) collective-permute-start(bf16[256,768]{1,0:T(8,128)(2,1)} %bitcast.23), channel_id=1, source_target_pairs={{0,8},{4,124},{8,16},{12,4},{16,24},{20,12},{24,32},{28,20},{32,40... | collective-permute-start | bytes 1179656 | tf_op jit(solution)/shard_map/ppermute | solution.py:36
  35.5 4.6 %attn_cotangent.1.after_a.d_ref = bf16[256,768]{1,0:T(8,128)(2,1)S(1)} custom-call(bf16[256,768]{1,0:T(8,128)(2,1)} %bitcast.32, bf16[256,768]{1,0:T(8,128)(2,1)S(1)} %collective-permute-done.d1, bf16[256,768]{1,0:T(8,128)(2,1)S(1)} %collective-permute-done.1.d2, bf16[256,768]{1,0:T(8,128)(2,1)S(1)} %collective-permute-done.2.d3, bf16[768,3072]{1,0:T(8,128)(2,1)} %w_ref.3), custom_call_target="tpu_custom_call" | custom-call | flops 6000000000 | bytes 1000 | tf_op jit(solution)/shard_map/attn_cotangent/pallas_call | solution.py:214
  40.2 6.5 %forward.1 = (bf16[256,768]{1,0:T(8,128)(2,1)S(1)}, bf16[8,256,1280]{2,1,0:T(8,128)(2,1)S(1)}, f32[2,256,128]{2,1,0:T(8,128)S(1)}) custom-call(s32[4,64]{1,0:T(4,128)S(1)} %bitcast.9, bf16[256,768]{1,0:T(8,128)(2,1)S(1)} %attn_cotangent.1.after_a.d_ref, bf16[16,128]{1,0:T(8,128)(2,1)S(1)} %collective-permute-done.4.after_b, bf16[256,768]{1,0:T(8,128)(2,1)} %bitcast.24, ...), custom_call_target="tpu_custom_call" | custom-call | flops 1000 | bytes 1000 | tf_op jit(solution)/shard_map/forward/pallas_call | solution.py:165
  46.7 0.0 copy-start.1
  46.7 4.0 %project.1 = (bf16[256,768]{1,0:T(8,128)(2,1)S(1)}, bf16[256,768]{1,0:T(8,128)(2,1)S(1)}, bf16[256,768]{1,0:T(8,128)(2,1)S(1)}, f32[256,768]{1,0:T(8,128)S(1)}, ...) custom-call(bf16[256,768]{1,0:T(8,128)(2,1)S(1)} %get-tuple-element.19.attn_ref, ...), custom_call_target="tpu_custom_call" | custom-call | flops 1000 | bytes 1000 | tf_op jit(solution)/shard_map/project/pallas_call | solution.py:262
  50.7 0.6 collective-permute-start.17
  51.3 0.1 collective-permute-start.16
  51.4 0.4 collective-permute-start.13
  51.8 4.8 %collective-permute-start.15 = (bf16[272,768]{1,0:T(8,128)(2,1)S(1)}, bf16[272,768]{1,0:T(8,128)(2,1)S(1)}, u32[]{:S(2)}, u32[]{:S(2)}) collective-permute-start(bf16[272,768]{1,0:T(8,128)(2,1)S(1)} %get-tuple-element.21.after_ref.refs_2_.refs_4_), channel_id=1, source_target_pairs={{0,8},{4,124},{8,16},{12,4},{16,24},{20,12},{24,32},{28,20},{32,40... | collective-permute-start | bytes 1253384 | tf_op jit(solution)/shard_map/ppermute | solution.py:36
  56.6 2.7 %collective-permute-start.11 = (bf16[256,768]{1,0:T(8,128)(2,1)S(1)}, bf16[256,768]{1,0:T(8,128)(2,1)S(1)}, u32[]{:S(2)}, u32[]{:S(2)}) collective-permute-start(bf16[256,768]{1,0:T(8,128)(2,1)S(1)} %get-tuple-element.24), channel_id=1, source_target_pairs={{0,3},{1,0},{2,1},{3,2},{4,7},{5,4},{6,5},{7,6},{8,11},{9,8},{10,9... | collective-permute-start | bytes 1179656 | tf_op jit(solution)/shard_map/ppermute | solution.py:36
  59.3 5.7 %query_grad.1.refs_2_ = bf16[256,768]{1,0:T(8,128)(2,1)} custom-call(bf16[8,256,1280]{2,1,0:T(8,128)(2,1)S(1)} %get-tuple-element.26.p_ref, bf16[256,768]{1,0:T(8,128)(2,1)S(1)} %attn_cotangent.1.after_a.d_ref, f32[2,256,128]{2,1,0:T(8,128)S(1)} %get-tuple-element.27.stat_ref, bf16[256,768]{1,0:T(8,128)(2,1)} %bitcast.14, ...), custom_call_target="tpu_custom_call" | custom-call | flops 300000000 | bytes 1000 | tf_op jit(solution)/shard_map/query_grad/pallas_call | solution.py:305
  65.0 4.8 %key_grad_near.1 = (f32[256,768]{1,0:T(8,128)S(1)}, f32[256,768]{1,0:T(8,128)S(1)}) custom-call(s32[4,64]{1,0:T(4,128)S(1)} %bitcast.10, bf16[256,768]{1,0:T(8,128)(2,1)} %bitcast.15, bf16[256,768]{1,0:T(8,128)(2,1)} %bitcast.20, bf16[256,768]{1,0:T(8,128)(2,1)} %bitcast.25, bf16[256,768]{1,0:T(8,128)(2,1)S(1)} %collective-permute-done.16.refs_1_, ...), custom_call_target="tpu_custom_call" | custom-call | flops 1000 | bytes 1000 | tf_op jit(solution)/shard_map/key_grad_near/pallas_call | solution.py:373
  69.9 0.1 collective-permute-start.18
  70.0 5.2 %collective-permute-done.11.b = bf16[256,768]{1,0:T(8,128)(2,1)S(1)} collective-permute-done((bf16[256,768]{1,0:T(8,128)(2,1)S(1)}, bf16[256,768]{1,0:T(8,128)(2,1)S(1)}, u32[]{:S(2)}, u32[]{:S(2)}) %collective-permute-start.11) | collective-permute-done | bytes 393248 | tf_op jit(solution)/shard_map/ppermute | solution.py:36
  75.2 1.0 %add_parts.1 = bf16[256,768]{1,0:T(8,128)(2,1)} custom-call(bf16[272,768]{1,0:T(8,128)(2,1)S(1)} %get-tuple-element.21.after_ref.refs_2_.refs_4_, f32[256,768]{1,0:T(8,128)S(1)} %get-tuple-element.22.own, bf16[256,768]{1,0:T(8,128)(2,1)S(1)} %collective-permute-done.10.a, bf16[256,768]{1,0:T(8,128)(2,1)S(1)} %collective-permute-done.11.b, ...), custom_call_target="tpu_custom_call" | custom-call | flops 300000000 | bytes 1000 | tf_op jit(solution)/shard_map/add_parts/pallas_call | solution.py:423
  76.2 7.0 %key_grad_far.1 = (bf16[256,768]{1,0:T(8,128)(2,1)}, bf16[256,768]{1,0:T(8,128)(2,1)}) custom-call(s32[4,64]{1,0:T(4,128)S(1)} %bitcast.11, bf16[256,768]{1,0:T(8,128)(2,1)} %bitcast.16, bf16[256,768]{1,0:T(8,128)(2,1)} %bitcast.21, bf16[256,768]{1,0:T(8,128)(2,1)S(1)} %collective-permute-done.8.qa_ref.refs_0_, ...), custom_call_target="tpu_custom_call" | custom-call | flops 300000000 | bytes 1000 | tf_op jit(solution)/shard_map/key_grad_far/pallas_call | solution.py:373
  (28 shorter events, 0.1 us)
Async XLA Ops:
  1.8 23.0 %collective-permute-start.3 = (bf16[512,768]{1,0:T(8,128)(2,1)S(1)}, bf16[512,768]{1,0:T(8,128)(2,1)S(1)}, u32[]{:S(2)}, u32[]{:S(2)}) collective-permute-start(bf16[512,768]{1,0:T(8,128)(2,1)S(1)} %pack.1), channel_id=1, source_target_pairs={{0,8},{4,124},{8,16},{12,4},{16,24},{20,12},{24,32},{28,20},{32,40... | collective-permute-start | bytes 2359304 | tf_op jit(solution)/shard_map/ppermute | solution.py:36
  8.7 18.7 %collective-permute-start.6 = (bf16[512,768]{1,0:T(8,128)(2,1)S(1)}, bf16[512,768]{1,0:T(8,128)(2,1)S(1)}, u32[]{:S(2)}, u32[]{:S(2)}) collective-permute-start(bf16[512,768]{1,0:T(8,128)(2,1)S(1)} %pack.1), channel_id=1, source_target_pairs={{0,120},{4,12},{8,0},{12,20},{16,8},{20,28},{24,16},{28,36},{32,24... | collective-permute-start | bytes 2359304 | tf_op jit(solution)/shard_map/ppermute | solution.py:36
  8.7 18.7 %collective-permute-start = (bf16[256,768]{1,0:T(8,128)(2,1)}, bf16[256,768]{1,0:T(8,128)(2,1)S(1)}, u32[]{:S(2)}, u32[]{:S(2)}) collective-permute-start(bf16[256,768]{1,0:T(8,128)(2,1)} %bitcast.29), channel_id=1, source_target_pairs={{0,3},{1,0},{2,1},{3,2},{4,7},{5,4},{6,5},{7,6},{8,11},{9,8},{10,9... | collective-permute-start | bytes 1179656 | tf_op jit(solution)/shard_map/ppermute | solution.py:36
  11.4 16.0 %collective-permute-start.1 = (bf16[256,768]{1,0:T(8,128)(2,1)}, bf16[256,768]{1,0:T(8,128)(2,1)S(1)}, u32[]{:S(2)}, u32[]{:S(2)}) collective-permute-start(bf16[256,768]{1,0:T(8,128)(2,1)} %bitcast.30), channel_id=1, source_target_pairs={{0,1},{1,2},{2,3},{3,0},{4,5},{5,6},{6,7},{7,4},{8,9},{9,10},{10,1... | collective-permute-start | bytes 1179656 | tf_op jit(solution)/shard_map/ppermute | solution.py:36
  11.4 24.1 %collective-permute-start.2 = (bf16[256,768]{1,0:T(8,128)(2,1)}, bf16[256,768]{1,0:T(8,128)(2,1)S(1)}, u32[]{:S(2)}, u32[]{:S(2)}) collective-permute-start(bf16[256,768]{1,0:T(8,128)(2,1)} %bitcast.31), channel_id=1, source_target_pairs={{0,2},{1,3},{2,0},{3,1},{4,6},{5,7},{6,4},{7,5},{8,10},{9,11},{10,... | collective-permute-start | bytes 1179656 | tf_op jit(solution)/shard_map/ppermute | solution.py:36
  24.8 15.4 %collective-permute-start.5 = (bf16[512,768]{1,0:T(8,128)(2,1)S(1)}, bf16[512,768]{1,0:T(8,128)(2,1)S(1)}, u32[]{:S(2)}, u32[]{:S(2)}) collective-permute-start(bf16[512,768]{1,0:T(8,128)(2,1)S(1)} %pack.1), channel_id=1, source_target_pairs={{0,4},{4,0},{8,12},{12,8},{16,20},{20,16},{24,28},{28,24},{32,36},... | collective-permute-start | bytes 2359304 | tf_op jit(solution)/shard_map/ppermute | solution.py:36
  27.3 12.9 %collective-permute-start.7 = (bf16[512,768]{1,0:T(8,128)(2,1)S(1)}, bf16[512,768]{1,0:T(8,128)(2,1)S(1)}, u32[]{:S(2)}, u32[]{:S(2)}) collective-permute-start(bf16[512,768]{1,0:T(8,128)(2,1)S(1)} %collective-permute-done.6.refs_2_.refs_7_), channel_id=1, source_target_pairs={{0,4},{4,0},{8,12},{12,8},{16,20},{20,16},{24,28},{28,24},{32,36},... | collective-permute-start | bytes 2359304 | tf_op jit(solution)/shard_map/ppermute | solution.py:36
  27.3 12.9 %copy-start = (s32[64,4]{0,1:T(4,128)S(1)}, s32[64,4]{0,1:T(4,128)}, u32[]{:S(2)}) copy-start(s32[64,4]{0,1:T(4,128)} %param.11) | copy-start | bytes 3076
  27.3 19.4 %collective-permute-start.8 = (bf16[256,768]{1,0:T(8,128)(2,1)}, bf16[256,768]{1,0:T(8,128)(2,1)S(1)}, u32[]{:S(2)}, u32[]{:S(2)}) collective-permute-start(bf16[256,768]{1,0:T(8,128)(2,1)} %bitcast.22), channel_id=1, source_target_pairs={{0,120},{4,12},{8,0},{12,20},{16,8},{20,28},{24,16},{28,36},{32,24... | collective-permute-start | bytes 1179656 | tf_op jit(solution)/shard_map/ppermute | solution.py:36
  27.4 19.3 %collective-permute-start.9 = (bf16[256,768]{1,0:T(8,128)(2,1)}, bf16[256,768]{1,0:T(8,128)(2,1)S(1)}, u32[]{:S(2)}, u32[]{:S(2)}) collective-permute-start(bf16[256,768]{1,0:T(8,128)(2,1)} %bitcast.23), channel_id=1, source_target_pairs={{0,8},{4,124},{8,16},{12,4},{16,24},{20,12},{24,32},{28,20},{32,40... | collective-permute-start | bytes 1179656 | tf_op jit(solution)/shard_map/ppermute | solution.py:36
  35.5 4.7 %collective-permute-start.4 = (bf16[16,128]{1,0:T(8,128)(2,1)S(1)}, bf16[16,128]{1,0:T(8,128)(2,1)S(1)}, u32[]{:S(2)}, u32[]{:S(2)}) collective-permute-start(bf16[16,128]{1,0:T(8,128)(2,1)S(1)} %corner.1), channel_id=1, source_target_pairs={{0,4},{4,0},{8,12},{12,8},{16,20},{20,16},{24,28},{28,24},{32,36},... | collective-permute-start | bytes 12296 | tf_op jit(solution)/shard_map/ppermute | solution.py:36
  46.7 4.6 %copy-start.1 = (bf16[2,128,768]{2,1,0:T(8,128)(2,1)S(1)}, bf16[2,128,768]{2,1,0:T(8,128)(2,1)}, u32[]{:S(2)}) copy-start(bf16[2,128,768]{2,1,0:T(8,128)(2,1)} %param.6) | copy-start | bytes 1179652
  50.7 8.6 %collective-permute-start.17 = (bf16[272,768]{1,0:T(8,128)(2,1)S(1)}, bf16[272,768]{1,0:T(8,128)(2,1)S(1)}, u32[]{:S(2)}, u32[]{:S(2)}) collective-permute-start(bf16[272,768]{1,0:T(8,128)(2,1)S(1)} %get-tuple-element.21.after_ref.refs_2_.refs_4_), channel_id=1, source_target_pairs={{0,4},{4,0},{8,12},{12,8},{16,20},{20,16},{24,28},{28,24},{32,36},... | collective-permute-start | bytes 1253384 | tf_op jit(solution)/shard_map/ppermute | solution.py:36
  51.3 5.3 %collective-permute-start.16 = (bf16[256,768]{1,0:T(8,128)(2,1)S(1)}, bf16[256,768]{1,0:T(8,128)(2,1)S(1)}, u32[]{:S(2)}, u32[]{:S(2)}) collective-permute-start(bf16[256,768]{1,0:T(8,128)(2,1)S(1)} %bitcast.26), channel_id=1, source_target_pairs={{0,4},{4,0},{8,12},{12,8},{16,20},{20,16},{24,28},{28,24},{32,36},... | collective-permute-start | bytes 1179656 | tf_op jit(solution)/shard_map/ppermute | solution.py:36
  51.4 5.2 %collective-permute-start.13 = (bf16[256,768]{1,0:T(8,128)(2,1)S(1)}, bf16[256,768]{1,0:T(8,128)(2,1)S(1)}, u32[]{:S(2)}, u32[]{:S(2)}) collective-permute-start(bf16[256,768]{1,0:T(8,128)(2,1)S(1)} %collective-permute-done.8.qa_ref.refs_0_), channel_id=1, source_target_pairs={{0,4},{4,0},{8,12},{12,8},{16,20},{20,16},{24,28},{28,24},{32,36},... | collective-permute-start | bytes 1179656 | tf_op jit(solution)/shard_map/ppermute | solution.py:36
  51.8 18.0 %collective-permute-start.14 = (bf16[272,768]{1,0:T(8,128)(2,1)S(1)}, bf16[272,768]{1,0:T(8,128)(2,1)S(1)}, u32[]{:S(2)}, u32[]{:S(2)}) collective-permute-start(bf16[272,768]{1,0:T(8,128)(2,1)S(1)} %get-tuple-element.21.after_ref.refs_2_.refs_4_), channel_id=1, source_target_pairs={{0,120},{4,12},{8,0},{12,20},{16,8},{20,28},{24,16},{28,36},{32,24... | collective-permute-start | bytes 1253384 | tf_op jit(solution)/shard_map/ppermute | solution.py:36
  51.8 18.0 %collective-permute-start.15 = (bf16[272,768]{1,0:T(8,128)(2,1)S(1)}, bf16[272,768]{1,0:T(8,128)(2,1)S(1)}, u32[]{:S(2)}, u32[]{:S(2)}) collective-permute-start(bf16[272,768]{1,0:T(8,128)(2,1)S(1)} %get-tuple-element.21.after_ref.refs_2_.refs_4_), channel_id=1, source_target_pairs={{0,8},{4,124},{8,16},{12,4},{16,24},{20,12},{24,32},{28,20},{32,40... | collective-permute-start | bytes 1253384 | tf_op jit(solution)/shard_map/ppermute | solution.py:36
  56.6 13.3 %collective-permute-start.10 = (bf16[256,768]{1,0:T(8,128)(2,1)S(1)}, bf16[256,768]{1,0:T(8,128)(2,1)S(1)}, u32[]{:S(2)}, u32[]{:S(2)}) collective-permute-start(bf16[256,768]{1,0:T(8,128)(2,1)S(1)} %get-tuple-element.23), channel_id=1, source_target_pairs={{0,1},{1,2},{2,3},{3,0},{4,5},{5,6},{6,7},{7,4},{8,9},{9,10},{10,1... | collective-permute-start | bytes 1179656 | tf_op jit(solution)/shard_map/ppermute | solution.py:36
  56.6 18.6 %collective-permute-start.11 = (bf16[256,768]{1,0:T(8,128)(2,1)S(1)}, bf16[256,768]{1,0:T(8,128)(2,1)S(1)}, u32[]{:S(2)}, u32[]{:S(2)}) collective-permute-start(bf16[256,768]{1,0:T(8,128)(2,1)S(1)} %get-tuple-element.24), channel_id=1, source_target_pairs={{0,3},{1,0},{2,1},{3,2},{4,7},{5,4},{6,5},{7,6},{8,11},{9,8},{10,9... | collective-permute-start | bytes 1179656 | tf_op jit(solution)/shard_map/ppermute | solution.py:36
  59.3 15.9 %collective-permute-start.12 = (bf16[256,768]{1,0:T(8,128)(2,1)S(1)}, bf16[256,768]{1,0:T(8,128)(2,1)S(1)}, u32[]{:S(2)}, u32[]{:S(2)}) collective-permute-start(bf16[256,768]{1,0:T(8,128)(2,1)S(1)} %get-tuple-element.25), channel_id=1, source_target_pairs={{0,2},{1,3},{2,0},{3,1},{4,6},{5,7},{6,4},{7,5},{8,10},{9,11},{10,... | collective-permute-start | bytes 1179656 | tf_op jit(solution)/shard_map/ppermute | solution.py:36
  69.9 6.3 %collective-permute-start.18 = (bf16[272,768]{1,0:T(8,128)(2,1)S(1)}, bf16[272,768]{1,0:T(8,128)(2,1)S(1)}, u32[]{:S(2)}, u32[]{:S(2)}) collective-permute-start(bf16[272,768]{1,0:T(8,128)(2,1)S(1)} %get-tuple-element.29.refs_3_.refs_6_), channel_id=1, source_target_pairs={{0,4},{4,0},{8,12},{12,8},{16,20},{20,16},{24,28},{28,24},{32,36},... | collective-permute-start | bytes 1253384 | tf_op jit(solution)/shard_map/ppermute | solution.py:36

commit v2 on v1

v2 whole, which is shorter than its diff:
```python
from functools import partial

import jax
import jax.numpy as jnp
from jax import lax
from jax.experimental import pallas as pl
from jax.experimental.pallas import tpu as pltpu
from jax.sharding import PartitionSpec as P

HEAD_DIM = 96
REACH = 4
GROUP = 4
COLS = GROUP * HEAD_DIM
BLOCKS = 5
SCALE = HEAD_DIM ** (-0.5)
LOG2E = 1.4426950408889634
FAR = -1e30
VMEM_LIMIT = 18 * 1024 * 1024
SMALL_LIMIT = 1024 * 1024
BF16 = jnp.bfloat16
F32 = jnp.float32
SCALARS = pl.BlockSpec(memory_space=pltpu.SMEM)
COST = pl.CostEstimate(flops=1000, bytes_accessed=1000, transcendentals=0)


def declared(megabytes):
    return pl.CostEstimate(flops=megabytes * 300_000_000, bytes_accessed=1000, transcendentals=0)


C0, C1, C2, C3 = 20, 1, 30, 1
ORDER = pl.BlockSpec(memory_space=pl.ANY)
HELD = pl.BlockSpec(memory_space=pltpu.VMEM)
STAT_ROWS = 16


def send(array, axis, pairs):
    return lax.ppermute(array, axis, pairs)


def to_sibling(array, count):
    return send(array, "view", [(i, i ^ 1) for i in range(count)])


def from_chip_a(array, count):
    return send(array, "view", [(i, (i + (2 if i % 2 else -2)) % count) for i in range(count)])


def from_chip_b(array, count):
    return send(array, "view", [(i, (i + (-2 if i % 2 else 2)) % count) for i in range(count)])


def in_hbm(array):
    return pltpu.with_memory_space_constraint(array, pltpu.HBM)


def in_vmem(arrays):
    return [pltpu.with_memory_space_constraint(a, pltpu.VMEM) for a in arrays]


def head_span(h):
    lo = h * HEAD_DIM // 128 * 128
    hi = -(-(h + 1) * HEAD_DIM // 128) * 128
    return lo, hi


def head_mask(i, rows, lo, hi):
    lane = lax.broadcasted_iota(jnp.int32, (rows, hi - lo), 1) + lo
    return (lane >= i * HEAD_DIM) & (lane < (i + 1) * HEAD_DIM)


def head_rows(ref, h, lo, hi, at=slice(None)):
    part = ref[at, lo:hi]
    mask = head_mask(h, 1, lo, hi).astype(F32).astype(BF16)
    return part * jnp.broadcast_to(mask, part.shape)


def dot_nt(a, b):
    return lax.dot_general(a, b, (((1,), (1,)), ((), ())), preferred_element_type=F32)


def dot_nn(a, b):
    return jnp.dot(a, b, preferred_element_type=F32)


def fill_bias(linked_ref, bias_ref):
    here = lax.axis_index("view")
    base, sign = 2 * here, 1 - 2 * (here % 2)
    views = linked_ref.shape[1]
    lane = lax.broadcasted_iota(jnp.int32, (1, bias_ref.shape[1] // BLOCKS), 1)
    half = bias_ref.shape[1] // BLOCKS // 2
    for local in range(2):
        for b, offset in enumerate((0, 2, 4, -2, -4)):
            shifts = []
            for other in range(2):
                gap = sign * offset + other - local
                lower = base + local + jnp.minimum(gap, 0)
                size = jnp.abs(gap)
                row = jnp.clip(lower, 0, views - 1)
                column = jnp.clip(size - 1, 0, REACH - 1)
                linked = (linked_ref[column, row] > 0) & (lower >= 0) & (size <= REACH)
                shifts.append(jnp.where(linked | (size == 0), 0.0, FAR).astype(F32))
            at = slice(2 * b * half, 2 * (b + 1) * half)
            bias_ref[local : local + 1, at] = jnp.where(lane < half, shifts[0], shifts[1])


def put_lane(tile, lane, column):
    at = lax.broadcasted_iota(jnp.int32, tile.shape, 1)
    return jnp.where(at == lane, column, tile)


def add_head(total, i, lo, hi, part):
    part = jnp.where(head_mask(i, part.shape[0], lo, hi), part, 0.0)
    total[:, lo:hi] += part


def forward_kernel(after_a, after_b, q_ref, bias_ref, *refs):
    windows = refs[:BLOCKS]
    attn_ref, p_ref, stat_ref, s_ref, total = refs[BLOCKS:]
    rows, width = q_ref.shape
    half = rows // 2
    total[...] = jnp.zeros_like(total)
    for g in range(width // COLS):
        stat = jnp.zeros((rows, 128), F32)
        for i in range(GROUP):
            h = g * GROUP + i
            lo, hi = head_span(h)
            query = head_rows(q_ref, h, lo, hi)
            top = jnp.full((rows, 1), FAR, F32)
            for b, window in enumerate(windows):
                at = slice(b * rows, (b + 1) * rows)
                scores = dot_nt(query, window[:rows, lo:hi]) * (SCALE * LOG2E)
                scores = jnp.concatenate(
                    [scores[:half] + bias_ref[0:1, at], scores[half:] + bias_ref[1:2, at]], axis=0
                )
                s_ref[h % 2, :, at] = scores
                top = jnp.maximum(top, jnp.max(scores, axis=1, keepdims=True))
            norm = jnp.zeros((rows, 1), F32)
            out = jnp.zeros((rows, hi - lo), F32)
            for b, window in enumerate(windows):
                at = slice(b * rows, (b + 1) * rows)
                weights = jnp.exp2(s_ref[h % 2, :, at] - top)
                norm += jnp.sum(weights, axis=1, keepdims=True)
                low = weights.astype(BF16)
                p_ref[h, :, at] = low
                out += dot_nn(low, window[rows:, lo:hi])
            add_head(total, h, lo, hi, out / norm)
            stat = put_lane(stat, i, top + jnp.log2(norm))
            stat = put_lane(stat, GROUP + i, SCALE / norm)
        stat_ref[g] = stat
    attn_ref[...] = total[...].astype(BF16)


def forward(after, q, bias, windows):
    rows, width = q.shape
    groups = width // COLS
    whole = pl.BlockSpec((rows, width), lambda: (0, 0))
    return pl.pallas_call(
        forward_kernel,
        in_specs=[ORDER, ORDER, whole] + [HELD] * (1 + len(windows)),
        out_specs=[HELD] * 3,
        out_shape=[
            jax.ShapeDtypeStruct((rows, width), BF16),
            jax.ShapeDtypeStruct((groups * GROUP, rows, BLOCKS * rows), BF16),
            jax.ShapeDtypeStruct((groups, rows, 128), F32),
        ],
        scratch_shapes=[
            pltpu.VMEM((2, rows, BLOCKS * rows), F32),
            pltpu.VMEM((rows, width), F32),
        ],
        compiler_params=pltpu.CompilerParams(vmem_limit_bytes=VMEM_LIMIT),
        cost_estimate=COST,
        name="forward",
    )(*after, in_hbm(q), *in_vmem((bias, *windows)))


def stage_kernel(linked_ref, w_ref, out_ref, bias_ref, sem):
    copy = pltpu.make_async_copy(w_ref, out_ref, sem)
    copy.start()
    fill_bias(linked_ref, bias_ref)
    copy.wait()


def stage(linked, w_out, rows):
    return pl.pallas_call(
        stage_kernel,
        in_specs=[SCALARS, ORDER],
        out_specs=[HELD] * 2,
        out_shape=[
            jax.ShapeDtypeStruct(w_out.shape, w_out.dtype),
            jax.ShapeDtypeStruct((2, BLOCKS * rows), F32),
        ],
        scratch_shapes=[pltpu.SemaphoreType.DMA],
        compiler_params=pltpu.CompilerParams(vmem_limit_bytes=SMALL_LIMIT),
        cost_estimate=COST,
        name="stage",
    )(linked, in_hbm(w_out))


def columns(w_ref, by):
    width = w_ref.shape[0]
    at = (lax.axis_index("head") + by) % (w_ref.shape[1] // width) * width
    return w_ref[:, pl.ds(pl.multiple_of(at, width), width)]


def d_attn_kernel(d0, d1, d2, d3, w_ref, out_ref):
    total = 0.0
    for by, d_ref in zip((0, 1, 3, 2), (d0, d1, d2, d3)):
        total += dot_nt(d_ref[...], columns(w_ref, by))
    out_ref[...] = total.astype(BF16)


def attn_cotangent(parts, w_held):
    rows, width = parts[0].shape
    whole = pl.BlockSpec((rows, width), lambda: (0, 0))
    return pl.pallas_call(
        d_attn_kernel,
        in_specs=[whole] + [HELD] * 4,
        out_specs=HELD,
        out_shape=jax.ShapeDtypeStruct((rows, width), BF16),
        compiler_params=pltpu.CompilerParams(vmem_limit_bytes=VMEM_LIMIT),
        cost_estimate=declared(C0),
        name="attn_cotangent",
    )(in_hbm(parts[0]), *in_vmem((*parts[1:], w_held)))


def project_kernel(q_ref, attn_ref, d_ref, stat_ref, w_ref, *refs):
    parts, stat_out, message = refs[:4], *refs[4:]
    rows = attn_ref.shape[0]
    message[:rows] = q_ref[...]
    message[rows : 2 * rows] = d_ref[...]
    product = attn_ref[...].astype(F32) * d_ref[...].astype(F32)
    slabs = []
    for g in range(stat_ref.shape[0]):
        stat = stat_ref[g]
        travels = stat
        for i in range(GROUP):
            lo, hi = head_span(i)
            mine = jnp.where(
                head_mask(i, rows, lo, hi), product[:, g * COLS + lo : g * COLS + hi], 0.0
            )
            delta = jnp.sum(mine, axis=1, keepdims=True)
            stat = put_lane(stat, 2 * GROUP + i, delta)
            travels = put_lane(travels, GROUP + i, delta)
        stat_out[g] = stat
        slabs.append(travels.T[: 2 * GROUP])
    rest = jnp.concatenate(slabs, axis=0)
    for n in range(3):
        piece = rest.astype(BF16)
        message[2 * rows :, n * rows : (n + 1) * rows] = piece
        rest = rest - piece.astype(F32)
    for by, out_ref in zip((1, 3, 2, 0), parts):
        out_ref[...] = dot_nn(attn_ref[...], columns(w_ref, by)).astype(out_ref.dtype)


def project(q, attn, d_attn, stat, w_out):
    rows, width = attn.shape
    groups = stat.shape[0]
    return pl.pallas_call(
        project_kernel,
        in_specs=[pl.BlockSpec((rows, width), lambda: (0, 0))] + [HELD] * 4,
        out_specs=[HELD] * 6,
        out_shape=[jax.ShapeDtypeStruct((rows, width), BF16)] * 3
        + [
            jax.ShapeDtypeStruct((rows, width), F32),
            jax.ShapeDtypeStruct((groups, rows, 128), F32),
            jax.ShapeDtypeStruct((2 * rows + STAT_ROWS, width), BF16),
        ],
        compiler_params=pltpu.CompilerParams(vmem_limit_bytes=VMEM_LIMIT),
        cost_estimate=COST,
        name="project",
    )(in_hbm(q), *in_vmem((attn, d_attn, stat, w_out)))


def query_grad_kernel(p_ref, d_ref, stat_ref, *refs):
    windows = refs[:BLOCKS]
    out_ref, total = refs[BLOCKS:]
    rows, width = d_ref.shape
    total[...] = jnp.zeros_like(total)
    for h in range(width // HEAD_DIM):
        g, i = h // GROUP, h % GROUP
        lo, hi = head_span(h)
        cot = head_rows(d_ref, h, lo, hi)
        delta = stat_ref[g, :, 2 * GROUP + i : 2 * GROUP + i + 1]
        scale = stat_ref[g, :, GROUP + i : GROUP + i + 1]
        key = jnp.concatenate([w[:rows, lo:hi] for w in windows])
        value = jnp.concatenate([w[rows:, lo:hi] for w in windows])
        d_probs = dot_nt(cot, value)
        d_scores = (p_ref[h].astype(F32) * (d_probs - delta)).astype(BF16)
        add_head(total, h, lo, hi, dot_nn(d_scores, key) * scale)
    out_ref[...] = total[...].astype(BF16)


def query_grad(p, d_attn, stat, windows):
    rows, width = d_attn.shape
    return pl.pallas_call(
        query_grad_kernel,
        in_specs=[HELD] * (3 + len(windows)),
        out_specs=pl.BlockSpec((rows, width), lambda: (0, 0)),
        out_shape=jax.ShapeDtypeStruct((rows, width), BF16),
        scratch_shapes=[pltpu.VMEM((rows, width), F32)],
        compiler_params=pltpu.CompilerParams(vmem_limit_bytes=VMEM_LIMIT),
        cost_estimate=declared(C3),
        name="query_grad",
    )(*in_vmem((p, d_attn, stat, *windows)))


def key_grad_kernel(blocks, bias_ref, kv_ref, *refs):
    count = len(blocks)
    messages = refs[:count]
    *so_far, gk_ref, gv_ref, total_k, total_v = refs[count:]
    final = len(so_far) > 2
    if final:
        so_far, out_ref = so_far[:-1], so_far[-1]
        add_parts(*so_far[2:], out_ref)
    rows, width = kv_ref.shape[0] // 2, kv_ref.shape[1]
    half = rows // 2
    stats = []
    for message in messages:
        packed = message[2 * rows :].astype(F32)
        stats.append(packed[:, :rows] + packed[:, rows : 2 * rows] + packed[:, 2 * rows :])
    stats = jnp.concatenate(stats, axis=1)
    bias = jnp.concatenate([bias_ref[:, b * rows : (b + 1) * rows] for b in blocks], axis=1)
    for total, ref in zip((total_k, total_v), so_far[:2] if len(so_far) > 1 else (None, None)):
        total[...] = jnp.zeros_like(total) if ref is None else ref[...]
    for h in range(width // HEAD_DIM):
        lo, hi = head_span(h)
        at_lse = h // GROUP * 2 * GROUP + h % GROUP
        at_delta = at_lse + GROUP
        key = head_rows(kv_ref, h, lo, hi, slice(0, rows))
        value = head_rows(kv_ref, h, lo, hi, slice(rows, 2 * rows))
        query = jnp.concatenate([ref[:rows, lo:hi] for ref in messages])
        cot = jnp.concatenate([ref[rows : 2 * rows, lo:hi] for ref in messages])
        shift = bias - stats[at_lse : at_lse + 1]
        delta = stats[at_delta : at_delta + 1]
        scores = dot_nt(key, query) * (SCALE * LOG2E)
        weights = jnp.exp2(
            jnp.concatenate([scores[:half] + shift[0:1], scores[half:] + shift[1:2]], axis=0)
        )
        grad_v = dot_nn(weights.astype(BF16), cot)
        d_probs = dot_nt(value, cot)
        grad_k = dot_nn((weights * (d_probs - delta)).astype(BF16), query)
        add_head(total_k, h, lo, hi, grad_k)
        add_head(total_v, h, lo, hi, grad_v)
    gk_ref[...] = (total_k[...] * SCALE if final else total_k[...]).astype(gk_ref.dtype)
    gv_ref[...] = total_v[...].astype(gv_ref.dtype)


def add_parts(own, a, b, c, out_ref):
    total = own[...] + a[...].astype(F32) + b[...].astype(F32) + c[...].astype(F32)
    out_ref[...] = total.astype(BF16)


def key_grad(name, blocks, bias, kv, messages, so_far=(), parts=()):
    rows, width = kv.shape[0] // 2, kv.shape[1]
    whole = pl.BlockSpec((rows, width), lambda: (0, 0))
    held = (bias, kv, *messages, *so_far, *parts)
    gives = [whole] * 3 if parts else [HELD] * 2
    return pl.pallas_call(
        partial(key_grad_kernel, blocks),
        in_specs=[HELD] * len(held),
        out_specs=gives,
        out_shape=[jax.ShapeDtypeStruct((rows, width), BF16 if parts else F32)] * len(gives),
        scratch_shapes=[pltpu.VMEM((rows, width), F32)] * 2,
        compiler_params=pltpu.CompilerParams(vmem_limit_bytes=VMEM_LIMIT),
        cost_estimate=COST,
        name=name,
    )(*in_vmem(held))


def gate_kernel(*refs):
    pass


def gate(arrays, after=(), cost=COST):
    return pl.pallas_call(
        gate_kernel,
        in_specs=[ORDER] * (len(arrays) + len(after)),
        out_specs=[ORDER] * len(arrays),
        out_shape=[jax.ShapeDtypeStruct(a.shape, a.dtype) for a in arrays],
        input_output_aliases={n: n for n in range(len(arrays))},
        compiler_params=pltpu.CompilerParams(vmem_limit_bytes=SMALL_LIMIT),
        cost_estimate=cost,
        name="gate",
    )(*in_vmem(arrays), *after)


def corner_kernel(*refs):
    refs[-1][...] = jnp.zeros_like(refs[-1])


def corner(array, devices):
    shape = (16, 128)
    tile = pl.pallas_call(
        corner_kernel,
        in_specs=[ORDER],
        out_specs=pl.BlockSpec(shape, lambda: (0, 0)),
        out_shape=jax.ShapeDtypeStruct(shape, BF16),
        compiler_params=pltpu.CompilerParams(vmem_limit_bytes=SMALL_LIMIT),
        cost_estimate=COST,
        name="corner",
    )(array)
    return to_sibling(tile, devices)


def pack_kernel(k_ref, v_ref, out_ref, sems):
    rows = k_ref.shape[0]
    copies = [
        pltpu.make_async_copy(ref, out_ref.at[n * rows : (n + 1) * rows], sems.at[n])
        for n, ref in enumerate((k_ref, v_ref))
    ]
    for copy in copies:
        copy.start()
    for copy in copies:
        copy.wait()


def pack(k, v):
    rows, width = k.shape
    return pl.pallas_call(
        pack_kernel,
        in_specs=[ORDER] * 2,
        out_specs=HELD,
        out_shape=jax.ShapeDtypeStruct((2 * rows, width), BF16),
        scratch_shapes=[pltpu.SemaphoreType.DMA((2,))],
        compiler_params=pltpu.CompilerParams(vmem_limit_bytes=SMALL_LIMIT),
        cost_estimate=COST,
        name="pack",
    )(in_hbm(k), in_hbm(v))


def body(queries, keys, values, d_out, w_out, intersection):
    count, length, width = queries.shape
    devices = lax.axis_size("view")
    groups = lax.axis_size("head")
    q, k, v, d = (a.reshape(count * length, width) for a in (queries, keys, values, d_out))

    def from_group(array, by):
        return send(array, "head", [(i, (i - by) % groups) for i in range(groups)])

    gathered = [from_group(d, by) for by in (1, 3, 2)]
    kv = pack(k, v)
    kv_a, kv_b = from_chip_a(kv, devices), from_chip_b(kv, devices)
    w_held, bias = stage(intersection.T, w_out, count * length)
    (kv_a,) = gate((kv_a,), (w_held,))
    windows = (kv, to_sibling(kv, devices), kv_a, to_sibling(kv_a, devices), kv_b)
    d_attn = attn_cotangent([d] + gathered, w_held)
    attn, p, stat = forward((d_attn, corner(kv_b, devices)), q, bias, windows)
    to_next, to_last, to_far, own, stat, message = project(q, attn, d_attn, stat, w_held)
    d_a, d_b = from_chip_a(message, devices), from_chip_b(message, devices)
    gained = [from_group(part, by) for part, by in ((to_next, 3), (to_last, 1), (to_far, 2))]
    grad_q = query_grad(p, d_attn, stat, windows)
    near = (message, to_sibling(message, devices))
    part = key_grad("key_grad_near", (0, 1), bias, kv, near)
    d_a, d_b = gate((d_a, d_b), (in_hbm(grad_q), part[0]))
    part = key_grad("key_grad_far", (2, 4), bias, kv, (d_a, d_b), part)
    d_last = to_sibling(d_a, devices)
    gained = gate(gained, part[:1], declared(C2))
    attended, grad_k, grad_v = key_grad(
        "key_grad_last", (3,), bias, kv, (d_last,), part, (own, *gained)
    )
    shape = (count, length, width)
    return tuple(a.reshape(shape) for a in (attended, grad_q, grad_k, grad_v))


def solution(mesh):
    columns = P("view", None, "head")
    return jax.shard_map(
        body,
        mesh=mesh,
        in_specs=(columns, columns, columns, columns, P("head", None), P()),
        out_specs=(columns, columns, columns, columns),
        check_vma=False,
    )
```

time: 83.4 us -> 71.3 us (0.85)
  Pallas kernels: 34.7 us -> 27.3 us
  waiting for transfers between devices: 19.6 us -> 15.5 us
  starting transfers between devices: 28 us -> 26.7 us
    pallas_call x8 -> x9, Pallas kernels: 34.7 us -> 27.2 us  [the longest x3 8.66 us: key_grad(): pl.pallas_call(partial(key_grad_kernel, blocks), in_specs=[HELD] * len(he...]
    ppermute x19 -> x15, waiting for transfers between devices: 19.6 us -> 15.5 us  [send(): return lax.ppermute(array, axis, pairs)]
    ppermute x19 -> x15, starting transfers between devices: 28 us -> 26.7 us  [send(): return lax.ppermute(array, axis, pairs)]
  transfers between devices with their start and end apart: 19 -> 15, of which waited for: 3 -> 4; matrix products, arithmetic and copies ran while one was open for 0% -> 0% of each run, Pallas kernels for 27% -> 22%
where the time goes in v2:
time: 71.3 us; the launch traced here: 71 us
  Pallas kernels  27.3 us (38%)
  starting transfers between devices  26.7 us (37%)
  waiting for transfers between devices  15.5 us (22%)
  between operations  0.76 us (1%)
    ppermute x15, starting transfers between devices, send(): return lax.ppermute(array, axis, pairs)  26.7 us
    ppermute x15, waiting for transfers between devices, send(): return lax.ppermute(array, axis, pairs)  15.5 us
    pallas_call x3, Pallas kernels, key_grad(): pl.pallas_call(partial(key_grad_kernel, blocks), in_specs=[HELD] * len(he...  8.66 us
    pallas_call x1, Pallas kernels, forward(): pl.pallas_call(forward_kernel, in_specs=[ORDER, ORDER, whole] + [HELD] *...  5.64 us
    pallas_call x1, Pallas kernels, query_grad(): pl.pallas_call(query_grad_kernel, in_specs=[HELD] * (3 + len(windows)), o...  3.86 us
    pallas_call x1, Pallas kernels, stage(): pl.pallas_call(stage_kernel, in_specs=[SCALARS, ORDER], out_specs=[HELD]...  2.91 us
    pallas_call x1, Pallas kernels, project(): pl.pallas_call(project_kernel, in_specs=[pl.BlockSpec((rows, width), lamb...  2.6 us
    pallas_call x1, Pallas kernels, attn_cotangent(): pl.pallas_call(d_attn_kernel, in_specs=[whole] + [HELD] * 4, out_specs=HE...  2.45 us
  transfers between devices with their start and end apart: 15, of which 4 were waited for; matrix products, arithmetic and copies ran while one was open for 0% of the time, Pallas kernels for 22%

profile of v2, /device:TPU:1, one launch (start us, length us, event | category | flops | bytes accessed | tf_op | source)
XLA Modules:
  0.0 71.0 jit_solution(2386812930794657578)
XLA Ops:
  0.6 1.1 %pack.1.refs_0_.kv_ref = bf16[512,768]{1,0:T(8,128)(2,1)S(1)} custom-call(bf16[256,768]{1,0:T(8,128)(2,1)} %bitcast.13, bf16[256,768]{1,0:T(8,128)(2,1)} %bitcast.14), custom_call_target="tpu_custom_call" | custom-call | flops 1000 | bytes 1000 | tf_op jit(solution)/shard_map/pack/pallas_call | solution.py:419
  1.8 2.5 %collective-permute-start.6 = (bf16[512,768]{1,0:T(8,128)(2,1)S(1)}, bf16[512,768]{1,0:T(8,128)(2,1)S(1)}, u32[]{:S(2)}, u32[]{:S(2)}) collective-permute-start(bf16[512,768]{1,0:T(8,128)(2,1)S(1)} %pack.1.refs_0_.kv_ref), channel_id=1, source_target_pairs={{0,120},{4,12},{8,0},{12,20},{16,8},{20,28},{24,16},{28,36},{32,24... | collective-permute-start | bytes 2359304 | tf_op jit(solution)/shard_map/ppermute | solution.py:37
  4.3 4.4 %collective-permute-start.3 = (bf16[512,768]{1,0:T(8,128)(2,1)S(1)}, bf16[512,768]{1,0:T(8,128)(2,1)S(1)}, u32[]{:S(2)}, u32[]{:S(2)}) collective-permute-start(bf16[512,768]{1,0:T(8,128)(2,1)S(1)} %pack.1.refs_0_.kv_ref), channel_id=1, source_target_pairs={{0,8},{4,124},{8,16},{12,4},{16,24},{20,12},{24,32},{28,20},{32,40... | collective-permute-start | bytes 2359304 | tf_op jit(solution)/shard_map/ppermute | solution.py:37
  8.7 2.9 %collective-permute-start.2 = (bf16[256,768]{1,0:T(8,128)(2,1)}, bf16[256,768]{1,0:T(8,128)(2,1)S(1)}, u32[]{:S(2)}, u32[]{:S(2)}) collective-permute-start(bf16[256,768]{1,0:T(8,128)(2,1)} %bitcast.15), channel_id=1, source_target_pairs={{0,2},{1,3},{2,0},{3,1},{4,6},{5,7},{6,4},{7,5},{8,10},{9,11},{10,... | collective-permute-start | bytes 1179656 | tf_op jit(solution)/shard_map/ppermute | solution.py:37
  12.0 2.3 %collective-permute-start = (bf16[256,768]{1,0:T(8,128)(2,1)}, bf16[256,768]{1,0:T(8,128)(2,1)S(1)}, u32[]{:S(2)}, u32[]{:S(2)}) collective-permute-start(bf16[256,768]{1,0:T(8,128)(2,1)} %bitcast.17), channel_id=1, source_target_pairs={{0,3},{1,0},{2,1},{3,2},{4,7},{5,4},{6,5},{7,6},{8,11},{9,8},{10,9... | collective-permute-start | bytes 1179656 | tf_op jit(solution)/shard_map/ppermute | solution.py:37
  14.3 0.7 copy-done
  15.0 2.9 %stage.1 = (bf16[768,3072]{1,0:T(8,128)(2,1)S(1)}, f32[2,1280]{1,0:T(2,128)S(1)}) custom-call(s32[4,64]{1,0:T(4,128)S(1)} %bitcast.9, bf16[768,3072]{1,0:T(8,128)(2,1)} %w_ref.1), custom_call_target="tpu_custom_call" | custom-call | flops 1000 | bytes 1000 | tf_op jit(solution)/shard_map/stage/pallas_call | solution.py:184
  17.9 2.6 %collective-permute-done.6.refs_0_ = bf16[512,768]{1,0:T(8,128)(2,1)S(1)} collective-permute-done((bf16[512,768]{1,0:T(8,128)(2,1)S(1)}, bf16[512,768]{1,0:T(8,128)(2,1)S(1)}, u32[]{:S(2)}, u32[]{:S(2)}) %collective-permute-start.6) | collective-permute-done | bytes 786464 | tf_op jit(solution)/shard_map/ppermute | solution.py:37
  20.5 6.0 %collective-permute-start.5 = (bf16[512,768]{1,0:T(8,128)(2,1)S(1)}, bf16[512,768]{1,0:T(8,128)(2,1)S(1)}, u32[]{:S(2)}, u32[]{:S(2)}) collective-permute-start(bf16[512,768]{1,0:T(8,128)(2,1)S(1)} %pack.1.refs_0_.kv_ref), channel_id=1, source_target_pairs={{0,4},{4,0},{8,12},{12,8},{16,20},{20,16},{24,28},{28,24},{32,36},... | collective-permute-start | bytes 2359304 | tf_op jit(solution)/shard_map/ppermute | solution.py:37
  27.2 2.7 %collective-permute-done.1.d2 = bf16[256,768]{1,0:T(8,128)(2,1)S(1)} collective-permute-done((bf16[256,768]{1,0:T(8,128)(2,1)}, bf16[256,768]{1,0:T(8,128)(2,1)S(1)}, u32[]{:S(2)}, u32[]{:S(2)}) %collective-permute-start.1) | collective-permute-done | bytes 393248 | tf_op jit(solution)/shard_map/ppermute | solution.py:37
  29.9 2.4 %attn_cotangent.1.after_a.d_ref = bf16[256,768]{1,0:T(8,128)(2,1)S(1)} custom-call(bf16[256,768]{1,0:T(8,128)(2,1)} %bitcast.18, bf16[256,768]{1,0:T(8,128)(2,1)S(1)} %collective-permute-done.d1, bf16[256,768]{1,0:T(8,128)(2,1)S(1)} %collective-permute-done.1.d2, bf16[256,768]{1,0:T(8,128)(2,1)S(1)} %collective-permute-done.2.d3, ...), custom_call_target="tpu_custom_call" | custom-call | flops 6000000000 | bytes 1000 | tf_op jit(solution)/shard_map/attn_cotangent/pallas_call | solution.py:215
  32.4 5.6 %forward.1 = (bf16[256,768]{1,0:T(8,128)(2,1)S(1)}, bf16[8,256,1280]{2,1,0:T(8,128)(2,1)S(1)}, f32[2,256,128]{2,1,0:T(8,128)S(1)}) custom-call(bf16[256,768]{1,0:T(8,128)(2,1)S(1)} %attn_cotangent.1.after_a.d_ref, bf16[16,128]{1,0:T(8,128)(2,1)S(1)} %collective-permute-done.4.after_b, bf16[256,768]{1,0:T(8,128)(2,1)} %bitcast.11, ...), custom_call_target="tpu_custom_call" | custom-call | flops 1000 | bytes 1000 | tf_op jit(solution)/shard_map/forward/pallas_call | solution.py:157
  38.0 2.6 %project.1 = (bf16[256,768]{1,0:T(8,128)(2,1)S(1)}, bf16[256,768]{1,0:T(8,128)(2,1)S(1)}, bf16[256,768]{1,0:T(8,128)(2,1)S(1)}, f32[256,768]{1,0:T(8,128)S(1)}, ...) custom-call(bf16[256,768]{1,0:T(8,128)(2,1)} %bitcast.12, bf16[256,768]{1,0:T(8,128)(2,1)S(1)} %get-tuple-element.29.attn_ref, ...), custom_call_target="tpu_custom_call" | custom-call | flops 1000 | bytes 1000 | tf_op jit(solution)/shard_map/project/pallas_call | solution.py:258
  40.6 0.9 %collective-permute-start.10 = (bf16[528,768]{1,0:T(8,128)(2,1)S(1)}, bf16[528,768]{1,0:T(8,128)(2,1)S(1)}, u32[]{:S(2)}, u32[]{:S(2)}) collective-permute-start(bf16[528,768]{1,0:T(8,128)(2,1)S(1)} %get-tuple-element.31.refs_0_), channel_id=1, source_target_pairs={{0,4},{4,0},{8,12},{12,8},{16,20},{20,16},{24,28},{28,24},{32,36},... | collective-permute-start | bytes 2433032 | tf_op jit(solution)/shard_map/ppermute | solution.py:37
  41.6 2.2 %collective-permute-start.9 = (bf16[528,768]{1,0:T(8,128)(2,1)S(1)}, bf16[528,768]{1,0:T(8,128)(2,1)S(1)}, u32[]{:S(2)}, u32[]{:S(2)}) collective-permute-start(bf16[528,768]{1,0:T(8,128)(2,1)S(1)} %get-tuple-element.31.refs_0_), channel_id=1, source_target_pairs={{0,8},{4,124},{8,16},{12,4},{16,24},{20,12},{24,32},{28,20},{32,40... | collective-permute-start | bytes 2433032 | tf_op jit(solution)/shard_map/ppermute | solution.py:37
  43.7 1.3 %collective-permute-start.12 = (bf16[256,768]{1,0:T(8,128)(2,1)S(1)}, bf16[256,768]{1,0:T(8,128)(2,1)S(1)}, u32[]{:S(2)}, u32[]{:S(2)}) collective-permute-start(bf16[256,768]{1,0:T(8,128)(2,1)S(1)} %get-tuple-element.41), channel_id=1, source_target_pairs={{0,1},{1,2},{2,3},{3,0},{4,5},{5,6},{6,7},{7,4},{8,9},{9,10},{10,1... | collective-permute-start | bytes 1179656 | tf_op jit(solution)/shard_map/ppermute | solution.py:37
  45.0 1.4 %collective-permute-start.13 = (bf16[256,768]{1,0:T(8,128)(2,1)S(1)}, bf16[256,768]{1,0:T(8,128)(2,1)S(1)}, u32[]{:S(2)}, u32[]{:S(2)}) collective-permute-start(bf16[256,768]{1,0:T(8,128)(2,1)S(1)} %get-tuple-element.42), channel_id=1, source_target_pairs={{0,3},{1,0},{2,1},{3,2},{4,7},{5,4},{6,5},{7,6},{8,11},{9,8},{10,9... | collective-permute-start | bytes 1179656 | tf_op jit(solution)/shard_map/ppermute | solution.py:37
  46.5 1.6 %collective-permute-start.14 = (bf16[256,768]{1,0:T(8,128)(2,1)S(1)}, bf16[256,768]{1,0:T(8,128)(2,1)S(1)}, u32[]{:S(2)}, u32[]{:S(2)}) collective-permute-start(bf16[256,768]{1,0:T(8,128)(2,1)S(1)} %get-tuple-element.43), channel_id=1, source_target_pairs={{0,2},{1,3},{2,0},{3,1},{4,6},{5,7},{6,4},{7,5},{8,10},{9,11},{10,... | collective-permute-start | bytes 1179656 | tf_op jit(solution)/shard_map/ppermute | solution.py:37
  48.1 3.9 %query_grad.1.refs_2_ = bf16[256,768]{1,0:T(8,128)(2,1)} custom-call(bf16[8,256,1280]{2,1,0:T(8,128)(2,1)S(1)} %get-tuple-element.32.p_ref, bf16[256,768]{1,0:T(8,128)(2,1)S(1)} %attn_cotangent.1.after_a.d_ref, f32[2,256,128]{2,1,0:T(8,128)S(1)} %get-tuple-element.33.stat_ref, bf16[512,768]{1,0:T(8,128)(2,1)S(1)} %pack.1.refs_0_.kv_ref, ...), custom_call_target="tpu_custom_call" | custom-call | flops 300000000 | bytes 1000 | tf_op jit(solution)/shard_map/query_grad/pallas_call | solution.py:295
  52.0 3.0 %key_grad_near.1 = (f32[256,768]{1,0:T(8,128)S(1)}, f32[256,768]{1,0:T(8,128)S(1)}) custom-call(f32[2,1280]{1,0:T(2,128)S(1)} %get-tuple-element.27.bias_ref, bf16[512,768]{1,0:T(8,128)(2,1)S(1)} %pack.1.refs_0_.kv_ref, bf16[528,768]{1,0:T(8,128)(2,1)S(1)} %get-tuple-element.31.refs_0_, bf16[528,768]{1,0:T(8,128)(2,1)S(1)} %collective-permute-done.10.refs_1_), custom_call_target="tpu_custom_call" | custom-call | flops 1000 | bytes 1000 | tf_op jit(solution)/shard_map/key_grad_near/pallas_call | solution.py:358
  55.0 6.1 %collective-permute-done.9.refs_1_ = bf16[528,768]{1,0:T(8,128)(2,1)S(1)} collective-permute-done((bf16[528,768]{1,0:T(8,128)(2,1)S(1)}, bf16[528,768]{1,0:T(8,128)(2,1)S(1)}, u32[]{:S(2)}, u32[]{:S(2)}) %collective-permute-start.9) | collective-permute-done | bytes 811040 | tf_op jit(solution)/shard_map/ppermute | solution.py:37
  61.1 4.1 %collective-permute-done.8.refs_0_ = bf16[528,768]{1,0:T(8,128)(2,1)S(1)} collective-permute-done((bf16[528,768]{1,0:T(8,128)(2,1)S(1)}, bf16[528,768]{1,0:T(8,128)(2,1)S(1)}, u32[]{:S(2)}, u32[]{:S(2)}) %collective-permute-start.8) | collective-permute-done | bytes 811040 | tf_op jit(solution)/shard_map/ppermute | solution.py:37
  65.2 3.1 %key_grad_far.1 = (f32[256,768]{1,0:T(8,128)S(1)}, f32[256,768]{1,0:T(8,128)S(1)}) custom-call(f32[2,1280]{1,0:T(2,128)S(1)} %get-tuple-element.27.bias_ref, bf16[512,768]{1,0:T(8,128)(2,1)S(1)} %pack.1.refs_0_.kv_ref, bf16[528,768]{1,0:T(8,128)(2,1)S(1)} %get-tuple-element.35.refs_0_, bf16[528,768]{1,0:T(8,128)(2,1)S(1)} %get-tuple-element.36.refs_1_, ...), custom_call_target="tpu_custom_call" | custom-call | flops 1000 | bytes 1000 | tf_op jit(solution)/shard_map/key_grad_far/pallas_call | solution.py:358
  68.4 2.6 %key_grad_last.1 = (bf16[256,768]{1,0:T(8,128)(2,1)}, bf16[256,768]{1,0:T(8,128)(2,1)}, bf16[256,768]{1,0:T(8,128)(2,1)}) custom-call(f32[2,1280]{1,0:T(2,128)S(1)} %get-tuple-element.27.bias_ref, bf16[512,768]{1,0:T(8,128)(2,1)S(1)} %pack.1.refs_0_.kv_ref, bf16[528,768]{1,0:T(8,128)(2,1)S(1)} %collective-permute-done.11.refs_0_, ...), custom_call_target="tpu_custom_call" | custom-call | flops 1000 | bytes 1000 | tf_op jit(solution)/shard_map/key_grad_last/pallas_call | solution.py:358
  (21 shorter events, 1.2 us)
Async XLA Ops:
  1.8 18.7 %collective-permute-start.6 = (bf16[512,768]{1,0:T(8,128)(2,1)S(1)}, bf16[512,768]{1,0:T(8,128)(2,1)S(1)}, u32[]{:S(2)}, u32[]{:S(2)}) collective-permute-start(bf16[512,768]{1,0:T(8,128)(2,1)S(1)} %pack.1.refs_0_.kv_ref), channel_id=1, source_target_pairs={{0,120},{4,12},{8,0},{12,20},{16,8},{20,28},{24,16},{28,36},{32,24... | collective-permute-start | bytes 2359304 | tf_op jit(solution)/shard_map/ppermute | solution.py:37
  4.3 22.2 %collective-permute-start.3 = (bf16[512,768]{1,0:T(8,128)(2,1)S(1)}, bf16[512,768]{1,0:T(8,128)(2,1)S(1)}, u32[]{:S(2)}, u32[]{:S(2)}) collective-permute-start(bf16[512,768]{1,0:T(8,128)(2,1)S(1)} %pack.1.refs_0_.kv_ref), channel_id=1, source_target_pairs={{0,8},{4,124},{8,16},{12,4},{16,24},{20,12},{24,32},{28,20},{32,40... | collective-permute-start | bytes 2359304 | tf_op jit(solution)/shard_map/ppermute | solution.py:37
  8.7 18.4 %collective-permute-start.2 = (bf16[256,768]{1,0:T(8,128)(2,1)}, bf16[256,768]{1,0:T(8,128)(2,1)S(1)}, u32[]{:S(2)}, u32[]{:S(2)}) collective-permute-start(bf16[256,768]{1,0:T(8,128)(2,1)} %bitcast.15), channel_id=1, source_target_pairs={{0,2},{1,3},{2,0},{3,1},{4,6},{5,7},{6,4},{7,5},{8,10},{9,11},{10,... | collective-permute-start | bytes 1179656 | tf_op jit(solution)/shard_map/ppermute | solution.py:37
  11.6 18.3 %collective-permute-start.1 = (bf16[256,768]{1,0:T(8,128)(2,1)}, bf16[256,768]{1,0:T(8,128)(2,1)S(1)}, u32[]{:S(2)}, u32[]{:S(2)}) collective-permute-start(bf16[256,768]{1,0:T(8,128)(2,1)} %bitcast.16), channel_id=1, source_target_pairs={{0,1},{1,2},{2,3},{3,0},{4,5},{5,6},{6,7},{7,4},{8,9},{9,10},{10,1... | collective-permute-start | bytes 1179656 | tf_op jit(solution)/shard_map/ppermute | solution.py:37
  12.0 17.9 %collective-permute-start = (bf16[256,768]{1,0:T(8,128)(2,1)}, bf16[256,768]{1,0:T(8,128)(2,1)S(1)}, u32[]{:S(2)}, u32[]{:S(2)}) collective-permute-start(bf16[256,768]{1,0:T(8,128)(2,1)} %bitcast.17), channel_id=1, source_target_pairs={{0,3},{1,0},{2,1},{3,2},{4,7},{5,4},{6,5},{7,6},{8,11},{9,8},{10,9... | collective-permute-start | bytes 1179656 | tf_op jit(solution)/shard_map/ppermute | solution.py:37
  14.3 0.7 copy-start
  20.5 11.9 %collective-permute-start.5 = (bf16[512,768]{1,0:T(8,128)(2,1)S(1)}, bf16[512,768]{1,0:T(8,128)(2,1)S(1)}, u32[]{:S(2)}, u32[]{:S(2)}) collective-permute-start(bf16[512,768]{1,0:T(8,128)(2,1)S(1)} %pack.1.refs_0_.kv_ref), channel_id=1, source_target_pairs={{0,4},{4,0},{8,12},{12,8},{16,20},{20,16},{24,28},{28,24},{32,36},... | collective-permute-start | bytes 2359304 | tf_op jit(solution)/shard_map/ppermute | solution.py:37
  26.5 5.9 %collective-permute-start.7 = (bf16[512,768]{1,0:T(8,128)(2,1)S(1)}, bf16[512,768]{1,0:T(8,128)(2,1)S(1)}, u32[]{:S(2)}, u32[]{:S(2)}) collective-permute-start(bf16[512,768]{1,0:T(8,128)(2,1)S(1)} %gate.3.refs_2_), channel_id=1, source_target_pairs={{0,4},{4,0},{8,12},{12,8},{16,20},{20,16},{24,28},{28,24},{32,36},... | collective-permute-start | bytes 2359304 | tf_op jit(solution)/shard_map/ppermute | solution.py:37
  27.1 5.2 %collective-permute-start.4 = (bf16[16,128]{1,0:T(8,128)(2,1)S(1)}, bf16[16,128]{1,0:T(8,128)(2,1)S(1)}, u32[]{:S(2)}, u32[]{:S(2)}) collective-permute-start(bf16[16,128]{1,0:T(8,128)(2,1)S(1)} %corner.1), channel_id=1, source_target_pairs={{0,4},{4,0},{8,12},{12,8},{16,20},{20,16},{24,28},{28,24},{32,36},... | collective-permute-start | bytes 12296 | tf_op jit(solution)/shard_map/ppermute | solution.py:37
  40.6 5.9 %collective-permute-start.10 = (bf16[528,768]{1,0:T(8,128)(2,1)S(1)}, bf16[528,768]{1,0:T(8,128)(2,1)S(1)}, u32[]{:S(2)}, u32[]{:S(2)}) collective-permute-start(bf16[528,768]{1,0:T(8,128)(2,1)S(1)} %get-tuple-element.31.refs_0_), channel_id=1, source_target_pairs={{0,4},{4,0},{8,12},{12,8},{16,20},{20,16},{24,28},{28,24},{32,36},... | collective-permute-start | bytes 2433032 | tf_op jit(solution)/shard_map/ppermute | solution.py:37
  41.6 19.5 %collective-permute-start.9 = (bf16[528,768]{1,0:T(8,128)(2,1)S(1)}, bf16[528,768]{1,0:T(8,128)(2,1)S(1)}, u32[]{:S(2)}, u32[]{:S(2)}) collective-permute-start(bf16[528,768]{1,0:T(8,128)(2,1)S(1)} %get-tuple-element.31.refs_0_), channel_id=1, source_target_pairs={{0,8},{4,124},{8,16},{12,4},{16,24},{20,12},{24,32},{28,20},{32,40... | collective-permute-start | bytes 2433032 | tf_op jit(solution)/shard_map/ppermute | solution.py:37
  43.7 21.5 %collective-permute-start.8 = (bf16[528,768]{1,0:T(8,128)(2,1)S(1)}, bf16[528,768]{1,0:T(8,128)(2,1)S(1)}, u32[]{:S(2)}, u32[]{:S(2)}) collective-permute-start(bf16[528,768]{1,0:T(8,128)(2,1)S(1)} %get-tuple-element.31.refs_0_), channel_id=1, source_target_pairs={{0,120},{4,12},{8,0},{12,20},{16,8},{20,28},{24,16},{28,36},{32,24... | collective-permute-start | bytes 2433032 | tf_op jit(solution)/shard_map/ppermute | solution.py:37
  43.7 24.6 %collective-permute-start.12 = (bf16[256,768]{1,0:T(8,128)(2,1)S(1)}, bf16[256,768]{1,0:T(8,128)(2,1)S(1)}, u32[]{:S(2)}, u32[]{:S(2)}) collective-permute-start(bf16[256,768]{1,0:T(8,128)(2,1)S(1)} %get-tuple-element.41), channel_id=1, source_target_pairs={{0,1},{1,2},{2,3},{3,0},{4,5},{5,6},{6,7},{7,4},{8,9},{9,10},{10,1... | collective-permute-start | bytes 1179656 | tf_op jit(solution)/shard_map/ppermute | solution.py:37
  45.0 23.3 %collective-permute-start.13 = (bf16[256,768]{1,0:T(8,128)(2,1)S(1)}, bf16[256,768]{1,0:T(8,128)(2,1)S(1)}, u32[]{:S(2)}, u32[]{:S(2)}) collective-permute-start(bf16[256,768]{1,0:T(8,128)(2,1)S(1)} %get-tuple-element.42), channel_id=1, source_target_pairs={{0,3},{1,0},{2,1},{3,2},{4,7},{5,4},{6,5},{7,6},{8,11},{9,8},{10,9... | collective-permute-start | bytes 1179656 | tf_op jit(solution)/shard_map/ppermute | solution.py:37
  46.5 21.9 %collective-permute-start.14 = (bf16[256,768]{1,0:T(8,128)(2,1)S(1)}, bf16[256,768]{1,0:T(8,128)(2,1)S(1)}, u32[]{:S(2)}, u32[]{:S(2)}) collective-permute-start(bf16[256,768]{1,0:T(8,128)(2,1)S(1)} %get-tuple-element.43), channel_id=1, source_target_pairs={{0,2},{1,3},{2,0},{3,1},{4,6},{5,7},{6,4},{7,5},{8,10},{9,11},{10,... | collective-permute-start | bytes 1179656 | tf_op jit(solution)/shard_map/ppermute | solution.py:37
  65.2 3.1 %collective-permute-start.11 = (bf16[528,768]{1,0:T(8,128)(2,1)S(1)}, bf16[528,768]{1,0:T(8,128)(2,1)S(1)}, u32[]{:S(2)}, u32[]{:S(2)}) collective-permute-start(bf16[528,768]{1,0:T(8,128)(2,1)S(1)} %get-tuple-element.35.refs_0_), channel_id=1, source_target_pairs={{0,4},{4,0},{8,12},{12,8},{16,20},{20,16},{24,28},{28,24},{32,36},... | collective-permute-start | bytes 2433032 | tf_op jit(solution)/shard_map/ppermute | solution.py:37

commit v3 on v2

--- a/solution.py
+++ b/solution.py
@@ -23,11 +23,10 @@
 COST = pl.CostEstimate(flops=1000, bytes_accessed=1000, transcendentals=0)
 
 
-def declared(megabytes):
-    return pl.CostEstimate(flops=megabytes * 300_000_000, bytes_accessed=1000, transcendentals=0)
-
-
-C0, C1, C2, C3 = 20, 1, 30, 1
+def declared(units):
+    return pl.CostEstimate(flops=units * 300_000_000, bytes_accessed=1000, transcendentals=0)
+
+
 ORDER = pl.BlockSpec(memory_space=pl.ANY)
 HELD = pl.BlockSpec(memory_space=pltpu.VMEM)
 STAT_ROWS = 16
@@ -113,6 +112,9 @@
     total[:, lo:hi] += part
 
 
+CHUNKS = ((0, 2), (2, 4), (4, 5))
+
+
 def forward_kernel(after_a, after_b, q_ref, bias_ref, *refs):
     windows = refs[:BLOCKS]
     attn_ref, p_ref, stat_ref, s_ref, total = refs[BLOCKS:]
@@ -126,9 +128,10 @@
             lo, hi = head_span(h)
             query = head_rows(q_ref, h, lo, hi)
             top = jnp.full((rows, 1), FAR, F32)
-            for b, window in enumerate(windows):
-                at = slice(b * rows, (b + 1) * rows)
-                scores = dot_nt(query, window[:rows, lo:hi]) * (SCALE * LOG2E)
+            for first, past in CHUNKS:
+                at = slice(first * rows, past * rows)
+                key = jnp.concatenate([w[:rows, lo:hi] for w in windows[first:past]])
+                scores = dot_nt(query, key) * (SCALE * LOG2E)
                 scores = jnp.concatenate(
                     [scores[:half] + bias_ref[0:1, at], scores[half:] + bias_ref[1:2, at]], axis=0
                 )
@@ -136,13 +139,13 @@
                 top = jnp.maximum(top, jnp.max(scores, axis=1, keepdims=True))
             norm = jnp.zeros((rows, 1), F32)
             out = jnp.zeros((rows, hi - lo), F32)
-            for b, window in enumerate(windows):
-                at = slice(b * rows, (b + 1) * rows)
+            for first, past in CHUNKS:
+                at = slice(first * rows, past * rows)
                 weights = jnp.exp2(s_ref[h % 2, :, at] - top)
                 norm += jnp.sum(weights, axis=1, keepdims=True)
                 low = weights.astype(BF16)
                 p_ref[h, :, at] = low
-                out += dot_nn(low, window[rows:, lo:hi])
+                out += dot_nn(low, jnp.concatenate([w[rows:, lo:hi] for w in windows[first:past]]))
             add_head(total, h, lo, hi, out / norm)
             stat = put_lane(stat, i, top + jnp.log2(norm))
             stat = put_lane(stat, GROUP + i, SCALE / norm)
@@ -156,7 +159,7 @@
     whole = pl.BlockSpec((rows, width), lambda: (0, 0))
     return pl.pallas_call(
         forward_kernel,
-        in_specs=[ORDER, ORDER, whole] + [HELD] * (1 + len(windows)),
+        in_specs=[ORDER, ORDER] + [HELD] * (2 + len(windows)),
         out_specs=[HELD] * 3,
         out_shape=[
             jax.ShapeDtypeStruct((rows, width), BF16),
@@ -170,30 +173,32 @@
         compiler_params=pltpu.CompilerParams(vmem_limit_bytes=VMEM_LIMIT),
         cost_estimate=COST,
         name="forward",
-    )(*after, in_hbm(q), *in_vmem((bias, *windows)))
-
-
-def stage_kernel(linked_ref, w_ref, out_ref, bias_ref, sem):
-    copy = pltpu.make_async_copy(w_ref, out_ref, sem)
-    copy.start()
+    )(*after, *in_vmem((q, bias, *windows)))
+
+
+def stage_kernel(linked_ref, w_ref, d_ref, q_ref, w_out, d_out, q_out, bias_ref, sems):
+    pairs = ((w_ref, w_out), (d_ref, d_out), (q_ref, q_out))
+    copies = [pltpu.make_async_copy(*pair, sems.at[n]) for n, pair in enumerate(pairs)]
+    for copy in copies:
+        copy.start()
     fill_bias(linked_ref, bias_ref)
-    copy.wait()
-
-
-def stage(linked, w_out, rows):
+    for copy in copies:
+        copy.wait()
+
+
+def stage(linked, w_out, d, q):
+    arrays = (w_out, d, q)
     return pl.pallas_call(
         stage_kernel,
-        in_specs=[SCALARS, ORDER],
-        out_specs=[HELD] * 2,
-        out_shape=[
-            jax.ShapeDtypeStruct(w_out.shape, w_out.dtype),
-            jax.ShapeDtypeStruct((2, BLOCKS * rows), F32),
-        ],
-        scratch_shapes=[pltpu.SemaphoreType.DMA],
+        in_specs=[SCALARS] + [ORDER] * 3,
+        out_specs=[HELD] * 4,
+        out_shape=[jax.ShapeDtypeStruct(a.shape, a.dtype) for a in arrays]
+        + [jax.ShapeDtypeStruct((2, BLOCKS * q.shape[0]), F32)],
+        scratch_shapes=[pltpu.SemaphoreType.DMA((3,))],
         compiler_params=pltpu.CompilerParams(vmem_limit_bytes=SMALL_LIMIT),
         cost_estimate=COST,
         name="stage",
-    )(linked, in_hbm(w_out))
+    )(linked, *(in_hbm(a) for a in arrays))
 
 
 def columns(w_ref, by):
@@ -211,23 +216,25 @@
 
 def attn_cotangent(parts, w_held):
     rows, width = parts[0].shape
-    whole = pl.BlockSpec((rows, width), lambda: (0, 0))
     return pl.pallas_call(
         d_attn_kernel,
-        in_specs=[whole] + [HELD] * 4,
+        in_specs=[HELD] * 5,
         out_specs=HELD,
         out_shape=jax.ShapeDtypeStruct((rows, width), BF16),
         compiler_params=pltpu.CompilerParams(vmem_limit_bytes=VMEM_LIMIT),
-        cost_estimate=declared(C0),
+        cost_estimate=declared(20),
         name="attn_cotangent",
-    )(in_hbm(parts[0]), *in_vmem((*parts[1:], w_held)))
-
-
-def project_kernel(q_ref, attn_ref, d_ref, stat_ref, w_ref, *refs):
-    parts, stat_out, message = refs[:4], *refs[4:]
+    )(*in_vmem((*parts, w_held)))
+
+
+def message_kernel(q_ref, attn_ref, d_ref, stat_ref, stat_out, message, sems):
     rows = attn_ref.shape[0]
-    message[:rows] = q_ref[...]
-    message[rows : 2 * rows] = d_ref[...]
+    copies = [
+        pltpu.make_async_copy(ref, message.at[n * rows : (n + 1) * rows], sems.at[n])
+        for n, ref in enumerate((q_ref, d_ref))
+    ]
+    for copy in copies:
+        copy.start()
     product = attn_ref[...].astype(F32) * d_ref[...].astype(F32)
     slabs = []
     for g in range(stat_ref.shape[0]):
@@ -248,27 +255,43 @@
         piece = rest.astype(BF16)
         message[2 * rows :, n * rows : (n + 1) * rows] = piece
         rest = rest - piece.astype(F32)
+    for copy in copies:
+        copy.wait()
+
+
+def make_message(q, attn, d_attn, stat):
+    rows, width = attn.shape
+    return pl.pallas_call(
+        message_kernel,
+        in_specs=[HELD] * 4,
+        out_specs=[HELD] * 2,
+        out_shape=[
+            jax.ShapeDtypeStruct(stat.shape, F32),
+            jax.ShapeDtypeStruct((2 * rows + STAT_ROWS, width), BF16),
+        ],
+        scratch_shapes=[pltpu.SemaphoreType.DMA((2,))],
+        compiler_params=pltpu.CompilerParams(vmem_limit_bytes=VMEM_LIMIT),
+        cost_estimate=COST,
+        name="message",
+    )(*in_vmem((q, attn, d_attn, stat)))
+
+
+def project_kernel(attn_ref, w_ref, *parts):
     for by, out_ref in zip((1, 3, 2, 0), parts):
         out_ref[...] = dot_nn(attn_ref[...], columns(w_ref, by)).astype(out_ref.dtype)
 
 
-def project(q, attn, d_attn, stat, w_out):
-    rows, width = attn.shape
-    groups = stat.shape[0]
+def project(attn, w_out):
     return pl.pallas_call(
         project_kernel,
-        in_specs=[pl.BlockSpec((rows, width), lambda: (0, 0))] + [HELD] * 4,
-        out_specs=[HELD] * 6,
-        out_shape=[jax.ShapeDtypeStruct((rows, width), BF16)] * 3
-        + [
-            jax.ShapeDtypeStruct((rows, width), F32),
-            jax.ShapeDtypeStruct((groups, rows, 128), F32),
-            jax.ShapeDtypeStruct((2 * rows + STAT_ROWS, width), BF16),
-        ],
+        in_specs=[HELD] * 2,
+        out_specs=[HELD] * 4,
+        out_shape=[jax.ShapeDtypeStruct(attn.shape, BF16)] * 3
+        + [jax.ShapeDtypeStruct(attn.shape, F32)],
         compiler_params=pltpu.CompilerParams(vmem_limit_bytes=VMEM_LIMIT),
         cost_estimate=COST,
         name="project",
-    )(in_hbm(q), *in_vmem((attn, d_attn, stat, w_out)))
+    )(*in_vmem((attn, w_out)))
 
 
 def query_grad_kernel(p_ref, d_ref, stat_ref, *refs):
@@ -299,7 +322,7 @@
         out_shape=jax.ShapeDtypeStruct((rows, width), BF16),
         scratch_shapes=[pltpu.VMEM((rows, width), F32)],
         compiler_params=pltpu.CompilerParams(vmem_limit_bytes=VMEM_LIMIT),
-        cost_estimate=declared(C3),
+        cost_estimate=declared(1),
         name="query_grad",
     )(*in_vmem((p, d_attn, stat, *windows)))
 
@@ -440,12 +463,13 @@
     gathered = [from_group(d, by) for by in (1, 3, 2)]
     kv = pack(k, v)
     kv_a, kv_b = from_chip_a(kv, devices), from_chip_b(kv, devices)
-    w_held, bias = stage(intersection.T, w_out, count * length)
+    w_held, d, q, bias = stage(intersection.T, w_out, d, q)
     (kv_a,) = gate((kv_a,), (w_held,))
     windows = (kv, to_sibling(kv, devices), kv_a, to_sibling(kv_a, devices), kv_b)
     d_attn = attn_cotangent([d] + gathered, w_held)
     attn, p, stat = forward((d_attn, corner(kv_b, devices)), q, bias, windows)
-    to_next, to_last, to_far, own, stat, message = project(q, attn, d_attn, stat, w_held)
+    stat, message = make_message(q, attn, d_attn, stat)
+    to_next, to_last, to_far, own = project(attn, w_held)
     d_a, d_b = from_chip_a(message, devices), from_chip_b(message, devices)
     gained = [from_group(part, by) for part, by in ((to_next, 3), (to_last, 1), (to_far, 2))]
     grad_q = query_grad(p, d_attn, stat, windows)
@@ -454,7 +478,7 @@
     d_a, d_b = gate((d_a, d_b), (in_hbm(grad_q), part[0]))
     part = key_grad("key_grad_far", (2, 4), bias, kv, (d_a, d_b), part)
     d_last = to_sibling(d_a, devices)
-    gained = gate(gained, part[:1], declared(C2))
+    gained = gate(gained, part[:1], declared(30))
     attended, grad_k, grad_v = key_grad(
         "key_grad_last", (3,), bias, kv, (d_last,), part, (own, *gained)
     )

time: 71.3 us -> 67.2 us (0.942)
  waiting for transfers between devices: 15.5 us -> 12.9 us
  Pallas kernels: 27.3 us -> 24.9 us
  starting transfers between devices: 26.7 us -> 27.8 us
    ppermute x15, waiting for transfers between devices: 15.5 us -> 12.9 us  [send(): return lax.ppermute(array, axis, pairs)]
    pallas_call x4 -> x5, Pallas kernels: 13.6 us -> 11.3 us  [the longest x1 4.48 us: forward(): pl.pallas_call(forward_kernel, in_specs=[ORDER, ORDER] + [HELD] * (2 + le...]
    ppermute x15, starting transfers between devices: 26.7 us -> 27.8 us  [send(): return lax.ppermute(array, axis, pairs)]
  transfers between devices with their start and end apart: 15 -> 15, of which waited for: 4 -> 4; matrix products, arithmetic and copies ran while one was open for 0% -> 0% of each run, Pallas kernels for 22% -> 24%
where the time goes in v3:
time: 67.2 us; the launch traced here: 67 us
  starting transfers between devices  27.8 us (41%)
  Pallas kernels  24.9 us (37%)
  waiting for transfers between devices  12.9 us (19%)
  between operations  0.77 us (1%)
  local copies, waits for them, and re-layouts  0.68 us (1%)
    ppermute x15, starting transfers between devices, send(): return lax.ppermute(array, axis, pairs)  27.8 us
    ppermute x15, waiting for transfers between devices, send(): return lax.ppermute(array, axis, pairs)  12.9 us
    pallas_call x3, Pallas kernels, key_grad(): pl.pallas_call(partial(key_grad_kernel, blocks), in_specs=[HELD] * len(he...  8.69 us
    pallas_call x1, Pallas kernels, forward(): pl.pallas_call(forward_kernel, in_specs=[ORDER, ORDER] + [HELD] * (2 + le...  4.48 us
    pallas_call x1, Pallas kernels, query_grad(): pl.pallas_call(query_grad_kernel, in_specs=[HELD] * (3 + len(windows)), o...  3.74 us
    pallas_call x1, Pallas kernels, stage(): pl.pallas_call(stage_kernel, in_specs=[SCALARS] + [ORDER] * 3, out_specs=...  3.12 us
    pallas_call x1, Pallas kernels, attn_cotangent(): pl.pallas_call(d_attn_kernel, in_specs=[HELD] * 5, out_specs=HELD, out_sh...  1.46 us
    pallas_call x1, Pallas kernels, project(): pl.pallas_call(project_kernel, in_specs=[HELD] * 2, out_specs=[HELD] * 4,...  1.45 us
  transfers between devices with their start and end apart: 15, of which 4 were waited for; matrix products, arithmetic and copies ran while one was open for 0% of the time, Pallas kernels for 24%

profile of v3, /device:TPU:1, one launch (start us, length us, event | category | flops | bytes accessed | tf_op | source)
XLA Modules:
  0.0 67.0 jit_solution(12014602152768442641)
XLA Ops:
  0.6 1.1 %pack.1.refs_0_.kv_ref = bf16[512,768]{1,0:T(8,128)(2,1)S(1)} custom-call(bf16[256,768]{1,0:T(8,128)(2,1)} %bitcast.16, bf16[256,768]{1,0:T(8,128)(2,1)} %bitcast.17), custom_call_target="tpu_custom_call" | custom-call | flops 1000 | bytes 1000 | tf_op jit(solution)/shard_map/pack/pallas_call | solution.py:442
  1.8 2.5 %collective-permute-start.6 = (bf16[512,768]{1,0:T(8,128)(2,1)S(1)}, bf16[512,768]{1,0:T(8,128)(2,1)S(1)}, u32[]{:S(2)}, u32[]{:S(2)}) collective-permute-start(bf16[512,768]{1,0:T(8,128)(2,1)S(1)} %pack.1.refs_0_.kv_ref), channel_id=1, source_target_pairs={{0,120},{4,12},{8,0},{12,20},{16,8},{20,28},{24,16},{28,36},{32,24... | collective-permute-start | bytes 2359304 | tf_op jit(solution)/shard_map/ppermute | solution.py:36
  4.3 4.4 %collective-permute-start.3 = (bf16[512,768]{1,0:T(8,128)(2,1)S(1)}, bf16[512,768]{1,0:T(8,128)(2,1)S(1)}, u32[]{:S(2)}, u32[]{:S(2)}) collective-permute-start(bf16[512,768]{1,0:T(8,128)(2,1)S(1)} %pack.1.refs_0_.kv_ref), channel_id=1, source_target_pairs={{0,8},{4,124},{8,16},{12,4},{16,24},{20,12},{24,32},{28,20},{32,40... | collective-permute-start | bytes 2359304 | tf_op jit(solution)/shard_map/ppermute | solution.py:36
  8.7 2.9 %collective-permute-start.2 = (bf16[256,768]{1,0:T(8,128)(2,1)}, bf16[256,768]{1,0:T(8,128)(2,1)S(1)}, u32[]{:S(2)}, u32[]{:S(2)}) collective-permute-start(bf16[256,768]{1,0:T(8,128)(2,1)} %bitcast.12), channel_id=1, source_target_pairs={{0,2},{1,3},{2,0},{3,1},{4,6},{5,7},{6,4},{7,5},{8,10},{9,11},{10,... | collective-permute-start | bytes 1179656 | tf_op jit(solution)/shard_map/ppermute | solution.py:36
  12.0 2.3 %collective-permute-start = (bf16[256,768]{1,0:T(8,128)(2,1)}, bf16[256,768]{1,0:T(8,128)(2,1)S(1)}, u32[]{:S(2)}, u32[]{:S(2)}) collective-permute-start(bf16[256,768]{1,0:T(8,128)(2,1)} %bitcast.14), channel_id=1, source_target_pairs={{0,3},{1,0},{2,1},{3,2},{4,7},{5,4},{6,5},{7,6},{8,11},{9,8},{10,9... | collective-permute-start | bytes 1179656 | tf_op jit(solution)/shard_map/ppermute | solution.py:36
  15.0 3.1 %stage.1 = (bf16[768,3072]{1,0:T(8,128)(2,1)S(1)}, bf16[256,768]{1,0:T(8,128)(2,1)S(1)}, bf16[256,768]{1,0:T(8,128)(2,1)S(1)}, f32[2,1280]{1,0:T(2,128)S(1)}) custom-call(s32[4,64]{1,0:T(4,128)S(1)} %bitcast.9, bf16[768,3072]{1,0:T(8,128)(2,1)} %w_ref.1, bf16[256,768]{1,0:T(8,128)(2,1)} %bitcast.15, bf16[256,768]{1,0:T(8,128)(2,1)} %bitcast.11), custom_call_target="tpu_custom_call" | custom-call | flops 1000 | bytes 1000 | tf_op jit(solution)/shard_map/stage/pallas_call | solution.py:191
  18.1 2.4 %collective-permute-done.6.refs_0_ = bf16[512,768]{1,0:T(8,128)(2,1)S(1)} collective-permute-done((bf16[512,768]{1,0:T(8,128)(2,1)S(1)}, bf16[512,768]{1,0:T(8,128)(2,1)S(1)}, u32[]{:S(2)}, u32[]{:S(2)}) %collective-permute-start.6) | collective-permute-done | bytes 786464 | tf_op jit(solution)/shard_map/ppermute | solution.py:36
  20.5 6.0 %collective-permute-start.5 = (bf16[512,768]{1,0:T(8,128)(2,1)S(1)}, bf16[512,768]{1,0:T(8,128)(2,1)S(1)}, u32[]{:S(2)}, u32[]{:S(2)}) collective-permute-start(bf16[512,768]{1,0:T(8,128)(2,1)S(1)} %pack.1.refs_0_.kv_ref), channel_id=1, source_target_pairs={{0,4},{4,0},{8,12},{12,8},{16,20},{20,16},{24,28},{28,24},{32,36},... | collective-permute-start | bytes 2359304 | tf_op jit(solution)/shard_map/ppermute | solution.py:36
  27.2 2.7 %collective-permute-done.1.d2 = bf16[256,768]{1,0:T(8,128)(2,1)S(1)} collective-permute-done((bf16[256,768]{1,0:T(8,128)(2,1)}, bf16[256,768]{1,0:T(8,128)(2,1)S(1)}, u32[]{:S(2)}, u32[]{:S(2)}) %collective-permute-start.1) | collective-permute-done | bytes 393248 | tf_op jit(solution)/shard_map/ppermute | solution.py:36
  29.9 1.5 %attn_cotangent.1.after_a.d_ref = bf16[256,768]{1,0:T(8,128)(2,1)S(1)} custom-call(bf16[256,768]{1,0:T(8,128)(2,1)S(1)} %get-tuple-element.31.d0, bf16[256,768]{1,0:T(8,128)(2,1)S(1)} %collective-permute-done.d1, bf16[256,768]{1,0:T(8,128)(2,1)S(1)} %collective-permute-done.1.d2, bf16[256,768]{1,0:T(8,128)(2,1)S(1)} %collective-permute-done.2.d3, ...), custom_call_target="tpu_custom_call" | custom-call | flops 6000000000 | bytes 1000 | tf_op jit(solution)/shard_map/attn_cotangent/pallas_call | solution.py:219
  31.4 4.5 %forward.1 = (bf16[256,768]{1,0:T(8,128)(2,1)S(1)}, bf16[8,256,1280]{2,1,0:T(8,128)(2,1)S(1)}, f32[2,256,128]{2,1,0:T(8,128)S(1)}) custom-call(bf16[256,768]{1,0:T(8,128)(2,1)S(1)} %attn_cotangent.1.after_a.d_ref, bf16[16,128]{1,0:T(8,128)(2,1)S(1)} %collective-permute-done.4.after_b, bf16[256,768]{1,0:T(8,128)(2,1)S(1)} %get-tuple-element.30.q_ref, ...), custom_call_target="tpu_custom_call" | custom-call | flops 1000 | bytes 1000 | tf_op jit(solution)/shard_map/forward/pallas_call | solution.py:160
  35.9 0.8 %message.1 = (f32[2,256,128]{2,1,0:T(8,128)S(1)}, bf16[528,768]{1,0:T(8,128)(2,1)S(1)}) custom-call(bf16[256,768]{1,0:T(8,128)(2,1)S(1)} %get-tuple-element.30.q_ref, bf16[256,768]{1,0:T(8,128)(2,1)S(1)} %get-tuple-element.33.attn_ref, bf16[256,768]{1,0:T(8,128)(2,1)S(1)} %attn_cotangent.1.after_a.d_ref, f32[2,256,128]{2,1,0:T(8,128)S(1)} %get-tuple-element.34.stat_ref), custom_call_target="tpu_custom_call" | custom-call | flops 1000 | bytes 1000 | tf_op jit(solution)/shard_map/message/pallas_call | solution.py:264
  36.7 1.0 %collective-permute-start.10 = (bf16[528,768]{1,0:T(8,128)(2,1)S(1)}, bf16[528,768]{1,0:T(8,128)(2,1)S(1)}, u32[]{:S(2)}, u32[]{:S(2)}) collective-permute-start(bf16[528,768]{1,0:T(8,128)(2,1)S(1)} %get-tuple-element.35.refs_0_), channel_id=1, source_target_pairs={{0,4},{4,0},{8,12},{12,8},{16,20},{20,16},{24,28},{28,24},{32,36},... | collective-permute-start | bytes 2433032 | tf_op jit(solution)/shard_map/ppermute | solution.py:36
  37.6 3.1 %collective-permute-start.9 = (bf16[528,768]{1,0:T(8,128)(2,1)S(1)}, bf16[528,768]{1,0:T(8,128)(2,1)S(1)}, u32[]{:S(2)}, u32[]{:S(2)}) collective-permute-start(bf16[528,768]{1,0:T(8,128)(2,1)S(1)} %get-tuple-element.35.refs_0_), channel_id=1, source_target_pairs={{0,8},{4,124},{8,16},{12,4},{16,24},{20,12},{24,32},{28,20},{32,40... | collective-permute-start | bytes 2433032 | tf_op jit(solution)/shard_map/ppermute | solution.py:36
  40.8 1.5 %project.1 = (bf16[256,768]{1,0:T(8,128)(2,1)S(1)}, bf16[256,768]{1,0:T(8,128)(2,1)S(1)}, bf16[256,768]{1,0:T(8,128)(2,1)S(1)}, f32[256,768]{1,0:T(8,128)S(1)}) custom-call(bf16[256,768]{1,0:T(8,128)(2,1)S(1)} %get-tuple-element.33.attn_ref, bf16[768,3072]{1,0:T(8,128)(2,1)S(1)} %get-tuple-element.32.w_ref.refs_1_), custom_call_target="tpu_custom_call" | custom-call | flops 1000 | bytes 1000 | tf_op jit(solution)/shard_map/project/pallas_call | solution.py:285
  42.2 1.4 %collective-permute-start.12 = (bf16[256,768]{1,0:T(8,128)(2,1)S(1)}, bf16[256,768]{1,0:T(8,128)(2,1)S(1)}, u32[]{:S(2)}, u32[]{:S(2)}) collective-permute-start(bf16[256,768]{1,0:T(8,128)(2,1)S(1)} %get-tuple-element.45), channel_id=1, source_target_pairs={{0,1},{1,2},{2,3},{3,0},{4,5},{5,6},{6,7},{7,4},{8,9},{9,10},{10,1... | collective-permute-start | bytes 1179656 | tf_op jit(solution)/shard_map/ppermute | solution.py:36
  43.6 1.5 %collective-permute-start.13 = (bf16[256,768]{1,0:T(8,128)(2,1)S(1)}, bf16[256,768]{1,0:T(8,128)(2,1)S(1)}, u32[]{:S(2)}, u32[]{:S(2)}) collective-permute-start(bf16[256,768]{1,0:T(8,128)(2,1)S(1)} %get-tuple-element.46), channel_id=1, source_target_pairs={{0,3},{1,0},{2,1},{3,2},{4,7},{5,4},{6,5},{7,6},{8,11},{9,8},{10,9... | collective-permute-start | bytes 1179656 | tf_op jit(solution)/shard_map/ppermute | solution.py:36
  45.1 1.6 %collective-permute-start.14 = (bf16[256,768]{1,0:T(8,128)(2,1)S(1)}, bf16[256,768]{1,0:T(8,128)(2,1)S(1)}, u32[]{:S(2)}, u32[]{:S(2)}) collective-permute-start(bf16[256,768]{1,0:T(8,128)(2,1)S(1)} %get-tuple-element.47), channel_id=1, source_target_pairs={{0,2},{1,3},{2,0},{3,1},{4,6},{5,7},{6,4},{7,5},{8,10},{9,11},{10,... | collective-permute-start | bytes 1179656 | tf_op jit(solution)/shard_map/ppermute | solution.py:36
  46.7 3.7 %query_grad.1.refs_2_ = bf16[256,768]{1,0:T(8,128)(2,1)} custom-call(bf16[8,256,1280]{2,1,0:T(8,128)(2,1)S(1)} %get-tuple-element.36.p_ref, bf16[256,768]{1,0:T(8,128)(2,1)S(1)} %attn_cotangent.1.after_a.d_ref, f32[2,256,128]{2,1,0:T(8,128)S(1)} %get-tuple-element.37.stat_ref, bf16[512,768]{1,0:T(8,128)(2,1)S(1)} %pack.1.refs_0_.kv_ref, ...), custom_call_target="tpu_custom_call" | custom-call | flops 300000000 | bytes 1000 | tf_op jit(solution)/shard_map/query_grad/pallas_call | solution.py:318
  50.4 3.0 %key_grad_near.1 = (f32[256,768]{1,0:T(8,128)S(1)}, f32[256,768]{1,0:T(8,128)S(1)}) custom-call(f32[2,1280]{1,0:T(2,128)S(1)} %get-tuple-element.29.bias_ref, bf16[512,768]{1,0:T(8,128)(2,1)S(1)} %pack.1.refs_0_.kv_ref, bf16[528,768]{1,0:T(8,128)(2,1)S(1)} %get-tuple-element.35.refs_0_, bf16[528,768]{1,0:T(8,128)(2,1)S(1)} %collective-permute-done.10.refs_1_), custom_call_target="tpu_custom_call" | custom-call | flops 1000 | bytes 1000 | tf_op jit(solution)/shard_map/key_grad_near/pallas_call | solution.py:381
  53.5 3.7 %collective-permute-done.9.refs_1_ = bf16[528,768]{1,0:T(8,128)(2,1)S(1)} collective-permute-done((bf16[528,768]{1,0:T(8,128)(2,1)S(1)}, bf16[528,768]{1,0:T(8,128)(2,1)S(1)}, u32[]{:S(2)}, u32[]{:S(2)}) %collective-permute-start.9) | collective-permute-done | bytes 811040 | tf_op jit(solution)/shard_map/ppermute | solution.py:36
  57.2 4.1 %collective-permute-done.8.refs_0_ = bf16[528,768]{1,0:T(8,128)(2,1)S(1)} collective-permute-done((bf16[528,768]{1,0:T(8,128)(2,1)S(1)}, bf16[528,768]{1,0:T(8,128)(2,1)S(1)}, u32[]{:S(2)}, u32[]{:S(2)}) %collective-permute-start.8) | collective-permute-done | bytes 811040 | tf_op jit(solution)/shard_map/ppermute | solution.py:36
  61.3 3.1 %key_grad_far.1 = (f32[256,768]{1,0:T(8,128)S(1)}, f32[256,768]{1,0:T(8,128)S(1)}) custom-call(f32[2,1280]{1,0:T(2,128)S(1)} %get-tuple-element.29.bias_ref, bf16[512,768]{1,0:T(8,128)(2,1)S(1)} %pack.1.refs_0_.kv_ref, bf16[528,768]{1,0:T(8,128)(2,1)S(1)} %get-tuple-element.39.refs_0_, bf16[528,768]{1,0:T(8,128)(2,1)S(1)} %get-tuple-element.40.refs_1_, ...), custom_call_target="tpu_custom_call" | custom-call | flops 1000 | bytes 1000 | tf_op jit(solution)/shard_map/key_grad_far/pallas_call | solution.py:381
  64.4 2.6 %key_grad_last.1 = (bf16[256,768]{1,0:T(8,128)(2,1)}, bf16[256,768]{1,0:T(8,128)(2,1)}, bf16[256,768]{1,0:T(8,128)(2,1)}) custom-call(f32[2,1280]{1,0:T(2,128)S(1)} %get-tuple-element.29.bias_ref, bf16[512,768]{1,0:T(8,128)(2,1)S(1)} %pack.1.refs_0_.kv_ref, bf16[528,768]{1,0:T(8,128)(2,1)S(1)} %collective-permute-done.11.refs_0_, ...), custom_call_target="tpu_custom_call" | custom-call | flops 1000 | bytes 1000 | tf_op jit(solution)/shard_map/key_grad_last/pallas_call | solution.py:381
  (22 shorter events, 1.9 us)
Async XLA Ops:
  1.8 18.7 %collective-permute-start.6 = (bf16[512,768]{1,0:T(8,128)(2,1)S(1)}, bf16[512,768]{1,0:T(8,128)(2,1)S(1)}, u32[]{:S(2)}, u32[]{:S(2)}) collective-permute-start(bf16[512,768]{1,0:T(8,128)(2,1)S(1)} %pack.1.refs_0_.kv_ref), channel_id=1, source_target_pairs={{0,120},{4,12},{8,0},{12,20},{16,8},{20,28},{24,16},{28,36},{32,24... | collective-permute-start | bytes 2359304 | tf_op jit(solution)/shard_map/ppermute | solution.py:36
  4.3 22.2 %collective-permute-start.3 = (bf16[512,768]{1,0:T(8,128)(2,1)S(1)}, bf16[512,768]{1,0:T(8,128)(2,1)S(1)}, u32[]{:S(2)}, u32[]{:S(2)}) collective-permute-start(bf16[512,768]{1,0:T(8,128)(2,1)S(1)} %pack.1.refs_0_.kv_ref), channel_id=1, source_target_pairs={{0,8},{4,124},{8,16},{12,4},{16,24},{20,12},{24,32},{28,20},{32,40... | collective-permute-start | bytes 2359304 | tf_op jit(solution)/shard_map/ppermute | solution.py:36
  8.7 18.4 %collective-permute-start.2 = (bf16[256,768]{1,0:T(8,128)(2,1)}, bf16[256,768]{1,0:T(8,128)(2,1)S(1)}, u32[]{:S(2)}, u32[]{:S(2)}) collective-permute-start(bf16[256,768]{1,0:T(8,128)(2,1)} %bitcast.12), channel_id=1, source_target_pairs={{0,2},{1,3},{2,0},{3,1},{4,6},{5,7},{6,4},{7,5},{8,10},{9,11},{10,... | collective-permute-start | bytes 1179656 | tf_op jit(solution)/shard_map/ppermute | solution.py:36
  11.6 18.3 %collective-permute-start.1 = (bf16[256,768]{1,0:T(8,128)(2,1)}, bf16[256,768]{1,0:T(8,128)(2,1)S(1)}, u32[]{:S(2)}, u32[]{:S(2)}) collective-permute-start(bf16[256,768]{1,0:T(8,128)(2,1)} %bitcast.13), channel_id=1, source_target_pairs={{0,1},{1,2},{2,3},{3,0},{4,5},{5,6},{6,7},{7,4},{8,9},{9,10},{10,1... | collective-permute-start | bytes 1179656 | tf_op jit(solution)/shard_map/ppermute | solution.py:36
  12.0 17.9 %collective-permute-start = (bf16[256,768]{1,0:T(8,128)(2,1)}, bf16[256,768]{1,0:T(8,128)(2,1)S(1)}, u32[]{:S(2)}, u32[]{:S(2)}) collective-permute-start(bf16[256,768]{1,0:T(8,128)(2,1)} %bitcast.14), channel_id=1, source_target_pairs={{0,3},{1,0},{2,1},{3,2},{4,7},{5,4},{6,5},{7,6},{8,11},{9,8},{10,9... | collective-permute-start | bytes 1179656 | tf_op jit(solution)/shard_map/ppermute | solution.py:36
  14.3 0.7 %copy-start = (s32[64,4]{0,1:T(4,128)S(1)}, s32[64,4]{0,1:T(4,128)}, u32[]{:S(2)}) copy-start(s32[64,4]{0,1:T(4,128)} %param.11) | copy-start | bytes 3076
  20.5 10.9 %collective-permute-start.5 = (bf16[512,768]{1,0:T(8,128)(2,1)S(1)}, bf16[512,768]{1,0:T(8,128)(2,1)S(1)}, u32[]{:S(2)}, u32[]{:S(2)}) collective-permute-start(bf16[512,768]{1,0:T(8,128)(2,1)S(1)} %pack.1.refs_0_.kv_ref), channel_id=1, source_target_pairs={{0,4},{4,0},{8,12},{12,8},{16,20},{20,16},{24,28},{28,24},{32,36},... | collective-permute-start | bytes 2359304 | tf_op jit(solution)/shard_map/ppermute | solution.py:36
  26.5 4.9 %collective-permute-start.7 = (bf16[512,768]{1,0:T(8,128)(2,1)S(1)}, bf16[512,768]{1,0:T(8,128)(2,1)S(1)}, u32[]{:S(2)}, u32[]{:S(2)}) collective-permute-start(bf16[512,768]{1,0:T(8,128)(2,1)S(1)} %gate.3.refs_2_), channel_id=1, source_target_pairs={{0,4},{4,0},{8,12},{12,8},{16,20},{20,16},{24,28},{28,24},{32,36},... | collective-permute-start | bytes 2359304 | tf_op jit(solution)/shard_map/ppermute | solution.py:36
  27.1 4.2 %collective-permute-start.4 = (bf16[16,128]{1,0:T(8,128)(2,1)S(1)}, bf16[16,128]{1,0:T(8,128)(2,1)S(1)}, u32[]{:S(2)}, u32[]{:S(2)}) collective-permute-start(bf16[16,128]{1,0:T(8,128)(2,1)S(1)} %corner.1), channel_id=1, source_target_pairs={{0,4},{4,0},{8,12},{12,8},{16,20},{20,16},{24,28},{28,24},{32,36},... | collective-permute-start | bytes 12296 | tf_op jit(solution)/shard_map/ppermute | solution.py:36
  36.7 8.4 %collective-permute-start.10 = (bf16[528,768]{1,0:T(8,128)(2,1)S(1)}, bf16[528,768]{1,0:T(8,128)(2,1)S(1)}, u32[]{:S(2)}, u32[]{:S(2)}) collective-permute-start(bf16[528,768]{1,0:T(8,128)(2,1)S(1)} %get-tuple-element.35.refs_0_), channel_id=1, source_target_pairs={{0,4},{4,0},{8,12},{12,8},{16,20},{20,16},{24,28},{28,24},{32,36},... | collective-permute-start | bytes 2433032 | tf_op jit(solution)/shard_map/ppermute | solution.py:36
  37.6 19.5 %collective-permute-start.9 = (bf16[528,768]{1,0:T(8,128)(2,1)S(1)}, bf16[528,768]{1,0:T(8,128)(2,1)S(1)}, u32[]{:S(2)}, u32[]{:S(2)}) collective-permute-start(bf16[528,768]{1,0:T(8,128)(2,1)S(1)} %get-tuple-element.35.refs_0_), channel_id=1, source_target_pairs={{0,8},{4,124},{8,16},{12,4},{16,24},{20,12},{24,32},{28,20},{32,40... | collective-permute-start | bytes 2433032 | tf_op jit(solution)/shard_map/ppermute | solution.py:36
  40.8 20.5 %collective-permute-start.8 = (bf16[528,768]{1,0:T(8,128)(2,1)S(1)}, bf16[528,768]{1,0:T(8,128)(2,1)S(1)}, u32[]{:S(2)}, u32[]{:S(2)}) collective-permute-start(bf16[528,768]{1,0:T(8,128)(2,1)S(1)} %get-tuple-element.35.refs_0_), channel_id=1, source_target_pairs={{0,120},{4,12},{8,0},{12,20},{16,8},{20,28},{24,16},{28,36},{32,24... | collective-permute-start | bytes 2433032 | tf_op jit(solution)/shard_map/ppermute | solution.py:36
  42.2 22.1 %collective-permute-start.12 = (bf16[256,768]{1,0:T(8,128)(2,1)S(1)}, bf16[256,768]{1,0:T(8,128)(2,1)S(1)}, u32[]{:S(2)}, u32[]{:S(2)}) collective-permute-start(bf16[256,768]{1,0:T(8,128)(2,1)S(1)} %get-tuple-element.45), channel_id=1, source_target_pairs={{0,1},{1,2},{2,3},{3,0},{4,5},{5,6},{6,7},{7,4},{8,9},{9,10},{10,1... | collective-permute-start | bytes 1179656 | tf_op jit(solution)/shard_map/ppermute | solution.py:36
  43.6 20.8 %collective-permute-start.13 = (bf16[256,768]{1,0:T(8,128)(2,1)S(1)}, bf16[256,768]{1,0:T(8,128)(2,1)S(1)}, u32[]{:S(2)}, u32[]{:S(2)}) collective-permute-start(bf16[256,768]{1,0:T(8,128)(2,1)S(1)} %get-tuple-element.46), channel_id=1, source_target_pairs={{0,3},{1,0},{2,1},{3,2},{4,7},{5,4},{6,5},{7,6},{8,11},{9,8},{10,9... | collective-permute-start | bytes 1179656 | tf_op jit(solution)/shard_map/ppermute | solution.py:36
  45.1 19.3 %collective-permute-start.14 = (bf16[256,768]{1,0:T(8,128)(2,1)S(1)}, bf16[256,768]{1,0:T(8,128)(2,1)S(1)}, u32[]{:S(2)}, u32[]{:S(2)}) collective-permute-start(bf16[256,768]{1,0:T(8,128)(2,1)S(1)} %get-tuple-element.47), channel_id=1, source_target_pairs={{0,2},{1,3},{2,0},{3,1},{4,6},{5,7},{6,4},{7,5},{8,10},{9,11},{10,... | collective-permute-start | bytes 1179656 | tf_op jit(solution)/shard_map/ppermute | solution.py:36
  61.3 3.1 %collective-permute-start.11 = (bf16[528,768]{1,0:T(8,128)(2,1)S(1)}, bf16[528,768]{1,0:T(8,128)(2,1)S(1)}, u32[]{:S(2)}, u32[]{:S(2)}) collective-permute-start(bf16[528,768]{1,0:T(8,128)(2,1)S(1)} %get-tuple-element.39.refs_0_), channel_id=1, source_target_pairs={{0,4},{4,0},{8,12},{12,8},{16,20},{20,16},{24,28},{28,24},{32,36},... | collective-permute-start | bytes 2433032 | tf_op jit(solution)/shard_map/ppermute | solution.py:36

commit v4 on v3

--- a/solution.py
+++ b/solution.py
@@ -112,10 +112,10 @@
     total[:, lo:hi] += part
 
 
-CHUNKS = ((0, 2), (2, 4), (4, 5))
-
-
-def forward_kernel(after_a, after_b, q_ref, bias_ref, *refs):
+CHUNKS = ((0, 3), (3, 5))
+
+
+def forward_kernel(after_ref, q_ref, bias_ref, *refs):
     windows = refs[:BLOCKS]
     attn_ref, p_ref, stat_ref, s_ref, total = refs[BLOCKS:]
     rows, width = q_ref.shape
@@ -159,7 +159,7 @@
     whole = pl.BlockSpec((rows, width), lambda: (0, 0))
     return pl.pallas_call(
         forward_kernel,
-        in_specs=[ORDER, ORDER] + [HELD] * (2 + len(windows)),
+        in_specs=[ORDER] + [HELD] * (2 + len(windows)),
         out_specs=[HELD] * 3,
         out_shape=[
             jax.ShapeDtypeStruct((rows, width), BF16),
@@ -173,7 +173,7 @@
         compiler_params=pltpu.CompilerParams(vmem_limit_bytes=VMEM_LIMIT),
         cost_estimate=COST,
         name="forward",
-    )(*after, *in_vmem((q, bias, *windows)))
+    )(after, *in_vmem((q, bias, *windows)))
 
 
 def stage_kernel(linked_ref, w_ref, d_ref, q_ref, w_out, d_out, q_out, bias_ref, sems):
@@ -407,24 +407,6 @@
     )(*in_vmem(arrays), *after)
 
 
-def corner_kernel(*refs):
-    refs[-1][...] = jnp.zeros_like(refs[-1])
-
-
-def corner(array, devices):
-    shape = (16, 128)
-    tile = pl.pallas_call(
-        corner_kernel,
-        in_specs=[ORDER],
-        out_specs=pl.BlockSpec(shape, lambda: (0, 0)),
-        out_shape=jax.ShapeDtypeStruct(shape, BF16),
-        compiler_params=pltpu.CompilerParams(vmem_limit_bytes=SMALL_LIMIT),
-        cost_estimate=COST,
-        name="corner",
-    )(array)
-    return to_sibling(tile, devices)
-
-
 def pack_kernel(k_ref, v_ref, out_ref, sems):
     rows = k_ref.shape[0]
     copies = [
@@ -467,11 +449,11 @@
     (kv_a,) = gate((kv_a,), (w_held,))
     windows = (kv, to_sibling(kv, devices), kv_a, to_sibling(kv_a, devices), kv_b)
     d_attn = attn_cotangent([d] + gathered, w_held)
-    attn, p, stat = forward((d_attn, corner(kv_b, devices)), q, bias, windows)
+    attn, p, stat = forward(d_attn, q, bias, windows)
     stat, message = make_message(q, attn, d_attn, stat)
     to_next, to_last, to_far, own = project(attn, w_held)
     d_a, d_b = from_chip_a(message, devices), from_chip_b(message, devices)
-    gained = [from_group(part, by) for part, by in ((to_next, 3), (to_last, 1), (to_far, 2))]
+    gained = [from_group(part, by) for part, by in ((to_far, 2), (to_next, 3), (to_last, 1))]
     grad_q = query_grad(p, d_attn, stat, windows)
     near = (message, to_sibling(message, devices))
     part = key_grad("key_grad_near", (0, 1), bias, kv, near)

time: 67.2 us -> 66.6 us (level)
  waiting for transfers between devices: 12.9 us -> 8.36 us
  starting transfers between devices: 27.8 us -> 31.4 us
    ppermute x15 -> x14, waiting for transfers between devices: 12.9 us -> 8.36 us  [send(): return lax.ppermute(array, axis, pairs)]
    ppermute x15 -> x14, starting transfers between devices: 27.8 us -> 31.4 us  [send(): return lax.ppermute(array, axis, pairs)]
    pallas_call x2 -> x1, Pallas kernels: 4.48 us -> 4.66 us  [forward(): pl.pallas_call(forward_kernel, in_specs=[ORDER] + [HELD] * (2 + len(windo...]
  transfers between devices with their start and end apart: 15 -> 14, of which waited for: 4 -> 3; matrix products, arithmetic and copies ran while one was open for 0% -> 0% of each run, Pallas kernels for 24% -> 24%
where the time goes in v4:
time: 66.6 us; the launch traced here: 66.5 us
  starting transfers between devices  31.4 us (47%)
  Pallas kernels  25.3 us (38%)
  waiting for transfers between devices  8.36 us (13%)
  between operations  0.76 us (1%)
  local copies, waits for them, and re-layouts  0.68 us (1%)
    ppermute x14, starting transfers between devices, send(): return lax.ppermute(array, axis, pairs)  31.4 us
    pallas_call x3, Pallas kernels, key_grad(): pl.pallas_call(partial(key_grad_kernel, blocks), in_specs=[HELD] * len(he...  8.69 us
    ppermute x14, waiting for transfers between devices, send(): return lax.ppermute(array, axis, pairs)  8.36 us
    pallas_call x1, Pallas kernels, forward(): pl.pallas_call(forward_kernel, in_specs=[ORDER] + [HELD] * (2 + len(windo...  4.66 us
    pallas_call x1, Pallas kernels, query_grad(): pl.pallas_call(query_grad_kernel, in_specs=[HELD] * (3 + len(windows)), o...  3.95 us
    pallas_call x1, Pallas kernels, stage(): pl.pallas_call(stage_kernel, in_specs=[SCALARS] + [ORDER] * 3, out_specs=...  3.12 us
    pallas_call x1, Pallas kernels, attn_cotangent(): pl.pallas_call(d_attn_kernel, in_specs=[HELD] * 5, out_specs=HELD, out_sh...  1.46 us
    pallas_call x1, Pallas kernels, project(): pl.pallas_call(project_kernel, in_specs=[HELD] * 2, out_specs=[HELD] * 4,...  1.45 us
  transfers between devices with their start and end apart: 14, of which 3 were waited for; matrix products, arithmetic and copies ran while one was open for 0% of the time, Pallas kernels for 24%

profile of v4, /device:TPU:1, one launch (start us, length us, event | category | flops | bytes accessed | tf_op | source)
XLA Modules:
  0.0 66.5 jit_solution(11421901690279536783)
XLA Ops:
  0.6 1.1 %pack.1.refs_0_.kv_ref = bf16[512,768]{1,0:T(8,128)(2,1)S(1)} custom-call(bf16[256,768]{1,0:T(8,128)(2,1)} %bitcast.16, bf16[256,768]{1,0:T(8,128)(2,1)} %bitcast.17), custom_call_target="tpu_custom_call" | custom-call | flops 1000 | bytes 1000 | tf_op jit(solution)/shard_map/pack/pallas_call | solution.py:424
  1.8 2.5 %collective-permute-start.4 = (bf16[512,768]{1,0:T(8,128)(2,1)S(1)}, bf16[512,768]{1,0:T(8,128)(2,1)S(1)}, u32[]{:S(2)}, u32[]{:S(2)}) collective-permute-start(bf16[512,768]{1,0:T(8,128)(2,1)S(1)} %pack.1.refs_0_.kv_ref), channel_id=1, source_target_pairs={{0,120},{4,12},{8,0},{12,20},{16,8},{20,28},{24,16},{28,36},{32,24... | collective-permute-start | bytes 2359304 | tf_op jit(solution)/shard_map/ppermute | solution.py:36
  4.3 2.9 %collective-permute-start.2 = (bf16[256,768]{1,0:T(8,128)(2,1)}, bf16[256,768]{1,0:T(8,128)(2,1)S(1)}, u32[]{:S(2)}, u32[]{:S(2)}) collective-permute-start(bf16[256,768]{1,0:T(8,128)(2,1)} %bitcast.12), channel_id=1, source_target_pairs={{0,2},{1,3},{2,0},{3,1},{4,6},{5,7},{6,4},{7,5},{8,10},{9,11},{10,... | collective-permute-start | bytes 1179656 | tf_op jit(solution)/shard_map/ppermute | solution.py:36
  7.2 0.4 collective-permute-start.1
  7.6 2.3 %collective-permute-start = (bf16[256,768]{1,0:T(8,128)(2,1)}, bf16[256,768]{1,0:T(8,128)(2,1)S(1)}, u32[]{:S(2)}, u32[]{:S(2)}) collective-permute-start(bf16[256,768]{1,0:T(8,128)(2,1)} %bitcast.14), channel_id=1, source_target_pairs={{0,3},{1,0},{2,1},{3,2},{4,7},{5,4},{6,5},{7,6},{8,11},{9,8},{10,9... | collective-permute-start | bytes 1179656 | tf_op jit(solution)/shard_map/ppermute | solution.py:36
  9.9 4.4 %collective-permute-start.6 = (bf16[512,768]{1,0:T(8,128)(2,1)S(1)}, bf16[512,768]{1,0:T(8,128)(2,1)S(1)}, u32[]{:S(2)}, u32[]{:S(2)}) collective-permute-start(bf16[512,768]{1,0:T(8,128)(2,1)S(1)} %pack.1.refs_0_.kv_ref), channel_id=1, source_target_pairs={{0,8},{4,124},{8,16},{12,4},{16,24},{20,12},{24,32},{28,20},{32,40... | collective-permute-start | bytes 2359304 | tf_op jit(solution)/shard_map/ppermute | solution.py:36
  14.3 0.7 %copy-done = s32[64,4]{0,1:T(4,128)S(1)} copy-done((s32[64,4]{0,1:T(4,128)S(1)}, s32[64,4]{0,1:T(4,128)}, u32[]{:S(2)}) %copy-start) | copy-done | bytes 1048
  15.0 3.1 %stage.1 = (bf16[768,3072]{1,0:T(8,128)(2,1)S(1)}, bf16[256,768]{1,0:T(8,128)(2,1)S(1)}, bf16[256,768]{1,0:T(8,128)(2,1)S(1)}, f32[2,1280]{1,0:T(2,128)S(1)}) custom-call(s32[4,64]{1,0:T(4,128)S(1)} %bitcast.9, bf16[768,3072]{1,0:T(8,128)(2,1)} %w_ref.1, bf16[256,768]{1,0:T(8,128)(2,1)} %bitcast.15, bf16[256,768]{1,0:T(8,128)(2,1)} %bitcast.11), custom_call_target="tpu_custom_call" | custom-call | flops 1000 | bytes 1000 | tf_op jit(solution)/shard_map/stage/pallas_call | solution.py:191
  18.1 4.8 %collective-permute-start.3 = (bf16[512,768]{1,0:T(8,128)(2,1)S(1)}, bf16[512,768]{1,0:T(8,128)(2,1)S(1)}, u32[]{:S(2)}, u32[]{:S(2)}) collective-permute-start(bf16[512,768]{1,0:T(8,128)(2,1)S(1)} %pack.1.refs_0_.kv_ref), channel_id=1, source_target_pairs={{0,4},{4,0},{8,12},{12,8},{16,20},{20,16},{24,28},{28,24},{32,36},... | collective-permute-start | bytes 2359304 | tf_op jit(solution)/shard_map/ppermute | solution.py:36
  22.9 1.5 %attn_cotangent.1.after_ref.d_ref = bf16[256,768]{1,0:T(8,128)(2,1)S(1)} custom-call(bf16[256,768]{1,0:T(8,128)(2,1)S(1)} %get-tuple-element.31.d0, bf16[256,768]{1,0:T(8,128)(2,1)S(1)} %collective-permute-done.d1, bf16[256,768]{1,0:T(8,128)(2,1)S(1)} %collective-permute-done.1.d2, bf16[256,768]{1,0:T(8,128)(2,1)S(1)} %collective-permute-done.2.d3, ...), custom_call_target="tpu_custom_call" | custom-call | flops 6000000000 | bytes 1000 | tf_op jit(solution)/shard_map/attn_cotangent/pallas_call | solution.py:219
  24.4 2.7 %collective-permute-done.6.refs_4_ = bf16[512,768]{1,0:T(8,128)(2,1)S(1)} collective-permute-done((bf16[512,768]{1,0:T(8,128)(2,1)S(1)}, bf16[512,768]{1,0:T(8,128)(2,1)S(1)}, u32[]{:S(2)}, u32[]{:S(2)}) %collective-permute-start.6) | collective-permute-done | bytes 786464 | tf_op jit(solution)/shard_map/ppermute | solution.py:36
  27.1 4.7 %forward.1 = (bf16[256,768]{1,0:T(8,128)(2,1)S(1)}, bf16[8,256,1280]{2,1,0:T(8,128)(2,1)S(1)}, f32[2,256,128]{2,1,0:T(8,128)S(1)}) custom-call(bf16[256,768]{1,0:T(8,128)(2,1)S(1)} %attn_cotangent.1.after_ref.d_ref, bf16[256,768]{1,0:T(8,128)(2,1)S(1)} %get-tuple-element.30.q_ref, f32[2,1280]{1,0:T(2,128)S(1)} %get-tuple-element.29.bias_ref, ...), custom_call_target="tpu_custom_call" | custom-call | flops 1000 | bytes 1000 | tf_op jit(solution)/shard_map/forward/pallas_call | solution.py:160
  31.8 0.8 %message.1 = (f32[2,256,128]{2,1,0:T(8,128)S(1)}, bf16[528,768]{1,0:T(8,128)(2,1)S(1)}) custom-call(bf16[256,768]{1,0:T(8,128)(2,1)S(1)} %get-tuple-element.30.q_ref, bf16[256,768]{1,0:T(8,128)(2,1)S(1)} %get-tuple-element.33.attn_ref, bf16[256,768]{1,0:T(8,128)(2,1)S(1)} %attn_cotangent.1.after_ref.d_ref, f32[2,256,128]{2,1,0:T(8,128)S(1)} %get-tuple-element.34.stat_ref), custom_call_target="tpu_custom_call" | custom-call | flops 1000 | bytes 1000 | tf_op jit(solution)/shard_map/message/pallas_call | solution.py:264
  32.6 4.3 %collective-permute-start.9 = (bf16[528,768]{1,0:T(8,128)(2,1)S(1)}, bf16[528,768]{1,0:T(8,128)(2,1)S(1)}, u32[]{:S(2)}, u32[]{:S(2)}) collective-permute-start(bf16[528,768]{1,0:T(8,128)(2,1)S(1)} %get-tuple-element.35.refs_0_), channel_id=1, source_target_pairs={{0,4},{4,0},{8,12},{12,8},{16,20},{20,16},{24,28},{28,24},{32,36},... | collective-permute-start | bytes 2433032 | tf_op jit(solution)/shard_map/ppermute | solution.py:36
  36.9 1.1 %collective-permute-start.8 = (bf16[528,768]{1,0:T(8,128)(2,1)S(1)}, bf16[528,768]{1,0:T(8,128)(2,1)S(1)}, u32[]{:S(2)}, u32[]{:S(2)}) collective-permute-start(bf16[528,768]{1,0:T(8,128)(2,1)S(1)} %get-tuple-element.35.refs_0_), channel_id=1, source_target_pairs={{0,8},{4,124},{8,16},{12,4},{16,24},{20,12},{24,32},{28,20},{32,40... | collective-permute-start | bytes 2433032 | tf_op jit(solution)/shard_map/ppermute | solution.py:36
  38.4 1.5 %project.1 = (bf16[256,768]{1,0:T(8,128)(2,1)S(1)}, bf16[256,768]{1,0:T(8,128)(2,1)S(1)}, bf16[256,768]{1,0:T(8,128)(2,1)S(1)}, f32[256,768]{1,0:T(8,128)S(1)}) custom-call(bf16[256,768]{1,0:T(8,128)(2,1)S(1)} %get-tuple-element.33.attn_ref, bf16[768,3072]{1,0:T(8,128)(2,1)S(1)} %get-tuple-element.32.w_ref.refs_1_), custom_call_target="tpu_custom_call" | custom-call | flops 1000 | bytes 1000 | tf_op jit(solution)/shard_map/project/pallas_call | solution.py:285
  39.8 5.5 %collective-permute-start.11 = (bf16[256,768]{1,0:T(8,128)(2,1)S(1)}, bf16[256,768]{1,0:T(8,128)(2,1)S(1)}, u32[]{:S(2)}, u32[]{:S(2)}) collective-permute-start(bf16[256,768]{1,0:T(8,128)(2,1)S(1)} %get-tuple-element.45), channel_id=1, source_target_pairs={{0,2},{1,3},{2,0},{3,1},{4,6},{5,7},{6,4},{7,5},{8,10},{9,11},{10,... | collective-permute-start | bytes 1179656 | tf_op jit(solution)/shard_map/ppermute | solution.py:36
  45.3 2.7 %collective-permute-start.13 = (bf16[256,768]{1,0:T(8,128)(2,1)S(1)}, bf16[256,768]{1,0:T(8,128)(2,1)S(1)}, u32[]{:S(2)}, u32[]{:S(2)}) collective-permute-start(bf16[256,768]{1,0:T(8,128)(2,1)S(1)} %get-tuple-element.47), channel_id=1, source_target_pairs={{0,3},{1,0},{2,1},{3,2},{4,7},{5,4},{6,5},{7,6},{8,11},{9,8},{10,9... | collective-permute-start | bytes 1179656 | tf_op jit(solution)/shard_map/ppermute | solution.py:36
  48.0 3.9 %query_grad.1.refs_2_ = bf16[256,768]{1,0:T(8,128)(2,1)} custom-call(bf16[8,256,1280]{2,1,0:T(8,128)(2,1)S(1)} %get-tuple-element.36.p_ref, bf16[256,768]{1,0:T(8,128)(2,1)S(1)} %attn_cotangent.1.after_ref.d_ref, f32[2,256,128]{2,1,0:T(8,128)S(1)} %get-tuple-element.37.stat_ref, bf16[512,768]{1,0:T(8,128)(2,1)S(1)} %pack.1.refs_0_.kv_ref, ...), custom_call_target="tpu_custom_call" | custom-call | flops 300000000 | bytes 1000 | tf_op jit(solution)/shard_map/query_grad/pallas_call | solution.py:318
  51.9 3.0 %key_grad_near.1 = (f32[256,768]{1,0:T(8,128)S(1)}, f32[256,768]{1,0:T(8,128)S(1)}) custom-call(f32[2,1280]{1,0:T(2,128)S(1)} %get-tuple-element.29.bias_ref, bf16[512,768]{1,0:T(8,128)(2,1)S(1)} %pack.1.refs_0_.kv_ref, bf16[528,768]{1,0:T(8,128)(2,1)S(1)} %get-tuple-element.35.refs_0_, bf16[528,768]{1,0:T(8,128)(2,1)S(1)} %collective-permute-done.9.refs_1_), custom_call_target="tpu_custom_call" | custom-call | flops 1000 | bytes 1000 | tf_op jit(solution)/shard_map/key_grad_near/pallas_call | solution.py:381
  55.0 1.5 %collective-permute-done.8.refs_1_ = bf16[528,768]{1,0:T(8,128)(2,1)S(1)} collective-permute-done((bf16[528,768]{1,0:T(8,128)(2,1)S(1)}, bf16[528,768]{1,0:T(8,128)(2,1)S(1)}, u32[]{:S(2)}, u32[]{:S(2)}) %collective-permute-start.8) | collective-permute-done | bytes 811040 | tf_op jit(solution)/shard_map/ppermute | solution.py:36
  56.4 4.1 %collective-permute-done.7.refs_0_ = bf16[528,768]{1,0:T(8,128)(2,1)S(1)} collective-permute-done((bf16[528,768]{1,0:T(8,128)(2,1)S(1)}, bf16[528,768]{1,0:T(8,128)(2,1)S(1)}, u32[]{:S(2)}, u32[]{:S(2)}) %collective-permute-start.7) | collective-permute-done | bytes 811040 | tf_op jit(solution)/shard_map/ppermute | solution.py:36
  60.8 3.1 %key_grad_far.1 = (f32[256,768]{1,0:T(8,128)S(1)}, f32[256,768]{1,0:T(8,128)S(1)}) custom-call(f32[2,1280]{1,0:T(2,128)S(1)} %get-tuple-element.29.bias_ref, bf16[512,768]{1,0:T(8,128)(2,1)S(1)} %pack.1.refs_0_.kv_ref, bf16[528,768]{1,0:T(8,128)(2,1)S(1)} %get-tuple-element.39.refs_0_, bf16[528,768]{1,0:T(8,128)(2,1)S(1)} %get-tuple-element.40.refs_1_, ...), custom_call_target="tpu_custom_call" | custom-call | flops 1000 | bytes 1000 | tf_op jit(solution)/shard_map/key_grad_far/pallas_call | solution.py:381
  63.9 2.6 %key_grad_last.1 = (bf16[256,768]{1,0:T(8,128)(2,1)}, bf16[256,768]{1,0:T(8,128)(2,1)}, bf16[256,768]{1,0:T(8,128)(2,1)}) custom-call(f32[2,1280]{1,0:T(2,128)S(1)} %get-tuple-element.29.bias_ref, bf16[512,768]{1,0:T(8,128)(2,1)S(1)} %pack.1.refs_0_.kv_ref, bf16[528,768]{1,0:T(8,128)(2,1)S(1)} %collective-permute-done.10.refs_0_, ...), custom_call_target="tpu_custom_call" | custom-call | flops 1000 | bytes 1000 | tf_op jit(solution)/shard_map/key_grad_last/pallas_call | solution.py:381
  (19 shorter events, 0.6 us)
Async XLA Ops:
  1.8 16.4 %collective-permute-start.4 = (bf16[512,768]{1,0:T(8,128)(2,1)S(1)}, bf16[512,768]{1,0:T(8,128)(2,1)S(1)}, u32[]{:S(2)}, u32[]{:S(2)}) collective-permute-start(bf16[512,768]{1,0:T(8,128)(2,1)S(1)} %pack.1.refs_0_.kv_ref), channel_id=1, source_target_pairs={{0,120},{4,12},{8,0},{12,20},{16,8},{20,28},{24,16},{28,36},{32,24... | collective-permute-start | bytes 2359304 | tf_op jit(solution)/shard_map/ppermute | solution.py:36
  4.3 18.6 %collective-permute-start.2 = (bf16[256,768]{1,0:T(8,128)(2,1)}, bf16[256,768]{1,0:T(8,128)(2,1)S(1)}, u32[]{:S(2)}, u32[]{:S(2)}) collective-permute-start(bf16[256,768]{1,0:T(8,128)(2,1)} %bitcast.12), channel_id=1, source_target_pairs={{0,2},{1,3},{2,0},{3,1},{4,6},{5,7},{6,4},{7,5},{8,10},{9,11},{10,... | collective-permute-start | bytes 1179656 | tf_op jit(solution)/shard_map/ppermute | solution.py:36
  7.2 15.7 %collective-permute-start.1 = (bf16[256,768]{1,0:T(8,128)(2,1)}, bf16[256,768]{1,0:T(8,128)(2,1)S(1)}, u32[]{:S(2)}, u32[]{:S(2)}) collective-permute-start(bf16[256,768]{1,0:T(8,128)(2,1)} %bitcast.13), channel_id=1, source_target_pairs={{0,1},{1,2},{2,3},{3,0},{4,5},{5,6},{6,7},{7,4},{8,9},{9,10},{10,1... | collective-permute-start | bytes 1179656 | tf_op jit(solution)/shard_map/ppermute | solution.py:36
  7.6 15.3 %collective-permute-start = (bf16[256,768]{1,0:T(8,128)(2,1)}, bf16[256,768]{1,0:T(8,128)(2,1)S(1)}, u32[]{:S(2)}, u32[]{:S(2)}) collective-permute-start(bf16[256,768]{1,0:T(8,128)(2,1)} %bitcast.14), channel_id=1, source_target_pairs={{0,3},{1,0},{2,1},{3,2},{4,7},{5,4},{6,5},{7,6},{8,11},{9,8},{10,9... | collective-permute-start | bytes 1179656 | tf_op jit(solution)/shard_map/ppermute | solution.py:36
  9.9 17.2 %collective-permute-start.6 = (bf16[512,768]{1,0:T(8,128)(2,1)S(1)}, bf16[512,768]{1,0:T(8,128)(2,1)S(1)}, u32[]{:S(2)}, u32[]{:S(2)}) collective-permute-start(bf16[512,768]{1,0:T(8,128)(2,1)S(1)} %pack.1.refs_0_.kv_ref), channel_id=1, source_target_pairs={{0,8},{4,124},{8,16},{12,4},{16,24},{20,12},{24,32},{28,20},{32,40... | collective-permute-start | bytes 2359304 | tf_op jit(solution)/shard_map/ppermute | solution.py:36
  14.3 0.7 %copy-start = (s32[64,4]{0,1:T(4,128)S(1)}, s32[64,4]{0,1:T(4,128)}, u32[]{:S(2)}) copy-start(s32[64,4]{0,1:T(4,128)} %param.11) | copy-start | bytes 3076
  18.1 9.0 %collective-permute-start.3 = (bf16[512,768]{1,0:T(8,128)(2,1)S(1)}, bf16[512,768]{1,0:T(8,128)(2,1)S(1)}, u32[]{:S(2)}, u32[]{:S(2)}) collective-permute-start(bf16[512,768]{1,0:T(8,128)(2,1)S(1)} %pack.1.refs_0_.kv_ref), channel_id=1, source_target_pairs={{0,4},{4,0},{8,12},{12,8},{16,20},{20,16},{24,28},{28,24},{32,36},... | collective-permute-start | bytes 2359304 | tf_op jit(solution)/shard_map/ppermute | solution.py:36
  22.9 4.2 %collective-permute-start.5 = (bf16[512,768]{1,0:T(8,128)(2,1)S(1)}, bf16[512,768]{1,0:T(8,128)(2,1)S(1)}, u32[]{:S(2)}, u32[]{:S(2)}) collective-permute-start(bf16[512,768]{1,0:T(8,128)(2,1)S(1)} %gate.3.refs_2_), channel_id=1, source_target_pairs={{0,4},{4,0},{8,12},{12,8},{16,20},{20,16},{24,28},{28,24},{32,36},... | collective-permute-start | bytes 2359304 | tf_op jit(solution)/shard_map/ppermute | solution.py:36
  32.6 12.7 %collective-permute-start.9 = (bf16[528,768]{1,0:T(8,128)(2,1)S(1)}, bf16[528,768]{1,0:T(8,128)(2,1)S(1)}, u32[]{:S(2)}, u32[]{:S(2)}) collective-permute-start(bf16[528,768]{1,0:T(8,128)(2,1)S(1)} %get-tuple-element.35.refs_0_), channel_id=1, source_target_pairs={{0,4},{4,0},{8,12},{12,8},{16,20},{20,16},{24,28},{28,24},{32,36},... | collective-permute-start | bytes 2433032 | tf_op jit(solution)/shard_map/ppermute | solution.py:36
  36.9 19.5 %collective-permute-start.8 = (bf16[528,768]{1,0:T(8,128)(2,1)S(1)}, bf16[528,768]{1,0:T(8,128)(2,1)S(1)}, u32[]{:S(2)}, u32[]{:S(2)}) collective-permute-start(bf16[528,768]{1,0:T(8,128)(2,1)S(1)} %get-tuple-element.35.refs_0_), channel_id=1, source_target_pairs={{0,8},{4,124},{8,16},{12,4},{16,24},{20,12},{24,32},{28,20},{32,40... | collective-permute-start | bytes 2433032 | tf_op jit(solution)/shard_map/ppermute | solution.py:36
  38.0 22.5 %collective-permute-start.7 = (bf16[528,768]{1,0:T(8,128)(2,1)S(1)}, bf16[528,768]{1,0:T(8,128)(2,1)S(1)}, u32[]{:S(2)}, u32[]{:S(2)}) collective-permute-start(bf16[528,768]{1,0:T(8,128)(2,1)S(1)} %get-tuple-element.35.refs_0_), channel_id=1, source_target_pairs={{0,120},{4,12},{8,0},{12,20},{16,8},{20,28},{24,16},{28,36},{32,24... | collective-permute-start | bytes 2433032 | tf_op jit(solution)/shard_map/ppermute | solution.py:36
  39.8 24.0 %collective-permute-start.11 = (bf16[256,768]{1,0:T(8,128)(2,1)S(1)}, bf16[256,768]{1,0:T(8,128)(2,1)S(1)}, u32[]{:S(2)}, u32[]{:S(2)}) collective-permute-start(bf16[256,768]{1,0:T(8,128)(2,1)S(1)} %get-tuple-element.45), channel_id=1, source_target_pairs={{0,2},{1,3},{2,0},{3,1},{4,6},{5,7},{6,4},{7,5},{8,10},{9,11},{10,... | collective-permute-start | bytes 1179656 | tf_op jit(solution)/shard_map/ppermute | solution.py:36
  45.3 18.5 %collective-permute-start.12 = (bf16[256,768]{1,0:T(8,128)(2,1)S(1)}, bf16[256,768]{1,0:T(8,128)(2,1)S(1)}, u32[]{:S(2)}, u32[]{:S(2)}) collective-permute-start(bf16[256,768]{1,0:T(8,128)(2,1)S(1)} %get-tuple-element.46), channel_id=1, source_target_pairs={{0,1},{1,2},{2,3},{3,0},{4,5},{5,6},{6,7},{7,4},{8,9},{9,10},{10,1... | collective-permute-start | bytes 1179656 | tf_op jit(solution)/shard_map/ppermute | solution.py:36
  45.3 18.5 %collective-permute-start.13 = (bf16[256,768]{1,0:T(8,128)(2,1)S(1)}, bf16[256,768]{1,0:T(8,128)(2,1)S(1)}, u32[]{:S(2)}, u32[]{:S(2)}) collective-permute-start(bf16[256,768]{1,0:T(8,128)(2,1)S(1)} %get-tuple-element.47), channel_id=1, source_target_pairs={{0,3},{1,0},{2,1},{3,2},{4,7},{5,4},{6,5},{7,6},{8,11},{9,8},{10,9... | collective-permute-start | bytes 1179656 | tf_op jit(solution)/shard_map/ppermute | solution.py:36
  60.6 3.3 %collective-permute-start.10 = (bf16[528,768]{1,0:T(8,128)(2,1)S(1)}, bf16[528,768]{1,0:T(8,128)(2,1)S(1)}, u32[]{:S(2)}, u32[]{:S(2)}) collective-permute-start(bf16[528,768]{1,0:T(8,128)(2,1)S(1)} %get-tuple-element.39.refs_0_), channel_id=1, source_target_pairs={{0,4},{4,0},{8,12},{12,8},{16,20},{20,16},{24,28},{28,24},{32,36},... | collective-permute-start | bytes 2433032 | tf_op jit(solution)/shard_map/ppermute | solution.py:36
